TPU v7x, 1024 devices: a whole 4x4x32 slice. The times are simulated.
1024 devices in a mesh: dp: 32 (over z_hi, x, y), fsdp: 32 (over z_lo, core).
Axes of the slice: x: 4, y: 4, z: 32 (z_hi: 2, z_lo: 16; z = z_hi * 16 + z_lo), core: 2. Of those that a mesh axis runs over, the one named last changes fastest.
Arguments:
- activations: bfloat16 [131072, 2560], P(('dp', 'fsdp')), may hold values from -0.09375 to 0.09375
- value_weight: bfloat16 [2560, 512], P('fsdp'), may hold values from -0.125 to 0.125
- queries: bfloat16 [196608, 2560], P(('dp', 'fsdp')), may hold values from -24 to 24
- key_rows: bfloat16 [196608, 512], P(('dp', 'fsdp')), may hold values from -8 to 8
- context_grad: bfloat16 [196608, 2560], P(('dp', 'fsdp')), may hold values from -6 to 6
- segment: int32 [131072], P(('dp', 'fsdp')), may hold values from 0 to 10, as said below
- send_slot: int32 [131072], P(('dp', 'fsdp')), may hold values from 0 to 191, as said below
Outputs:
- input_grad: bfloat16 [131072, 2560], P(('dp', 'fsdp'))
- weight_grad: bfloat16 [2560, 512], P('fsdp')
Inputs may be any that keep to these rules, and one draw needn't show every extreme that they name: A token either keeps send_slot equal to its own position, or its whole response is sent: its tokens go in order to consecutive slots of one section's block, starting at that block's first slot. In each section, of every pair of devices whose dp indices differ by 32 / 2^(s+1) (same fsdp index), exactly one sends exactly one response of 16 to 32 tokens and the other sends none; the pair that holds dp index 0 sends a full 32. `segment`: never falls along one device's tokens; one id is one whole response.
All inputs are finite; a program needn't handle non-finite values.
Results may differ from a plain program's by a relative error of at most 0.015.
Values may be sent and summed in bfloat16 or wider, within the bound.
No kernel may reach another device: no remote copies, remote signals or barrier semaphores. Data moves between devices by JAX's collectives and lax.ppermute only.
A program may use at most 64 MiB of HBM per device.

v0:
```python
import math

import jax
import jax.numpy as jnp
from jax import lax
from jax.sharding import PartitionSpec as P

KVH = 4
GROUP = 5
HD = 128
SECTIONS = 2


def swapped(block, axis, distance):
    count = lax.axis_size(axis)
    route = []
    for low in range(count):
        high = low | 1 << distance
        if high != low and high < count:
            route += [(low, high), (high, low)]
    return lax.ppermute(block, axis, route)


def attend_block(query_rows, key_rows, context_rows, block_segment):
    count = query_rows.shape[0]
    query_heads = query_rows.reshape(count, KVH, GROUP * HD).transpose(1, 0, 2)
    key_heads = key_rows.reshape(count, KVH, HD).transpose(1, 0, 2)
    context_heads = context_rows.reshape(count, KVH, GROUP * HD).transpose(1, 0, 2)
    row_ids = jnp.arange(count, dtype=jnp.int32)
    allowed = (block_segment[:, None] == block_segment[None, :]) & (block_segment[:, None] >= 0)
    allowed = allowed & (row_ids[None, :] <= row_ids[:, None])
    allowed = allowed | (row_ids[:, None] == row_ids[None, :])

    def one_head(members):
        query_one, key_one, context_one = members
        scores = jnp.einsum(
            "igd,jd->gij",
            query_one.reshape(count, GROUP, HD),
            key_one,
            preferred_element_type=jnp.float32,
        ) / math.sqrt(HD)
        masked = jnp.where(allowed, scores, -jnp.inf)
        highest = jnp.max(masked, axis=-1, keepdims=True)
        exponent = jnp.where(allowed, jnp.exp(masked - highest), 0.0)
        attn_probs = (exponent / jnp.sum(exponent, axis=-1, keepdims=True)).astype(jnp.bfloat16)
        gradient = jnp.einsum(
            "gij,igd->jd",
            attn_probs,
            context_one.reshape(count, GROUP, HD),
            preferred_element_type=jnp.float32,
        )
        return gradient.astype(jnp.bfloat16)

    grads = lax.map(one_head, (query_heads, key_heads, context_heads))
    return grads.transpose(1, 0, 2).reshape(count, KVH * HD)


def value_gradient(queries, key_rows, context_grad, slot_segment, tok_count, block_size):
    pieces = [
        attend_block(
            queries[:tok_count],
            key_rows[:tok_count],
            context_grad[:tok_count],
            slot_segment[:tok_count],
        )
    ]
    for section in range(SECTIONS):
        low = tok_count + section * block_size
        pieces.append(
            attend_block(
                queries[low : low + block_size],
                key_rows[low : low + block_size],
                context_grad[low : low + block_size],
                slot_segment[low : low + block_size],
            )
        )
    return jnp.concatenate(pieces, axis=0)


def project_back(row_grads, weight_shard):
    return lax.dot_general(
        row_grads,
        lax.all_gather(weight_shard, "fsdp", axis=0, tiled=True),
        (((1,), (1,)), ((), ())),
        preferred_element_type=jnp.float32,
    ).astype(jnp.bfloat16)


def weight_gradient(rows_in, grads_in):
    summed = lax.psum_scatter(
        lax.dot_general(
            rows_in, grads_in, (((0,), (0,)), ((), ())), preferred_element_type=jnp.float32
        ),
        "fsdp",
        scatter_dimension=0,
        tiled=True,
    )
    return lax.psum(summed, "dp").astype(jnp.bfloat16)


def local(activations, value_weight, queries, key_rows, context_grad, segment, send_slot):
    tok_count = activations.shape[0]
    slot_count = queries.shape[0]
    block_size = (slot_count - tok_count) // SECTIONS
    log_size = lax.axis_size("dp").bit_length() - 1
    sent_segment = jnp.full((slot_count,), -1, jnp.int32).at[send_slot].set(segment)
    segment_parts = [sent_segment[:tok_count]]
    sent_rows = (
        jnp.zeros((slot_count, activations.shape[1]), activations.dtype)
        .at[send_slot]
        .set(activations)
    )
    row_parts = [sent_rows[:tok_count]]
    for section in range(SECTIONS):
        low = tok_count + section * block_size
        got_rows, got_segment = swapped(
            (sent_rows[low : low + block_size], sent_segment[low : low + block_size]),
            "dp",
            log_size - 1 - section,
        )
        row_parts.append(got_rows)
        segment_parts.append(got_segment)
    arrived_rows = jnp.concatenate(row_parts, axis=0)
    slot_segment = jnp.concatenate(segment_parts, axis=0)
    slot_grads = value_gradient(
        queries, key_rows, context_grad, slot_segment, tok_count, block_size
    )
    slot_inputs = project_back(slot_grads, value_weight)
    back_parts = [slot_inputs[:tok_count]]
    for section in range(SECTIONS):
        low = tok_count + section * block_size
        back_parts.append(
            swapped(slot_inputs[low : low + block_size], "dp", log_size - 1 - section)
        )
    input_grad = jnp.concatenate(back_parts, axis=0)[send_slot]
    weight_grad = weight_gradient(arrived_rows, slot_grads)
    return (input_grad, weight_grad)


def solution(mesh):
    placed = (
        P(("dp", "fsdp"), None),
        P("fsdp", None),
        P(("dp", "fsdp"), None),
        P(("dp", "fsdp"), None),
        P(("dp", "fsdp"), None),
        P(("dp", "fsdp")),
        P(("dp", "fsdp")),
    )
    return jax.shard_map(
        local,
        mesh=mesh,
        in_specs=placed,
        out_specs=(P(("dp", "fsdp"), None), P("fsdp", None)),
        check_vma=False,
    )
```

profile of v0, /device:TPU:22, one launch (start us, length us, event | category | flops | bytes accessed | tf_op | source)
XLA Modules:
  0.0 1184.4 jit_solution(16945107266606970646)
XLA Ops:
  7.2 0.7 all-gather.2.cloned.1.call-update
  8.0 0.7 compare_select_fusion
  8.6 1.1 scatter_custom_fusion
  9.7 0.6 fusion.112
  10.3 29.0 %collective-permute-start = (s32[32]{0:T(128)}, s32[32]{0:T(128)S(1)}, u32[]{:S(2)}, u32[]{:S(2)}) collective-permute-start(s32[32]{0:T(128)} %get-tuple-element.236), channel_id=1, source_target_pairs={{0,512},{512,0},{32,544},{544,32},{64,576},{576,64},{96,608},{608,... | collective-permute-start | bytes 392 | tf_op jit(solution)/shard_map/ppermute | solution.py:21
  39.3 3.4 collective-permute-start.1
  42.8 2.4 scatter_custom_fusion.1
  45.2 0.8 fusion.107
  46.0 1.9 collective-permute-start.4
  47.9 4.0 collective-permute-start.5
  51.9 0.8 fusion.111
  52.7 1.6 slice.55
  54.3 0.7 fusion.110
  55.1 1.8 copy.39
  56.9 1.0 reshape.87
  58.8 6.3 while.33
  59.0 1.1 fusion.148
  60.5 1.1 fusion.148
  62.1 1.1 fusion.148
  63.7 1.1 fusion.148
  65.2 3.4 while.34
  68.7 3.4 while.35
  72.3 23.7 %collective-permute-done.4 = bf16[32,2560]{1,0:T(8,128)(2,1)} collective-permute-done((bf16[32,2560]{1,0:T(8,128)(2,1)}, bf16[32,2560]{1,0:T(8,128)(2,1)}, u32[]{:S(2)}, u32[]{:S(2)}) %collective-permute-start.4) | collective-permute-done | bytes 163872 | tf_op jit(solution)/shard_map/ppermute | solution.py:21
  96.0 4.3 fusion.82
  100.3 254.6 %all-gather.2.cloned.1.call-done = bf16[2560,512]{1,0:T(8,128)(2,1)} async-done(((bf16[80,512]{1,0:T(8,128)(2,1)}), bf16[2560,512]{1,0:T(8,128)(2,1)}) %all-gather.2.cloned.1.call-update) | async-done | bytes 2621456 | tf_op jit(solution)/shard_map/all_gather | solution.py:83
  354.9 2.9 convolution_convert_fusion
  357.9 21.2 %collective-permute-start.2 = (bf16[32,2560]{1,0:T(8,128)(2,1)S(1)}, bf16[32,2560]{1,0:T(8,128)(2,1)S(1)}, u32[]{:S(2)}, u32[]{:S(2)}) collective-permute-start(bf16[32,2560]{1,0:T(8,128)(2,1)S(1)} %get-tuple-element.228), channel_id=1, source_target_pairs={{0,512},{512,0},{32,544},{544,32},{64,576},{576,64},{96,608},{608,... | collective-permute-start | bytes 491528 | tf_op jit(solution)/shard_map/ppermute | solution.py:21
  379.1 5.2 collective-permute-start.3
  384.4 3.5 collective-permute-done.3
  387.9 1.8 gather_fusion
  389.7 339.5 %reduce-scatter.2.cloned.1.call-done = f32[80,512]{1,0:T(8,128)} async-done(((f32[2560,512]{1,0:T(8,128)}), f32[80,512]{1,0:T(8,128)}) %reduce-scatter.2.cloned.1.call-update) | async-done | bytes 163856 | tf_op jit(solution)/shard_map/reduce_scatter | solution.py:90
  729.2 448.3 %all-reduce.1 = bf16[80,512]{1,0:T(8,128)(2,1)} all-reduce(f32[80,512]{1,0:T(8,128)} %reduce-scatter.2.cloned.1.call-done), channel_id=1, replica_groups=mesh['dp'=32,'fsdp'=32] {'dp'}, use_global_device_ids=true, to_apply=%region_15.16 | all-reduce | flops 40960 | bytes 245760 | tf_op jit(solution)/shard_map/psum | solution.py:98
  (131 shorter events, 9.9 us)
Async XLA Ops:
  7.2 47.1 %copy-start.1 = (bf16[192,2560]{1,0:T(8,128)(2,1)S(1)}, bf16[192,2560]{1,0:T(8,128)(2,1)}, u32[]{:S(2)}) copy-start(bf16[192,2560]{1,0:T(8,128)(2,1)} %param.15) | copy-start | bytes 2949124
  7.2 347.8 %all-gather.2.cloned.1.call-start = ((), (), s32[]{:S(2)}) async-start(), calls=%async_computation.1 | async-start | bytes 2703360 | tf_op jit(solution)/shard_map/all_gather | solution.py:83
  7.9 721.3 %reduce-scatter.2.cloned.1.call-start = ((), (), s32[]{:S(2)}) async-start(), calls=%async_computation.2 | async-start | bytes 5406720 | tf_op jit(solution)/shard_map/reduce_scatter | solution.py:90
  8.6 45.7 %copy-start.5 = (s32[128]{0:T(128)}, s32[128]{0:T(128)S(1)}, u32[]{:S(2)}) copy-start(s32[128]{0:T(128)S(1)} %compare_select_fusion) | copy-start | bytes 1540
  9.7 45.3 %copy-start.4 = (s32[192]{0:T(256)}, s32[192]{0:T(256)S(1)}, u32[]{:S(2)}) copy-start(s32[192]{0:T(256)S(1)} %scatter_custom_fusion) | copy-start | bytes 2308
  10.3 54.9 %collective-permute-start = (s32[32]{0:T(128)}, s32[32]{0:T(128)S(1)}, u32[]{:S(2)}, u32[]{:S(2)}) collective-permute-start(s32[32]{0:T(128)} %get-tuple-element.236), channel_id=1, source_target_pairs={{0,512},{512,0},{32,544},{544,32},{64,576},{576,64},{96,608},{608,... | collective-permute-start | bytes 392 | tf_op jit(solution)/shard_map/ppermute | solution.py:21
  39.3 15.7 %copy-start.2 = (bf16[192,2560]{1,0:T(8,128)(2,1)S(1)}, bf16[192,2560]{1,0:T(8,128)(2,1)}, u32[]{:S(2)}) copy-start(bf16[192,2560]{1,0:T(8,128)(2,1)} %param.17) | copy-start | bytes 2949124
  39.3 29.3 %collective-permute-start.1 = (s32[32]{0:T(128)}, s32[32]{0:T(128)S(1)}, u32[]{:S(2)}, u32[]{:S(2)}) collective-permute-start(s32[32]{0:T(128)} %get-tuple-element.237), channel_id=1, source_target_pairs={{0,256},{256,0},{32,288},{288,32},{64,320},{320,64},{96,352},{352,... | collective-permute-start | bytes 392 | tf_op jit(solution)/shard_map/ppermute | solution.py:21
  45.2 9.9 copy-start
  46.0 50.0 %collective-permute-start.4 = (bf16[32,2560]{1,0:T(8,128)(2,1)}, bf16[32,2560]{1,0:T(8,128)(2,1)}, u32[]{:S(2)}, u32[]{:S(2)}) collective-permute-start(bf16[32,2560]{1,0:T(8,128)(2,1)} %get-tuple-element.226), channel_id=1, source_target_pairs={{0,512},{512,0},{32,544},{544,32},{64,576},{576,64},{96,608},{608,... | collective-permute-start | bytes 491528 | tf_op jit(solution)/shard_map/ppermute | solution.py:21
  47.9 48.1 %collective-permute-start.5 = (bf16[32,2560]{1,0:T(8,128)(2,1)}, bf16[32,2560]{1,0:T(8,128)(2,1)}, u32[]{:S(2)}, u32[]{:S(2)}) collective-permute-start(bf16[32,2560]{1,0:T(8,128)(2,1)} %get-tuple-element.227), channel_id=1, source_target_pairs={{0,256},{256,0},{32,288},{288,32},{64,320},{320,64},{96,352},{352,... | collective-permute-start | bytes 491528 | tf_op jit(solution)/shard_map/ppermute | solution.py:21
  55.0 3.1 slice-start.1
  55.1 3.3 slice-start.2
  57.9 0.9 copy-start.3
  57.9 0.9 slice-start.3
  68.7 27.4 %slice-start = ((bf16[192,2560]{1,0:T(8,128)(2,1)}), bf16[128,2560]{1,0:T(8,128)(2,1)S(1)}, s32[]{:S(2)}) async-start(bf16[192,2560]{1,0:T(8,128)(2,1)} %copy-done), calls=%async_computation.3 | async-start | bytes 1310720 | tf_op jit(solution)/shard_map/slice | solution.py:113
  100.3 284.0 %copy-start.6 = (s32[128]{0:T(128)S(1)}, s32[128]{0:T(128)}, u32[]{:S(2)}) copy-start(s32[128]{0:T(128)} %copy-done.5) | copy-start | bytes 1540
  357.9 26.5 %collective-permute-start.2 = (bf16[32,2560]{1,0:T(8,128)(2,1)S(1)}, bf16[32,2560]{1,0:T(8,128)(2,1)S(1)}, u32[]{:S(2)}, u32[]{:S(2)}) collective-permute-start(bf16[32,2560]{1,0:T(8,128)(2,1)S(1)} %get-tuple-element.228), channel_id=1, source_target_pairs={{0,512},{512,0},{32,544},{544,32},{64,576},{576,64},{96,608},{608,... | collective-permute-start | bytes 491528 | tf_op jit(solution)/shard_map/ppermute | solution.py:21
  379.1 8.7 collective-permute-start.3
Sparse Core Ops, SparseCore 0:
  10.7 344.2 all-gather.1
  358.4 370.8 reduce-scatter.1
where the time goes:
time: 1190 us; the launch traced here: 1180 us
  waiting for transfers between devices  622 us (52%)
  blocking collectives  448 us (38%)
  starting transfers between devices  64.8 us (5%)
  matrix products  17.1 us (1%)
  local copies, waits for them, and re-layouts  15.6 us (1%)
  between operations  14.4 us (1%)
    psum x1, blocking collectives, weight_gradient(): return lax.psum(summed, 'dp').astype(jnp.bfloat16)  448 us
    reduce_scatter x1, waiting for transfers between devices, weight_gradient(): lax.psum_scatter(lax.dot_general(rows_in, grads_in, (((0,), (0,)), ((), (...  339 us
    all_gather x1, waiting for transfers between devices, project_back(): lax.all_gather(weight_shard, 'fsdp', axis=0, tiled=True)  255 us
    ppermute x6, starting transfers between devices, swapped(): return lax.ppermute(block, axis, route)  64.8 us
    ppermute x6, waiting for transfers between devices, swapped(): return lax.ppermute(block, axis, route)  27.1 us
  transfers between devices with their start and end apart: 8, of which 4 were waited for; matrix products, arithmetic and copies ran while one was open for 3% of the time, Pallas kernels for 0%

commit v1 on v0

v1 whole, which is shorter than its diff:
```python
import functools
import math

import jax
import jax.numpy as jnp
from jax import lax
from jax.experimental import pallas as pl
from jax.experimental.pallas import tpu as pltpu
from jax.sharding import PartitionSpec as P

KVH = 4
GROUP = 5
HD = 128
SECTIONS = 2
PLANE = 16
DEPTH = 16
ROWS = 24
CUTS = 4
BOTH = ("dp", "fsdp")
BF16 = jnp.bfloat16
F32 = jnp.float32


def swapped(block, axis, distance):
    route = [(low, low ^ distance) for low in range(lax.axis_size(axis))]
    return lax.ppermute(block, axis, route)


def after(value, *others):
    return lax.optimization_barrier((value, *others))[0]


def attend_part(q_ref, k_ref, c_ref, low, count, allowed):
    rows = slice(low, low + count)
    query = jnp.concatenate([q_ref[rows, g * HD : (g + 1) * HD] for g in range(GROUP)], axis=0)
    context = jnp.concatenate([c_ref[rows, g * HD : (g + 1) * HD] for g in range(GROUP)], axis=0)
    scores = lax.dot_general(
        k_ref[rows, :], query, (((1,), (1,)), ((), ())), preferred_element_type=F32
    ) * (1.0 / math.sqrt(HD))
    bias = jnp.where(allowed, 0.0, -jnp.inf)
    masked = scores + jnp.concatenate([bias] * GROUP, axis=1)
    exponent = jnp.exp(masked - jnp.max(masked, axis=0, keepdims=True))
    probs = exponent * (1.0 / jnp.sum(exponent, axis=0, keepdims=True))
    return jnp.dot(probs.astype(BF16), context, preferred_element_type=F32).astype(BF16)


def attend_kernel(tok, block, col_ref, row_ref, q_ref, k_ref, c_ref, out_ref):
    for low, count in ((0, tok), (tok, SECTIONS * block)):
        col = col_ref[low : low + count, :]
        row = row_ref[:, low : low + count]
        j = lax.broadcasted_iota(jnp.int32, (count, count), 0)
        i = lax.broadcasted_iota(jnp.int32, (count, count), 1)
        same = (col == row) & (row >= 0) & (j <= i)
        if low:
            same = same & ((j < block) == (i < block))
        out_ref[low : low + count, :] = attend_part(q_ref, k_ref, c_ref, low, count, same | (i == j))


def attend(queries, key_rows, context_grad, ids, tok, block):
    slots = queries.shape[0]
    wide = pl.BlockSpec((slots, GROUP * HD), lambda h: (0, h))
    thin = pl.BlockSpec((slots, HD), lambda h: (0, h))
    return pl.pallas_call(
        functools.partial(attend_kernel, tok, block),
        grid=(KVH,),
        in_specs=[
            pl.BlockSpec((slots, 1), lambda h: (0, 0)),
            pl.BlockSpec((1, slots), lambda h: (0, 0)),
            wide,
            thin,
            wide,
        ],
        out_specs=thin,
        out_shape=jax.ShapeDtypeStruct((slots, KVH * HD), BF16),
        name="attend",
    )(ids.reshape(slots, 1), ids.reshape(1, slots), queries, key_rows, context_grad)


def gradient_kernel(core_ref, slot_ref, main_ref, first_ref, second_ref, act_ref, rows_ref, keep_ref, send_ref, whole):
    tok = slot_ref.shape[0]

    @pl.when(pl.program_id(0) == 0)
    def _():
        held = jnp.concatenate([main_ref[...], first_ref[...], second_ref[...]], axis=0)
        slots = lax.broadcasted_iota(jnp.int32, (tok, held.shape[0]), 1)
        chosen = (slot_ref[...] == slots).astype(F32).astype(BF16)
        rows_ref[...] = jnp.dot(chosen, held, preferred_element_type=F32).astype(BF16)

    whole[...] = lax.dot_general(
        act_ref[...], rows_ref[...], (((0,), (0,)), ((), ())), preferred_element_type=F32
    )
    core = core_ref[0]
    shard = whole.shape[0] // (2 * keep_ref.shape[1])
    for target, parity in ((keep_ref, core), (send_ref, 1 - core)):
        for z in range(keep_ref.shape[1]):
            for cut in range(CUTS):
                size = min(ROWS, shard - cut * ROWS)
                start = pl.multiple_of(z * 2 * shard + parity * shard + cut * ROWS, 8)
                part = whole[pl.ds(start, size), :]
                if size < ROWS:
                    part = jnp.concatenate([part, jnp.zeros((ROWS - size, part.shape[1]), F32)], axis=0)
                for k in range(CUTS):
                    target[cut * CUTS + k, z] = part[:, k * HD : (k + 1) * HD].astype(BF16)


def gradient_pieces(core, send_slot, main, first, second, activations):
    tok, features = activations.shape
    width = main.shape[1]
    steps = 4
    held = pl.BlockSpec((tok, width), lambda m, *_: (0, 0))
    back = pl.BlockSpec(first.shape, lambda m, *_: (0, 0))
    pieces = pl.BlockSpec((CUTS * CUTS, DEPTH // steps, ROWS, HD), lambda m, *_: (0, m, 0, 0))
    shape = jax.ShapeDtypeStruct((CUTS * CUTS, DEPTH, ROWS, HD), BF16)
    return pl.pallas_call(
        gradient_kernel,
        grid_spec=pltpu.PrefetchScalarGridSpec(
            num_scalar_prefetch=1,
            grid=(steps,),
            in_specs=[
                pl.BlockSpec((tok, 1), lambda m, *_: (0, 0)),
                held,
                back,
                back,
                pl.BlockSpec((tok, features // steps), lambda m, *_: (0, m)),
            ],
            out_specs=[held, pieces, pieces],
            scratch_shapes=[pltpu.VMEM((features // steps, width), F32)],
        ),
        out_shape=[jax.ShapeDtypeStruct((tok, width), BF16), shape, shape],
        compiler_params=pltpu.CompilerParams(vmem_limit_bytes=24 * 2**20),
        name="gradient_pieces",
    )(core, send_slot.reshape(tok, 1), main, first, second, activations)


def project_kernel(core_ref, rows_ref, own_ref, other_ref, out_ref, whole):
    core = core_ref[0]
    shard = whole.shape[0] // (2 * own_ref.shape[1])
    for source, parity in ((own_ref, core), (other_ref, 1 - core)):
        for z in range(own_ref.shape[1]):
            for cut in range(CUTS):
                size = min(ROWS, shard - cut * ROWS)
                start = pl.multiple_of(z * 2 * shard + parity * shard + cut * ROWS, 8)
                for k in range(CUTS):
                    part = source[cut * CUTS + k, z].astype(F32)
                    whole[pl.ds(start, size), k * HD : (k + 1) * HD] = part[:size]
    out_ref[...] = lax.dot_general(
        rows_ref[...], whole[...].astype(BF16), (((1,), (1,)), ((), ())), preferred_element_type=F32
    ).astype(BF16)


def project_back(core, row_grads, own, other):
    tok, width = row_grads.shape
    steps = 4
    features = 2 * DEPTH * 80
    pieces = pl.BlockSpec((CUTS * CUTS, DEPTH // steps, ROWS, HD), lambda m, *_: (0, m, 0, 0))
    return pl.pallas_call(
        project_kernel,
        grid_spec=pltpu.PrefetchScalarGridSpec(
            num_scalar_prefetch=1,
            grid=(steps,),
            in_specs=[pl.BlockSpec((tok, width), lambda m, *_: (0, 0)), pieces, pieces],
            out_specs=pl.BlockSpec((tok, features // steps), lambda m, *_: (0, m)),
            scratch_shapes=[pltpu.VMEM((features // steps, width), F32)],
        ),
        out_shape=jax.ShapeDtypeStruct((tok, features), BF16),
        compiler_params=pltpu.CompilerParams(vmem_limit_bytes=24 * 2**20),
        name="project_back",
    )(core, row_grads, own, other)


def plane_exchange(pieces):
    groups = [list(range(half * PLANE, (half + 1) * PLANE)) for half in range(2)]
    return lax.all_to_all(pieces, "dp", 0, 0, axis_index_groups=groups)


def plane_gather(piece):
    return plane_exchange(jnp.broadcast_to(piece[None], (PLANE, *piece.shape)))


def depth_gather(piece):
    groups = [[2 * z + core for z in range(DEPTH)] for core in range(2)]
    return lax.all_to_all(
        jnp.broadcast_to(piece[None], (DEPTH, *piece.shape)), "fsdp", 0, 0, axis_index_groups=groups
    )


def depth_exchange(pieces):
    count = 2 * DEPTH
    groups = [
        [(half * PLANE + at) * count + 2 * z + core for half in range(2) for z in range(DEPTH)]
        for at in range(PLANE)
        for core in range(2)
    ]
    return lax.all_to_all(
        jnp.concatenate([pieces, pieces], axis=0), BOTH, 0, 0, axis_index_groups=groups
    )


def total(parts):
    return jnp.sum(parts.astype(F32), axis=0).astype(BF16)


def cut_up(shard):
    padded = jnp.pad(shard, ((0, CUTS * ROWS - shard.shape[0]), (0, 0)))
    return padded.reshape(CUTS, ROWS, CUTS, HD).transpose(0, 2, 1, 3).reshape(CUTS * CUTS, ROWS, HD)


def put_together(pieces, rows):
    whole = pieces.reshape(CUTS, CUTS, ROWS, HD).transpose(0, 2, 1, 3)
    return whole.reshape(CUTS * ROWS, CUTS * HD)[:rows]


def local(activations, value_weight, queries, key_rows, context_grad, segment, send_slot):
    tok = activations.shape[0]
    block = (queries.shape[0] - tok) // SECTIONS
    half = lax.axis_size("dp") // 2
    place = lax.axis_index("dp") % PLANE
    core = (lax.axis_index("fsdp") % 2).astype(jnp.int32).reshape(1)

    slots = tok + jnp.arange(SECTIONS * block, dtype=jnp.int32)
    taken = send_slot[None, :] == slots[:, None]
    sent = jnp.max(jnp.where(taken, segment[None, :], -1), axis=1)
    got = [
        swapped(sent[s * block : (s + 1) * block], "dp", half >> s) for s in range(SECTIONS)
    ]

    piece = lax.dynamic_index_in_dim(cut_up(value_weight), place, 0, keepdims=False)
    depth_weight = depth_gather(after(piece, sent))

    ids = after(jnp.concatenate([segment, *got]), depth_weight)
    slot_grads = attend(queries, key_rows, context_grad, ids, tok, block)
    returned = [
        swapped(slot_grads[tok + s * block : tok + (s + 1) * block], "dp", half >> s)
        for s in range(SECTIONS)
    ]

    own_weight = plane_gather(after(depth_weight, slot_grads))
    first, second, own_weight = lax.optimization_barrier((*returned, own_weight))
    other_weight = swapped(own_weight, "fsdp", 1)

    row_grads, keep, send = gradient_pieces(core, send_slot, slot_grads[:tok], first, second, activations)
    came = swapped(send, "fsdp", 1)
    input_grad = project_back(core, row_grads, own_weight, other_weight)

    plane_part = total(plane_exchange((keep.astype(F32) + came.astype(F32)).astype(BF16)))
    depth_part = total(depth_exchange(plane_part))
    weight_grad = put_together(plane_gather(depth_part), value_weight.shape[0])
    return (input_grad, weight_grad)


def solution(mesh):
    rows = P(("dp", "fsdp"), None)
    flat = P(("dp", "fsdp"))
    return jax.shard_map(
        local,
        mesh=mesh,
        in_specs=(rows, P("fsdp", None), rows, rows, rows, flat, flat),
        out_specs=(rows, P("fsdp", None)),
        check_vma=False,
    )
```

time: 1190 us -> 201 us (0.17)
  the two profiles are of different devices: /device:TPU:22 before, /device:TPU:2 now
where the time goes in v1:
time: 201 us; the launch traced here: 200 us
  starting transfers between devices  96 us (48%)
  waiting for transfers between devices  56.8 us (28%)
  blocking collectives  27.8 us (14%)
  Pallas kernels  10.1 us (5%)
  local copies, waits for them, and re-layouts  5.4 us (3%)
  other arithmetic  2.95 us (1%)
    ppermute x6, starting transfers between devices, swapped(): return lax.ppermute(block, axis, route)  35.6 us
    all_to_all x1, waiting for transfers between devices, depth_exchange(): lax.all_to_all(jnp.concatenate([pieces, pieces], axis=0), BOTH, 0, 0, axi...  34 us
    all_to_all x1, blocking collectives, plane_exchange(): return lax.all_to_all(pieces, 'dp', 0, 0, axis_index_groups=groups)  27.8 us
    all_to_all x1, starting transfers between devices, depth_gather(): lax.all_to_all(jnp.broadcast_to(piece[None], (DEPTH, *piece.shape)), 'fsd...  25.9 us
    all_to_all x1, starting transfers between devices, depth_exchange(): lax.all_to_all(jnp.concatenate([pieces, pieces], axis=0), BOTH, 0, 0, axi...  21 us
    ppermute x6, waiting for transfers between devices, swapped(): return lax.ppermute(block, axis, route)  19.4 us
    all_to_all x2, starting transfers between devices, plane_exchange(): return lax.all_to_all(pieces, 'dp', 0, 0, axis_index_groups=groups)  13.6 us
    pallas_call x1, Pallas kernels, attend(): pl.pallas_call(functools.partial(attend_kernel, tok, block), grid=(KVH,),...  4.87 us
  transfers between devices with their start and end apart: 10, of which 5 were waited for; matrix products, arithmetic and copies ran while one was open for 1% of the time, Pallas kernels for 1%

profile of v1, /device:TPU:2, one launch (start us, length us, event | category | flops | bytes accessed | tf_op | source)
XLA Modules:
  0.0 199.8 jit_solution(12846514863079848737)
XLA Ops:
  0.7 0.9 pad.4
  1.6 0.9 select_reduce_fusion
  2.5 0.7 broadcast_in_dim.20
  3.1 25.9 %all-to-all-start = ((bf16[16,24,128]{2,1,0:T(8,128)(2,1)}), bf16[16,24,128]{2,1,0:T(8,128)(2,1)S(1)}, u32[]{:S(2)}, u32[]{:S(2)}) async-start(bf16[16,24,128]{2,1,0:T(8,128)(2,1)} %broadcast_in_dim.20), calls=%async_computation | async-start | bytes 196608 | tf_op jit(solution)/shard_map/all_to_all | solution.py:182
  29.0 0.1 fusion.1
  29.1 11.8 %collective-permute-start = (s32[32]{0:T(128)S(1)}, s32[32]{0:T(128)S(1)}, u32[]{:S(2)}, u32[]{:S(2)}) collective-permute-start(s32[32]{0:T(128)S(1)} %get-tuple-element.22), channel_id=1, source_target_pairs={{0,512},{32,544},{64,576},{96,608},{128,640},{160,672},{192,704},{... | collective-permute-start | bytes 392 | tf_op jit(solution)/shard_map/ppermute | solution.py:26
  41.0 4.0 %collective-permute-start.1 = (s32[32]{0:T(128)S(1)}, s32[32]{0:T(128)S(1)}, u32[]{:S(2)}, u32[]{:S(2)}) collective-permute-start(s32[32]{0:T(128)S(1)} %get-tuple-element.23), channel_id=1, source_target_pairs={{0,256},{32,288},{64,320},{96,352},{128,384},{160,416},{192,448},{... | collective-permute-start | bytes 392 | tf_op jit(solution)/shard_map/ppermute | solution.py:26
  45.0 7.9 %collective-permute-done = s32[32]{0:T(128)S(1)} collective-permute-done((s32[32]{0:T(128)S(1)}, s32[32]{0:T(128)S(1)}, u32[]{:S(2)}, u32[]{:S(2)}) %collective-permute-start) | collective-permute-done | bytes 160 | tf_op jit(solution)/shard_map/ppermute | solution.py:26
  52.9 0.7 pad_add_fusion
  53.6 0.8 copy.17.col_ref
  54.4 4.9 %attend.1 = bf16[192,512]{1,0:T(8,128)(2,1)} custom-call(s32[192,1]{1,0:T(8,128)} %copy.17.col_ref, s32[1,192]{1,0:T(1,128)} %bitcast.22, bf16[192,2560]{1,0:T(8,128)(2,1)} %q_ref.1, bf16[192,512]{1,0:T(8,128)(2,1)} %k_ref.1, bf16[192,2560]{1,0:T(8,128)(2,1)} %c_ref.1), custom_call_target="tpu_custom_call" | custom-call | tf_op jit(solution)/shard_map/attend/pallas_call | solution.py:63
  59.2 1.5 broadcast_in_dim.21
  60.7 7.6 %all-to-all-start.1 = ((bf16[16,16,24,128]{3,2,1,0:T(8,128)(2,1)}), bf16[16,16,24,128]{3,2,1,0:T(8,128)(2,1)S(1)}, u32[]{:S(2)}, u32[]{:S(2)}) async-start(bf16[16,16,24,128]{3,2,1,0:T(8,128)(2,1)} %broadcast_in_dim.21), calls=%async_computation.1 | async-start | bytes 3145728 | tf_op jit(solution)/shard_map/all_to_all | solution.py:173
  68.3 11.9 %collective-permute-start.2 = (bf16[32,512]{1,0:T(8,128)(2,1)S(1)}, bf16[32,512]{1,0:T(8,128)(2,1)S(1)}, u32[]{:S(2)}, u32[]{:S(2)}) collective-permute-start(bf16[32,512]{1,0:T(8,128)(2,1)S(1)} %get-tuple-element.21), channel_id=1, source_target_pairs={{0,512},{32,544},{64,576},{96,608},{128,640},{160,672},{192,704},{... | collective-permute-start | bytes 98312 | tf_op jit(solution)/shard_map/ppermute | solution.py:26
  80.2 4.0 %collective-permute-start.3 = (bf16[32,512]{1,0:T(8,128)(2,1)S(1)}, bf16[32,512]{1,0:T(8,128)(2,1)S(1)}, u32[]{:S(2)}, u32[]{:S(2)}) collective-permute-start(bf16[32,512]{1,0:T(8,128)(2,1)S(1)} %get-tuple-element.20), channel_id=1, source_target_pairs={{0,256},{32,288},{64,320},{96,352},{128,384},{160,416},{192,448},{... | collective-permute-start | bytes 98312 | tf_op jit(solution)/shard_map/ppermute | solution.py:26
  84.2 0.1 copy.18.slot_ref
  84.3 8.1 %collective-permute-done.2.first_ref = bf16[32,512]{1,0:T(8,128)(2,1)S(1)} collective-permute-done((bf16[32,512]{1,0:T(8,128)(2,1)S(1)}, bf16[32,512]{1,0:T(8,128)(2,1)S(1)}, u32[]{:S(2)}, u32[]{:S(2)}) %collective-permute-start.2) | collective-permute-done | bytes 32800 | tf_op jit(solution)/shard_map/ppermute | solution.py:26
  92.5 2.3 %gradient_pieces.1 = (bf16[128,512]{1,0:T(8,128)(2,1)S(1)}, bf16[16,16,24,128]{3,2,1,0:T(8,128)(2,1)S(1)}, bf16[16,16,24,128]{3,2,1,0:T(8,128)(2,1)S(1)}) custom-call(s32[1]{0:T(128)} %bitcast.core_ref, s32[128,1]{1,0:T(8,128)S(1)} %copy.18.slot_ref, bf16[128,512]{1,0:T(8,128)(2,1)S(1)} %slice.24.main_ref, ...), custom_call_target="tpu_custom_call" | custom-call | tf_op jit(solution)/shard_map/gradient_pieces/pallas_call | solution.py:114
  94.8 1.9 collective-permute-start.5
  96.7 3.4 %collective-permute-done.5 = bf16[16,16,24,128]{3,2,1,0:T(8,128)(2,1)S(1)} collective-permute-done((bf16[16,16,24,128]{3,2,1,0:T(8,128)(2,1)S(1)}, bf16[16,16,24,128]{3,2,1,0:T(8,128)(2,1)S(1)}, u32[]{:S(2)}, u32[]{:S(2)}) %collective-permute-start.5) | collective-permute-done | bytes 1572896 | tf_op jit(solution)/shard_map/ppermute | solution.py:26
  100.1 0.4 add_convert_fusion
  100.5 27.8 %all_to_all.25 = bf16[16,16,24,128]{3,2,1,0:T(8,128)(2,1)S(1)} all-to-all(bf16[16,16,24,128]{3,2,1,0:T(8,128)(2,1)S(1)} %add_convert_fusion), channel_id=1, replica_groups={{0,32,64,96,128,160,192,224,256,288,320,352,384,416,448,480},{512,544,5..., dimensions={0} | all-to-all | bytes 3145728 | tf_op jit(solution)/shard_map/all_to_all | solution.py:173
  128.3 0.2 reduce_sum.24
  128.5 0.7 pad_maximum_fusion
  129.2 21.0 %all-to-all-start.3 = ((bf16[32,24,128]{2,1,0:T(8,128)(2,1)}), bf16[32,24,128]{2,1,0:T(8,128)(2,1)S(1)}, u32[]{:S(2)}, u32[]{:S(2)}) async-start(bf16[32,24,128]{2,1,0:T(8,128)(2,1)} %pad_maximum_fusion), calls=%async_computation.3 | async-start | bytes 393216 | tf_op jit(solution)/shard_map/all_to_all | solution.py:194
  150.2 1.9 collective-permute-start.4
  152.2 34.0 %all-to-all-done.3 = bf16[32,24,128]{2,1,0:T(8,128)(2,1)S(1)} async-done(((bf16[32,24,128]{2,1,0:T(8,128)(2,1)}), bf16[32,24,128]{2,1,0:T(8,128)(2,1)S(1)}, u32[]{:S(2)}, u32[]{:S(2)}) %all-to-all-start.3) | async-done | bytes 196640 | tf_op jit(solution)/shard_map/all_to_all | solution.py:194
  186.2 0.6 broadcast_in_dim.22
  186.8 6.0 %all-to-all-start.4 = ((bf16[16,24,128]{2,1,0:T(8,128)(2,1)}), bf16[16,24,128]{2,1,0:T(8,128)(2,1)S(1)}, u32[]{:S(2)}, u32[]{:S(2)}) async-start(bf16[16,24,128]{2,1,0:T(8,128)(2,1)} %broadcast_in_dim.22), calls=%async_computation.4 | async-start | bytes 196608 | tf_op jit(solution)/shard_map/all_to_all | solution.py:173
  192.8 2.9 %project_back.1 = bf16[128,2560]{1,0:T(8,128)(2,1)} custom-call(s32[1]{0:T(128)} %bitcast.core_ref, bf16[128,512]{1,0:T(8,128)(2,1)S(1)} %get-tuple-element.16.rows_ref, bf16[16,16,24,128]{3,2,1,0:T(8,128)(2,1)S(1)} %all-to-all-done.1.own_ref, bf16[16,16,24,128]{3,2,1,0:T(8,128)(2,1)S(1)} %collective-permute-done.4.other_ref), custom_call_target="tpu_custom_call" | custom-call | tf_op jit(solution)/shard_map/project_back/pallas_call | solution.py:156
  195.7 3.4 %all-to-all-done.4 = bf16[16,24,128]{2,1,0:T(8,128)(2,1)S(1)} async-done(((bf16[16,24,128]{2,1,0:T(8,128)(2,1)}), bf16[16,24,128]{2,1,0:T(8,128)(2,1)S(1)}, u32[]{:S(2)}, u32[]{:S(2)}) %all-to-all-start.4) | async-done | bytes 98336 | tf_op jit(solution)/shard_map/all_to_all | solution.py:173
  199.2 0.6 slice.27
  (22 shorter events, 0.2 us)
Async XLA Ops:
  3.1 50.5 %all-to-all-start = ((bf16[16,24,128]{2,1,0:T(8,128)(2,1)}), bf16[16,24,128]{2,1,0:T(8,128)(2,1)S(1)}, u32[]{:S(2)}, u32[]{:S(2)}) async-start(bf16[16,24,128]{2,1,0:T(8,128)(2,1)} %broadcast_in_dim.20), calls=%async_computation | async-start | bytes 196608 | tf_op jit(solution)/shard_map/all_to_all | solution.py:182
  29.1 23.7 %collective-permute-start = (s32[32]{0:T(128)S(1)}, s32[32]{0:T(128)S(1)}, u32[]{:S(2)}, u32[]{:S(2)}) collective-permute-start(s32[32]{0:T(128)S(1)} %get-tuple-element.22), channel_id=1, source_target_pairs={{0,512},{32,544},{64,576},{96,608},{128,640},{160,672},{192,704},{... | collective-permute-start | bytes 392 | tf_op jit(solution)/shard_map/ppermute | solution.py:26
  41.0 11.9 %collective-permute-start.1 = (s32[32]{0:T(128)S(1)}, s32[32]{0:T(128)S(1)}, u32[]{:S(2)}, u32[]{:S(2)}) collective-permute-start(s32[32]{0:T(128)S(1)} %get-tuple-element.23), channel_id=1, source_target_pairs={{0,256},{32,288},{64,320},{96,352},{128,384},{160,416},{192,448},{... | collective-permute-start | bytes 392 | tf_op jit(solution)/shard_map/ppermute | solution.py:26
  53.6 0.8 copy-start.2
  60.7 7.6 %copy-start.1 = (bf16[192,512]{1,0:T(8,128)(2,1)S(1)}, bf16[192,512]{1,0:T(8,128)(2,1)}, u32[]{:S(2)}) copy-start(bf16[192,512]{1,0:T(8,128)(2,1)} %attend.1) | copy-start | bytes 589828
  60.7 23.5 %copy-start.3 = (s32[128]{0:T(128)S(1)}, s32[128]{0:T(128)}, u32[]{:S(2)}) copy-start(s32[128]{0:T(128)} %param.13) | copy-start | bytes 1540
  60.7 31.8 %copy-start = (bf16[128,2560]{1,0:T(8,128)(2,1)S(1)}, bf16[128,2560]{1,0:T(8,128)(2,1)}, u32[]{:S(2)}) copy-start(bf16[128,2560]{1,0:T(8,128)(2,1)} %act_ref.1) | copy-start | bytes 1966084
  60.7 31.8 %all-to-all-start.1 = ((bf16[16,16,24,128]{3,2,1,0:T(8,128)(2,1)}), bf16[16,16,24,128]{3,2,1,0:T(8,128)(2,1)S(1)}, u32[]{:S(2)}, u32[]{:S(2)}) async-start(bf16[16,16,24,128]{3,2,1,0:T(8,128)(2,1)} %broadcast_in_dim.21), calls=%async_computation.1 | async-start | bytes 3145728 | tf_op jit(solution)/shard_map/all_to_all | solution.py:173
  68.3 24.1 %collective-permute-start.2 = (bf16[32,512]{1,0:T(8,128)(2,1)S(1)}, bf16[32,512]{1,0:T(8,128)(2,1)S(1)}, u32[]{:S(2)}, u32[]{:S(2)}) collective-permute-start(bf16[32,512]{1,0:T(8,128)(2,1)S(1)} %get-tuple-element.21), channel_id=1, source_target_pairs={{0,512},{32,544},{64,576},{96,608},{128,640},{160,672},{192,704},{... | collective-permute-start | bytes 98312 | tf_op jit(solution)/shard_map/ppermute | solution.py:26
  80.2 12.3 %collective-permute-start.3 = (bf16[32,512]{1,0:T(8,128)(2,1)S(1)}, bf16[32,512]{1,0:T(8,128)(2,1)S(1)}, u32[]{:S(2)}, u32[]{:S(2)}) collective-permute-start(bf16[32,512]{1,0:T(8,128)(2,1)S(1)} %get-tuple-element.20), channel_id=1, source_target_pairs={{0,256},{32,288},{64,320},{96,352},{128,384},{160,416},{192,448},{... | collective-permute-start | bytes 98312 | tf_op jit(solution)/shard_map/ppermute | solution.py:26
  94.8 5.3 %collective-permute-start.5 = (bf16[16,16,24,128]{3,2,1,0:T(8,128)(2,1)S(1)}, bf16[16,16,24,128]{3,2,1,0:T(8,128)(2,1)S(1)}, u32[]{:S(2)}, u32[]{:S(2)}) collective-permute-start(bf16[16,16,24,128]{3,2,1,0:T(8,128)(2,1)S(1)} %get-tuple-element.19), channel_id=1, source_target_pairs={{0,1},{1,0},{2,3},{3,2},{4,5},{5,4},{6,7},{7,6},{8,9},{9,8},{10,11... | collective-permute-start | bytes 4718600 | tf_op jit(solution)/shard_map/ppermute | solution.py:26
  129.2 56.9 %all-to-all-start.3 = ((bf16[32,24,128]{2,1,0:T(8,128)(2,1)}), bf16[32,24,128]{2,1,0:T(8,128)(2,1)S(1)}, u32[]{:S(2)}, u32[]{:S(2)}) async-start(bf16[32,24,128]{2,1,0:T(8,128)(2,1)} %pad_maximum_fusion), calls=%async_computation.3 | async-start | bytes 393216 | tf_op jit(solution)/shard_map/all_to_all | solution.py:194
  150.2 42.6 %collective-permute-start.4 = (bf16[16,16,24,128]{3,2,1,0:T(8,128)(2,1)S(1)}, bf16[16,16,24,128]{3,2,1,0:T(8,128)(2,1)S(1)}, u32[]{:S(2)}, u32[]{:S(2)}) collective-permute-start(bf16[16,16,24,128]{3,2,1,0:T(8,128)(2,1)S(1)} %all-to-all-done.1.own_ref), channel_id=1, source_target_pairs={{0,1},{1,0},{2,3},{3,2},{4,5},{5,4},{6,7},{7,6},{8,9},{9,8},{10,11... | collective-permute-start | bytes 4718600 | tf_op jit(solution)/shard_map/ppermute | solution.py:26
  186.8 12.3 %all-to-all-start.4 = ((bf16[16,24,128]{2,1,0:T(8,128)(2,1)}), bf16[16,24,128]{2,1,0:T(8,128)(2,1)S(1)}, u32[]{:S(2)}, u32[]{:S(2)}) async-start(bf16[16,24,128]{2,1,0:T(8,128)(2,1)} %broadcast_in_dim.22), calls=%async_computation.4 | async-start | bytes 196608 | tf_op jit(solution)/shard_map/all_to_all | solution.py:173

commit v2 on v1

v2 whole, which is shorter than its diff:
```python
import functools
import math

import jax
import jax.numpy as jnp
from jax import lax
from jax.experimental import pallas as pl
from jax.experimental.pallas import tpu as pltpu
from jax.sharding import PartitionSpec as P

KVH = 4
GROUP = 5
HD = 128
SECTIONS = 2
LEAST = 16
PLANE = 16
DEPTH = 16
CUTS = 4
ROWS = 24
BOTH = ("dp", "fsdp")
BF16 = jnp.bfloat16
F32 = jnp.float32
WIDTH = KVH * HD
FEATURES = KVH * GROUP * HD
SUMS = FEATURES
PROBS = SUMS + 2 * WIDTH
MESSAGE = PROBS + 2 * KVH * HD
SCALE = 1.0 / math.sqrt(HD)
ON_COLUMNS = (((1,), (1,)), ((), ()))


def swapped(block, axis, distance):
    route = [(low, low ^ distance) for low in range(lax.axis_size(axis))]
    return lax.ppermute(block, axis, route)


def softmax_down(scores, allowed):
    masked = jnp.where(allowed, scores * SCALE, -jnp.inf)
    exponent = jnp.exp(masked - jnp.max(masked, axis=0, keepdims=True))
    return (exponent * (1.0 / jnp.sum(exponent, axis=0, keepdims=True))).astype(BF16)


def iota(shape, dim):
    return lax.broadcasted_iota(jnp.int32, shape, dim)


def message_kernel(block, q_ref, k_ref, c_ref, *out_refs):
    for section, out_ref in enumerate(out_refs):
        low = section * block
        copies_ref = None
        if section == 0:
            copies_ref, out_ref = out_ref, out_ref.at[0]
        out_ref[:, :FEATURES] = c_ref[low + LEAST : low + block, :]
        pad = jnp.zeros((HD - GROUP * LEAST, HD), BF16)
        for h in range(KVH):

            def stacked(ref, start):
                heads = [ref[start : start + LEAST, (h * GROUP + g) * HD : (h * GROUP + g + 1) * HD] for g in range(GROUP)]
                return jnp.concatenate([*heads, pad], axis=0)

            keys = k_ref[low : low + block, h * HD : (h + 1) * HD]
            scores = lax.dot_general(keys, stacked(q_ref, low + LEAST), ON_COLUMNS, preferred_element_type=F32)
            allowed = iota((block, HD), 0) <= iota((block, HD), 1) % LEAST + LEAST
            probs = softmax_down(scores, allowed)
            at = PROBS + 2 * h * HD
            out_ref[:, at : at + HD] = probs[:LEAST]
            out_ref[:, at + HD : at + 2 * HD] = probs[LEAST:]

            scores = lax.dot_general(keys[:LEAST], stacked(q_ref, low), ON_COLUMNS, preferred_element_type=F32)
            allowed = iota((LEAST, HD), 0) <= iota((LEAST, HD), 1) % LEAST
            probs = softmax_down(scores, allowed)
            sums = jnp.dot(probs, stacked(c_ref, low), preferred_element_type=F32)
            coarse = sums.astype(BF16)
            at = SUMS + h * HD
            out_ref[:, at : at + HD] = coarse
            out_ref[:, at + WIDTH : at + WIDTH + HD] = (sums - coarse.astype(F32)).astype(BF16)
        if copies_ref is not None:
            copies_ref[1] = copies_ref[0]


def messages(queries, key_rows, context_grad, tok, block):
    both = SECTIONS * block
    last = tok // both
    specs = [pl.BlockSpec((both, x.shape[1]), lambda i: (last, 0)) for x in (queries, key_rows, context_grad)]
    shape = (block - LEAST, MESSAGE)
    return pl.pallas_call(
        functools.partial(message_kernel, block),
        grid=(1,),
        in_specs=specs,
        out_specs=[pl.BlockSpec((2, *shape), lambda i: (0, 0, 0)), pl.BlockSpec(shape, lambda i: (0, 0))],
        out_shape=[jax.ShapeDtypeStruct((2, *shape), BF16), jax.ShapeDtypeStruct(shape, BF16)],
        compiler_params=pltpu.CompilerParams(vmem_limit_bytes=24 * 2**20),
        name="messages",
    )(queries, key_rows, context_grad)


def sent_block(slot, message_ref, low, block):
    inside = (slot >= low) & (slot < low + block)
    count = jnp.sum(inside.astype(jnp.int32), axis=0, keepdims=True)
    pad = jnp.zeros((HD - GROUP * LEAST, HD), BF16)
    heads = []
    for h in range(KVH):
        at = PROBS + 2 * h * HD
        probs = jnp.concatenate([message_ref[:, at : at + HD], message_ref[:, at + HD : at + 2 * HD]], axis=0)
        held = iota(probs.shape, 1) % LEAST + LEAST < count
        probs = jnp.where(held, probs.astype(F32), 0.0).astype(BF16)
        rows = [message_ref[:, (h * GROUP + g) * HD : (h * GROUP + g + 1) * HD] for g in range(GROUP)]
        late = jnp.dot(probs, jnp.concatenate([*rows, pad], axis=0), preferred_element_type=F32)
        at = SUMS + h * HD
        early = message_ref[:, at : at + HD].astype(F32) + message_ref[:, at + WIDTH : at + WIDTH + HD].astype(F32)
        heads.append(late + jnp.concatenate([early, jnp.zeros((block - LEAST, HD), F32)], axis=0))
    return jnp.concatenate(heads, axis=1).astype(BF16)


def attend_kernel(col_ref, row_ref, q_ref, k_ref, c_ref, behind_ref, out_ref):
    del behind_ref
    tok = q_ref.shape[0]
    query = jnp.concatenate([q_ref[:, g * HD : (g + 1) * HD] for g in range(GROUP)], axis=0)
    context = jnp.concatenate([c_ref[:, g * HD : (g + 1) * HD] for g in range(GROUP)], axis=0)
    allowed = (col_ref[...] == row_ref[...]) & (iota((tok, tok), 0) <= iota((tok, tok), 1))
    bias = jnp.where(allowed, 0.0, -jnp.inf)
    scores = lax.dot_general(k_ref[...], query, ON_COLUMNS, preferred_element_type=F32) * SCALE
    masked = scores + jnp.concatenate([bias] * GROUP, axis=1)
    exponent = jnp.exp(masked - jnp.max(masked, axis=0, keepdims=True))
    probs = (exponent * (1.0 / jnp.sum(exponent, axis=0, keepdims=True))).astype(BF16)
    out_ref[...] = jnp.dot(probs, context, preferred_element_type=F32).astype(BF16)


def attend(queries, key_rows, context_grad, segment, behind):
    tok = segment.shape[0]
    wide = pl.BlockSpec((tok, GROUP * HD), lambda h: (0, h))
    thin = pl.BlockSpec((tok, HD), lambda h: (0, h))
    return pl.pallas_call(
        attend_kernel,
        grid=(KVH,),
        in_specs=[
            pl.BlockSpec((tok, 1), lambda h: (0, 0)),
            pl.BlockSpec((1, tok), lambda h: (0, 0)),
            wide,
            thin,
            wide,
            pl.BlockSpec(memory_space=pl.ANY),
        ],
        out_specs=thin,
        out_shape=jax.ShapeDtypeStruct((tok, WIDTH), BF16),
        name="attend",
    )(segment.reshape(tok, 1), segment.reshape(1, tok), queries, key_rows, context_grad, behind)


def gradient_kernel(block, core_ref, half_ref, slot_ref, main_ref, first_ref, second_ref, act_ref, rows_ref, keep_ref, send_ref, whole):
    tok = slot_ref.shape[0]

    @pl.when(pl.program_id(0) == 0)
    def _():
        slot = slot_ref[...]
        refs = (first_ref.at[1 - half_ref[0]], second_ref)
        parts = [sent_block(slot, ref, tok + s * block, block) for s, ref in enumerate(refs)]
        held = jnp.concatenate([main_ref[...], *parts], axis=0)
        chosen = (slot == iota((tok, held.shape[0]), 1)).astype(F32).astype(BF16)
        rows_ref[...] = jnp.dot(chosen, held, preferred_element_type=F32).astype(BF16)

    whole[...] = lax.dot_general(
        act_ref[...], rows_ref[...], (((0,), (0,)), ((), ())), preferred_element_type=F32
    )
    core = core_ref[0]
    pairs = keep_ref.shape[1]
    shard = whole.shape[0] // (4 * pairs)
    upper = iota((8, WIDTH), 0) < 4
    for target, parity in ((keep_ref, core), (send_ref, 1 - core)):
        for pair in range(pairs):

            def rows(odd, start, size):
                at = (4 * pair + 2 * odd + parity) * shard + start
                return whole[pl.ds(pl.multiple_of(at, 8), size), :]

            for cut in range(CUTS):
                split = 16 * CUTS + 8 * (cut // 2)
                even, odd = rows(0, split, 8), pltpu.roll(rows(1, split, 8), 4, 0)
                mixed = jnp.where(upper, even, odd) if cut % 2 == 0 else jnp.where(upper, odd, even)
                piece = jnp.concatenate([rows(0, 16 * cut, 16), rows(1, 16 * cut, 16), mixed], axis=0).astype(BF16)
                for k in range(CUTS):
                    target[cut * CUTS + k, pair] = piece[:, k * HD : (k + 1) * HD]


def gradient_pieces(core, half, send_slot, main, first, second, activations, block):
    tok, features = activations.shape
    steps = 4
    held = pl.BlockSpec((tok, WIDTH), lambda m, *_: (0, 0))
    message = [pl.BlockSpec(x.shape, lambda m, *_, rank=x.ndim: (0,) * rank) for x in (first, second)]
    pieces = pl.BlockSpec((CUTS * CUTS, DEPTH // 2 // steps, 40, HD), lambda m, *_: (0, m, 0, 0))
    shape = jax.ShapeDtypeStruct((CUTS * CUTS, DEPTH // 2, 40, HD), BF16)
    return pl.pallas_call(
        functools.partial(gradient_kernel, block),
        grid_spec=pltpu.PrefetchScalarGridSpec(
            num_scalar_prefetch=2,
            grid=(steps,),
            in_specs=[
                pl.BlockSpec((tok, 1), lambda m, *_: (0, 0)),
                held,
                *message,
                pl.BlockSpec((tok, features // steps), lambda m, *_: (0, m)),
            ],
            out_specs=[held, pieces, pieces],
            scratch_shapes=[pltpu.VMEM((features // steps, WIDTH), F32)],
        ),
        out_shape=[jax.ShapeDtypeStruct((tok, WIDTH), BF16), shape, shape],
        compiler_params=pltpu.CompilerParams(vmem_limit_bytes=24 * 2**20),
        name="gradient_pieces",
    )(core, half, send_slot.reshape(tok, 1), main, first, second, activations)


def plane_sum_kernel(odd_ref, parts_ref, keep_ref, send_ref, whole):
    pairs, rows, _ = whole.shape
    for pair in range(pairs):
        whole[pair] = jnp.sum(parts_ref[:, pair * rows : (pair + 1) * rows, :].astype(F32), axis=0)
    odd = odd_ref[0]
    for target, parity in ((keep_ref, odd), (send_ref, 1 - odd)):
        for pair in range(whole.shape[0]):
            own = whole[pair, pl.ds(pl.multiple_of(parity * 16, 8), 16), :]
            target[pair] = jnp.concatenate([own, whole[pair, 32:40, :]], axis=0).astype(BF16)


def plane_sum(odd, parts, pairs, rows):
    count, _, lanes = parts.shape
    out = pl.BlockSpec((pairs, ROWS, lanes), lambda i, *_: (0, 0, 0))
    return pl.pallas_call(
        plane_sum_kernel,
        grid_spec=pltpu.PrefetchScalarGridSpec(
            num_scalar_prefetch=1,
            grid=(1,),
            in_specs=[pl.BlockSpec((count, pairs * rows, lanes), lambda i, *_: (0, 0, 0))],
            out_specs=[out, out],
            scratch_shapes=[pltpu.VMEM((pairs, rows, lanes), F32)],
        ),
        out_shape=[jax.ShapeDtypeStruct((pairs, ROWS, lanes), BF16)] * 2,
        compiler_params=pltpu.CompilerParams(vmem_limit_bytes=24 * 2**20),
        name="plane_sum",
    )(odd, parts)


def depth_sum_kernel(parts_ref, out_ref):
    total = jnp.sum(parts_ref[...].astype(F32), axis=0).astype(BF16)
    for at in range(out_ref.shape[0]):
        out_ref[at] = total


def depth_sum(parts):
    return pl.pallas_call(
        depth_sum_kernel,
        out_shape=jax.ShapeDtypeStruct((PLANE, *parts.shape[1:]), BF16),
        name="depth_sum",
    )(parts)


def join_kernel(odd_ref, pieces_ref, out_ref):
    odd = odd_ref[0]
    upper = iota((8, HD), 0) < 4
    for k in range(CUTS):
        lanes = slice(k * HD, (k + 1) * HD)
        tiles = []
        for cut in range(CUTS):
            out_ref[16 * cut : 16 * cut + 16, lanes] = pieces_ref[cut * CUTS + k, :16, :]
            tiles.append(pieces_ref[cut * CUTS + k, 16:, :].astype(F32))
        last = []
        for low, high in ((tiles[0], tiles[1]), (tiles[2], tiles[3])):
            from_odd = pltpu.roll(jnp.where(upper, high, low), 4, 0)
            last.append(jnp.where(odd == 1, from_odd, jnp.where(upper, low, high)))
        out_ref[16 * CUTS :, lanes] = jnp.concatenate(last, axis=0).astype(BF16)


def join(odd, pieces, rows):
    return pl.pallas_call(
        join_kernel,
        grid_spec=pltpu.PrefetchScalarGridSpec(
            num_scalar_prefetch=1,
            grid=(1,),
            in_specs=[pl.BlockSpec(pieces.shape, lambda i, *_: (0, 0, 0))],
            out_specs=pl.BlockSpec((rows, WIDTH), lambda i, *_: (0, 0)),
        ),
        out_shape=jax.ShapeDtypeStruct((rows, WIDTH), BF16),
        name="join",
    )(odd, pieces)


def project_kernel(core_ref, odd_ref, pair_ref, rows_ref, *refs):
    *source_refs, out_ref, whole = refs
    core, odd, swap = core_ref[0], odd_ref[0], pair_ref[0] % 2
    pairs = source_refs[0].shape[1]
    shard = whole.shape[0] // (4 * pairs)
    places = [(a, b) for b in (core, 1 - core) for a in (odd, 1 - odd)]
    for source, (z_parity, core_parity) in zip(source_refs, places, strict=True):
        for pair in range(pairs):
            for cut in range(CUTS):
                size = min(ROWS, shard - cut * ROWS)
                at = (4 * pair + 2 * z_parity + core_parity) * shard + cut * ROWS
                for k in range(CUTS):
                    part = source[cut * CUTS + k, pair ^ swap].astype(F32)
                    whole[pl.ds(pl.multiple_of(at, 8), size), k * HD : (k + 1) * HD] = part[:size]
    out_ref[...] = lax.dot_general(
        rows_ref[...], whole[...].astype(BF16), ON_COLUMNS, preferred_element_type=F32
    ).astype(BF16)


def project_back(core, odd, pair, row_grads, sources, features):
    tok, width = row_grads.shape
    steps = 4
    pieces = pl.BlockSpec((CUTS * CUTS, DEPTH // 2 // steps, ROWS, HD), lambda m, c, o, p: (0, m ^ (p[0] // 2), 0, 0))
    return pl.pallas_call(
        project_kernel,
        grid_spec=pltpu.PrefetchScalarGridSpec(
            num_scalar_prefetch=3,
            grid=(steps,),
            in_specs=[pl.BlockSpec((tok, width), lambda m, *_: (0, 0))] + [pieces] * len(sources),
            out_specs=pl.BlockSpec((tok, features // steps), lambda m, *_: (0, m)),
            scratch_shapes=[pltpu.VMEM((features // steps, width), F32)],
        ),
        out_shape=jax.ShapeDtypeStruct((tok, features), BF16),
        compiler_params=pltpu.CompilerParams(vmem_limit_bytes=24 * 2**20),
        name="project_back",
    )(core, odd, pair, row_grads, *sources)


def plane_exchange(pieces):
    groups = [list(range(half * PLANE, (half + 1) * PLANE)) for half in range(2)]
    return lax.all_to_all(pieces, "dp", 0, 0, axis_index_groups=groups)


def depth_gather(piece):
    pieces = piece[None]
    for bit in range(1, DEPTH.bit_length() - 1):
        pieces = jnp.concatenate([pieces, swapped(pieces, "fsdp", 2 << bit)], axis=0)
    return pieces.reshape(DEPTH // 2 * ROWS, HD)


def halves_exchange(copies):
    groups = [[at, at + PLANE] for at in range(PLANE)]
    return lax.all_to_all(copies, "dp", 0, 0, axis_index_groups=groups)


def depth_exchange(pieces):
    count = 2 * DEPTH
    groups = [
        [(half * PLANE + at) * count + 2 * z + core for half in range(2) for z in range(odd, DEPTH, 2)]
        for at in range(PLANE)
        for odd in range(2)
        for core in range(2)
    ]
    return lax.all_to_all(pieces, BOTH, 0, 0, axis_index_groups=groups)


def added(one, two):
    return (one.astype(F32) + two.astype(F32)).astype(BF16)


def cut_up(shard):
    padded = jnp.pad(shard, ((0, CUTS * ROWS - shard.shape[0]), (0, 0)))
    return padded.reshape(CUTS, ROWS, CUTS, HD).transpose(0, 2, 1, 3).reshape(CUTS * CUTS, ROWS, HD)


def local(activations, value_weight, queries, key_rows, context_grad, segment, send_slot):
    tok, features = activations.shape
    block = (queries.shape[0] - tok) // SECTIONS
    half = lax.axis_size("dp") // 2
    place = lax.axis_index("dp") % PLANE
    core, odd, pair, upper = (
        x.astype(jnp.int32).reshape(1)
        for x in (
            lax.axis_index("fsdp") % 2,
            lax.axis_index("fsdp") // 2 % 2,
            lax.axis_index("fsdp") // 4,
            lax.axis_index("dp") // half,
        )
    )

    piece = lax.dynamic_index_in_dim(cut_up(value_weight), place, 0, keepdims=False)
    first, second = messages(queries, key_rows, context_grad, tok, block)
    first = halves_exchange(first)
    second = swapped(second, "dp", half // 2)
    depth_weight = depth_gather(piece)
    main = attend(queries, key_rows, context_grad, segment, depth_weight)

    row_grads, keep, send = gradient_pieces(core, upper, send_slot, main, first, second, activations, block)
    came = swapped(send, "fsdp", 1)
    _, pairs, rows, _ = keep.shape
    gradient = added(keep, came).reshape(PLANE, pairs * rows, HD)
    weight = jnp.broadcast_to(depth_weight[None], (PLANE, *depth_weight.shape))
    parts = plane_exchange(jnp.concatenate([gradient, weight], axis=1))

    keep, send = plane_sum(odd, parts, pairs, rows)
    came = swapped(send, "fsdp", 2)
    depth_part, parts = lax.optimization_barrier((added(keep, came), parts))
    depth_parts = depth_exchange(jnp.concatenate([depth_part, depth_part], axis=0))

    weight = parts[:, pairs * rows :].reshape(CUTS * CUTS, DEPTH // 2, ROWS, HD)
    weights = [weight, swapped(weight, "fsdp", 2)]
    weights += [swapped(x, "fsdp", 1) for x in weights]
    finished = plane_exchange(depth_sum(depth_parts))
    input_grad = project_back(core, odd, pair, row_grads, weights, features)
    finished, input_grad = lax.optimization_barrier((finished, input_grad))
    weight_grad = join(odd, finished, value_weight.shape[0])
    return (input_grad, weight_grad)


def solution(mesh):
    rows = P(("dp", "fsdp"), None)
    flat = P(("dp", "fsdp"))
    return jax.shard_map(
        local,
        mesh=mesh,
        in_specs=(rows, P("fsdp", None), rows, rows, rows, flat, flat),
        out_specs=(rows, P("fsdp", None)),
        check_vma=False,
    )
```

time: 201 us -> 211 us (1.050)
  the two profiles are of different devices: /device:TPU:2 before, /device:TPU:32 now
where the time goes in v2:
time: 211 us; the launch traced here: 210 us
  waiting for transfers between devices  96.3 us (46%)
  starting transfers between devices  87.1 us (41%)
  Pallas kernels  16.3 us (8%)
  local copies, waits for them, and re-layouts  6.64 us (3%)
  other arithmetic  3.14 us (1%)
    ppermute x9, waiting for transfers between devices, swapped(): return lax.ppermute(block, axis, route)  43.4 us
    all_to_all x2, waiting for transfers between devices, plane_exchange(): return lax.all_to_all(pieces, 'dp', 0, 0, axis_index_groups=groups)  34.6 us
    all_to_all x1, starting transfers between devices, halves_exchange(): return lax.all_to_all(copies, 'dp', 0, 0, axis_index_groups=groups)  27.6 us
    all_to_all x1, starting transfers between devices, depth_exchange(): return lax.all_to_all(pieces, BOTH, 0, 0, axis_index_groups=groups)  24.4 us
    ppermute x9, starting transfers between devices, swapped(): return lax.ppermute(block, axis, route)  23 us
    all_to_all x1, waiting for transfers between devices, depth_exchange(): return lax.all_to_all(pieces, BOTH, 0, 0, axis_index_groups=groups)  18.3 us
    all_to_all x2, starting transfers between devices, plane_exchange(): return lax.all_to_all(pieces, 'dp', 0, 0, axis_index_groups=groups)  12.2 us
    unnamed x22, local copies, waits for them, and re-layouts  5.53 us
  transfers between devices with their start and end apart: 13, of which 8 were waited for; matrix products, arithmetic and copies ran while one was open for 1% of the time, Pallas kernels for 5%

profile of v2, /device:TPU:32, one launch (start us, length us, event | category | flops | bytes accessed | tf_op | source)
XLA Modules:
  0.0 210.4 jit_solution(7357935932295822837)
XLA Ops:
  0.6 1.2 copy-done
  1.8 1.2 copy-done.1
  3.0 0.9 copy-done.2
  4.0 2.0 messages.1
  6.0 27.6 %all-to-all-start = ((bf16[2,16,4608]{2,1,0:T(8,128)(2,1)}), bf16[2,16,4608]{2,1,0:T(8,128)(2,1)S(1)}, u32[]{:S(2)}, u32[]{:S(2)}) async-start(bf16[2,16,4608]{2,1,0:T(8,128)(2,1)} %get-tuple-element.13), calls=%async_computation | async-start | bytes 589824 | tf_op jit(solution)/shard_map/all_to_all | solution.py:337
  33.6 3.4 %collective-permute-start = (bf16[1,24,128]{2,1,0:T(8,128)(2,1)S(1)}, bf16[1,24,128]{2,1,0:T(8,128)(2,1)S(1)}, u32[]{:S(2)}, u32[]{:S(2)}) collective-permute-start(bf16[1,24,128]{2,1,0:T(8,128)(2,1)S(1)} %constant_dynamic-slice_fusion), channel_id=1, source_target_pairs={{0,4},{1,5},{2,6},{3,7},{4,0},{5,1},{6,2},{7,3},{8,12},{9,13},{10,... | collective-permute-start | bytes 18440 | tf_op jit(solution)/shard_map/ppermute | solution.py:34
  37.0 22.4 %collective-permute-done = bf16[1,24,128]{2,1,0:T(8,128)(2,1)S(1)} collective-permute-done((bf16[1,24,128]{2,1,0:T(8,128)(2,1)S(1)}, bf16[1,24,128]{2,1,0:T(8,128)(2,1)S(1)}, u32[]{:S(2)}, u32[]{:S(2)}) %collective-permute-start) | collective-permute-done | bytes 6176 | tf_op jit(solution)/shard_map/ppermute | solution.py:34
  59.4 1.9 collective-permute-start.1
  61.3 4.9 %collective-permute-start.3 = (bf16[16,4608]{1,0:T(8,128)(2,1)S(1)}, bf16[16,4608]{1,0:T(8,128)(2,1)S(1)}, u32[]{:S(2)}, u32[]{:S(2)}) collective-permute-start(bf16[16,4608]{1,0:T(8,128)(2,1)S(1)} %get-tuple-element.14), channel_id=1, source_target_pairs={{0,256},{32,288},{64,320},{96,352},{128,384},{160,416},{192,448},{... | collective-permute-start | bytes 442376 | tf_op jit(solution)/shard_map/ppermute | solution.py:34
  66.3 2.6 %collective-permute-done.1 = bf16[2,24,128]{2,1,0:T(8,128)(2,1)S(1)} collective-permute-done((bf16[2,24,128]{2,1,0:T(8,128)(2,1)S(1)}, bf16[2,24,128]{2,1,0:T(8,128)(2,1)S(1)}, u32[]{:S(2)}, u32[]{:S(2)}) %collective-permute-start.1) | collective-permute-done | bytes 12320 | tf_op jit(solution)/shard_map/ppermute | solution.py:34
  68.9 1.9 collective-permute-start.2
  71.7 11.6 %collective-permute-done.2 = bf16[4,24,128]{2,1,0:T(8,128)(2,1)S(1)} collective-permute-done((bf16[4,24,128]{2,1,0:T(8,128)(2,1)S(1)}, bf16[4,24,128]{2,1,0:T(8,128)(2,1)S(1)}, u32[]{:S(2)}, u32[]{:S(2)}) %collective-permute-start.2) | collective-permute-done | bytes 24608 | tf_op jit(solution)/shard_map/ppermute | solution.py:34
  84.0 4.2 %attend.1.main_ref = bf16[128,512]{1,0:T(8,128)(2,1)} custom-call(s32[128,1]{1,0:T(8,128)} %copy.10.col_ref, s32[1,128]{1,0:T(1,128)} %bitcast.20, bf16[192,2560]{1,0:T(8,128)(2,1)} %q_ref.3, bf16[192,512]{1,0:T(8,128)(2,1)} %k_ref.3, bf16[192,2560]{1,0:T(8,128)(2,1)} %c_ref.3, bf16[192,128]{1,0:T(8,128)(2,1)} %bitcast.16), custom_call_target="tpu_custom_call" | custom-call | tf_op jit(solution)/shard_map/attend/pallas_call | solution.py:133
  88.2 0.9 copy-done.4
  89.1 2.4 %gradient_pieces.1 = (bf16[128,512]{1,0:T(8,128)(2,1)S(1)}, bf16[16,8,40,128]{3,2,1,0:T(8,128)(2,1)S(1)}, bf16[16,8,40,128]{3,2,1,0:T(8,128)(2,1)S(1)}) custom-call(s32[1]{0:T(128)} %bitcast.1.core_ref, s32[1]{0:T(128)} %bitcast.2.half_ref, s32[128,1]{1,0:T(8,128)S(1)} %copy.11.slot_ref, bf16[128,512]{1,0:T(8,128)(2,1)S(1)} %copy-done.4, ...), custom_call_target="tpu_custom_call" | custom-call | tf_op jit(solution)/shard_map/gradient_pieces/pallas_call | solution.py:192
  91.5 2.1 collective-permute-start.4
  93.6 3.0 %collective-permute-done.4 = bf16[16,8,40,128]{3,2,1,0:T(8,128)(2,1)S(1)} collective-permute-done((bf16[16,8,40,128]{3,2,1,0:T(8,128)(2,1)S(1)}, bf16[16,8,40,128]{3,2,1,0:T(8,128)(2,1)S(1)}, u32[]{:S(2)}, u32[]{:S(2)}) %collective-permute-start.4) | collective-permute-done | bytes 1310752 | tf_op jit(solution)/shard_map/ppermute | solution.py:34
  97.1 1.5 pad_maximum_fusion
  98.6 7.0 %all-to-all-start.1 = ((bf16[16,512,128]{2,1,0:T(8,128)(2,1)}), bf16[16,512,128]{2,1,0:T(8,128)(2,1)S(1)}, u32[]{:S(2)}, u32[]{:S(2)}) async-start(bf16[16,512,128]{2,1,0:T(8,128)(2,1)} %pad_maximum_fusion), calls=%async_computation.1 | async-start | bytes 4194304 | tf_op jit(solution)/shard_map/all_to_all | solution.py:325
  105.7 31.1 %all-to-all-done.1.parts_ref = bf16[16,512,128]{2,1,0:T(8,128)(2,1)S(1)} async-done(((bf16[16,512,128]{2,1,0:T(8,128)(2,1)}), bf16[16,512,128]{2,1,0:T(8,128)(2,1)S(1)}, u32[]{:S(2)}, u32[]{:S(2)}) %all-to-all-start.1) | async-done | bytes 2097184 | tf_op jit(solution)/shard_map/all_to_all | solution.py:325
  137.1 2.2 %collective-permute-start.5 = (bf16[8,24,128]{2,1,0:T(8,128)(2,1)S(1)}, bf16[8,24,128]{2,1,0:T(8,128)(2,1)S(1)}, u32[]{:S(2)}, u32[]{:S(2)}) collective-permute-start(bf16[8,24,128]{2,1,0:T(8,128)(2,1)S(1)} %get-tuple-element.18), channel_id=1, source_target_pairs={{0,2},{1,3},{2,0},{3,1},{4,6},{5,7},{6,4},{7,5},{8,10},{9,11},{10,... | collective-permute-start | bytes 147464 | tf_op jit(solution)/shard_map/ppermute | solution.py:34
  139.3 3.8 %collective-permute-done.5 = bf16[8,24,128]{2,1,0:T(8,128)(2,1)S(1)} collective-permute-done((bf16[8,24,128]{2,1,0:T(8,128)(2,1)S(1)}, bf16[8,24,128]{2,1,0:T(8,128)(2,1)S(1)}, u32[]{:S(2)}, u32[]{:S(2)}) %collective-permute-start.5) | collective-permute-done | bytes 49184 | tf_op jit(solution)/shard_map/ppermute | solution.py:34
  143.1 2.2 %collective-permute-start.6 = (bf16[16,8,24,128]{3,2,1,0:T(8,128)(2,1)S(1)}, bf16[16,8,24,128]{3,2,1,0:T(8,128)(2,1)S(1)}, u32[]{:S(2)}, u32[]{:S(2)}) collective-permute-start(bf16[16,8,24,128]{3,2,1,0:T(8,128)(2,1)S(1)} %bitcast.12), channel_id=1, source_target_pairs={{0,2},{1,3},{2,0},{3,1},{4,6},{5,7},{6,4},{7,5},{8,10},{9,11},{10,... | collective-permute-start | bytes 2359304 | tf_op jit(solution)/shard_map/ppermute | solution.py:34
  146.0 24.4 %all-to-all-start.2 = ((bf16[16,24,128]{2,1,0:T(8,128)(2,1)}), bf16[16,24,128]{2,1,0:T(8,128)(2,1)S(1)}, u32[]{:S(2)}, u32[]{:S(2)}) async-start(bf16[16,24,128]{2,1,0:T(8,128)(2,1)} %pad_maximum_fusion.1), calls=%async_computation.2 | async-start | bytes 196608 | tf_op jit(solution)/shard_map/all_to_all | solution.py:348
  170.4 1.9 collective-permute-start.7
  172.4 2.4 %collective-permute-start.8 = (bf16[16,8,24,128]{3,2,1,0:T(8,128)(2,1)S(1)}, bf16[16,8,24,128]{3,2,1,0:T(8,128)(2,1)}, u32[]{:S(2)}, u32[]{:S(2)}) collective-permute-start(bf16[16,8,24,128]{3,2,1,0:T(8,128)(2,1)S(1)} %collective-permute-done.6.refs_1_), channel_id=1, source_target_pairs={{0,1},{1,0},{2,3},{3,2},{4,5},{5,4},{6,7},{7,6},{8,9},{9,8},{10,11... | collective-permute-start | bytes 2359304 | tf_op jit(solution)/shard_map/ppermute | solution.py:34
  174.8 18.3 %all-to-all-done.2.parts_ref = bf16[16,24,128]{2,1,0:T(8,128)(2,1)S(1)} async-done(((bf16[16,24,128]{2,1,0:T(8,128)(2,1)}), bf16[16,24,128]{2,1,0:T(8,128)(2,1)S(1)}, u32[]{:S(2)}, u32[]{:S(2)}) %all-to-all-start.2) | async-done | bytes 98336 | tf_op jit(solution)/shard_map/all_to_all | solution.py:348
  193.7 1.5 depth_sum.1
  195.3 5.2 %all-to-all-start.3 = ((bf16[16,24,128]{2,1,0:T(8,128)(2,1)}), bf16[16,24,128]{2,1,0:T(8,128)(2,1)S(1)}, u32[]{:S(2)}, u32[]{:S(2)}) async-start(bf16[16,24,128]{2,1,0:T(8,128)(2,1)} %depth_sum.1), calls=%async_computation.3 | async-start | bytes 196608 | tf_op jit(solution)/shard_map/all_to_all | solution.py:325
  200.5 4.3 %project_back.1 = bf16[128,2560]{1,0:T(8,128)(2,1)} custom-call(s32[1]{0:T(128)} %bitcast.1.core_ref, s32[1]{0:T(128)} %bitcast.odd_ref, s32[1]{0:T(128)} %bitcast.10.pair_ref, bf16[128,512]{1,0:T(8,128)(2,1)S(1)} %get-tuple-element.20.rows_ref, bf16[16,8,24,128]{3,2,1,0:T(8,128)(2,1)S(1)} %bitcast.14, ...), custom_call_target="tpu_custom_call" | custom-call | tf_op jit(solution)/shard_map/project_back/pallas_call | solution.py:308
  204.8 3.4 %all-to-all-done.3.pieces_ref = bf16[16,24,128]{2,1,0:T(8,128)(2,1)S(1)} async-done(((bf16[16,24,128]{2,1,0:T(8,128)(2,1)}), bf16[16,24,128]{2,1,0:T(8,128)(2,1)S(1)}, u32[]{:S(2)}, u32[]{:S(2)}) %all-to-all-start.3) | async-done | bytes 98336 | tf_op jit(solution)/shard_map/all_to_all | solution.py:325
  208.8 1.5 join.1
  (38 shorter events, 4.3 us)
Async XLA Ops:
  0.6 1.2 copy-start
  1.8 1.2 copy-start.1
  3.0 0.9 copy-start.2
  4.0 29.6 %copy-start.8 = (bf16[80,512]{1,0:T(8,128)(2,1)S(1)}, bf16[80,512]{1,0:T(8,128)(2,1)}, u32[]{:S(2)}) copy-start(bf16[80,512]{1,0:T(8,128)(2,1)} %param.8) | copy-start | bytes 245764
  4.0 66.9 %copy-start.9 = (s32[128]{0:T(128)S(1)}, s32[128]{0:T(128)}, u32[]{:S(2)}) copy-start(s32[128]{0:T(128)} %param.12) | copy-start | bytes 1540
  4.0 67.6 %copy-start.10 = (s32[128]{0:T(128)S(1)}, s32[128]{0:T(128)}, u32[]{:S(2)}) copy-start(s32[128]{0:T(128)} %param.13) | copy-start | bytes 1540
  6.0 82.2 %copy-start.3 = (bf16[128,2560]{1,0:T(8,128)(2,1)S(1)}, bf16[128,2560]{1,0:T(8,128)(2,1)}, u32[]{:S(2)}) copy-start(bf16[128,2560]{1,0:T(8,128)(2,1)} %act_ref.1) | copy-start | bytes 1966084
  6.0 82.2 %all-to-all-start = ((bf16[2,16,4608]{2,1,0:T(8,128)(2,1)}), bf16[2,16,4608]{2,1,0:T(8,128)(2,1)S(1)}, u32[]{:S(2)}, u32[]{:S(2)}) async-start(bf16[2,16,4608]{2,1,0:T(8,128)(2,1)} %get-tuple-element.13), calls=%async_computation | async-start | bytes 589824 | tf_op jit(solution)/shard_map/all_to_all | solution.py:337
  33.6 25.8 %collective-permute-start = (bf16[1,24,128]{2,1,0:T(8,128)(2,1)S(1)}, bf16[1,24,128]{2,1,0:T(8,128)(2,1)S(1)}, u32[]{:S(2)}, u32[]{:S(2)}) collective-permute-start(bf16[1,24,128]{2,1,0:T(8,128)(2,1)S(1)} %constant_dynamic-slice_fusion), channel_id=1, source_target_pairs={{0,4},{1,5},{2,6},{3,7},{4,0},{5,1},{6,2},{7,3},{8,12},{9,13},{10,... | collective-permute-start | bytes 18440 | tf_op jit(solution)/shard_map/ppermute | solution.py:34
  59.4 9.5 %collective-permute-start.1 = (bf16[2,24,128]{2,1,0:T(8,128)(2,1)S(1)}, bf16[2,24,128]{2,1,0:T(8,128)(2,1)S(1)}, u32[]{:S(2)}, u32[]{:S(2)}) collective-permute-start(bf16[2,24,128]{2,1,0:T(8,128)(2,1)S(1)} %pad_maximum_fusion.4), channel_id=1, source_target_pairs={{0,8},{1,9},{2,10},{3,11},{4,12},{5,13},{6,14},{7,15},{8,0},{9,1},... | collective-permute-start | bytes 36872 | tf_op jit(solution)/shard_map/ppermute | solution.py:34
  61.3 26.8 %collective-permute-start.3 = (bf16[16,4608]{1,0:T(8,128)(2,1)S(1)}, bf16[16,4608]{1,0:T(8,128)(2,1)S(1)}, u32[]{:S(2)}, u32[]{:S(2)}) collective-permute-start(bf16[16,4608]{1,0:T(8,128)(2,1)S(1)} %get-tuple-element.14), channel_id=1, source_target_pairs={{0,256},{32,288},{64,320},{96,352},{128,384},{160,416},{192,448},{... | collective-permute-start | bytes 442376 | tf_op jit(solution)/shard_map/ppermute | solution.py:34
  68.9 14.4 %collective-permute-start.2 = (bf16[4,24,128]{2,1,0:T(8,128)(2,1)S(1)}, bf16[4,24,128]{2,1,0:T(8,128)(2,1)S(1)}, u32[]{:S(2)}, u32[]{:S(2)}) collective-permute-start(bf16[4,24,128]{2,1,0:T(8,128)(2,1)S(1)} %pad_maximum_fusion.3), channel_id=1, source_target_pairs={{0,16},{1,17},{2,18},{3,19},{4,20},{5,21},{6,22},{7,23},{8,24},{9,... | collective-permute-start | bytes 73736 | tf_op jit(solution)/shard_map/ppermute | solution.py:34
  88.2 0.9 copy-start.4
  91.5 5.4 %copy-start.5 = (bf16[8,24,128]{2,1,0:T(8,128)(2,1)S(1)}, bf16[8,24,128]{2,1,0:T(8,128)(2,1)}, u32[]{:S(2)}) copy-start(bf16[8,24,128]{2,1,0:T(8,128)(2,1)} %pad_maximum_fusion.2) | copy-start | bytes 147460
  91.5 5.1 %collective-permute-start.4 = (bf16[16,8,40,128]{3,2,1,0:T(8,128)(2,1)S(1)}, bf16[16,8,40,128]{3,2,1,0:T(8,128)(2,1)S(1)}, u32[]{:S(2)}, u32[]{:S(2)}) collective-permute-start(bf16[16,8,40,128]{3,2,1,0:T(8,128)(2,1)S(1)} %get-tuple-element.16), channel_id=1, source_target_pairs={{0,1},{1,0},{2,3},{3,2},{4,5},{5,4},{6,7},{7,6},{8,9},{9,8},{10,11... | collective-permute-start | bytes 3932168 | tf_op jit(solution)/shard_map/ppermute | solution.py:34
  98.6 38.2 %all-to-all-start.1 = ((bf16[16,512,128]{2,1,0:T(8,128)(2,1)}), bf16[16,512,128]{2,1,0:T(8,128)(2,1)S(1)}, u32[]{:S(2)}, u32[]{:S(2)}) async-start(bf16[16,512,128]{2,1,0:T(8,128)(2,1)} %pad_maximum_fusion), calls=%async_computation.1 | async-start | bytes 4194304 | tf_op jit(solution)/shard_map/all_to_all | solution.py:325
  137.1 6.0 %collective-permute-start.5 = (bf16[8,24,128]{2,1,0:T(8,128)(2,1)S(1)}, bf16[8,24,128]{2,1,0:T(8,128)(2,1)S(1)}, u32[]{:S(2)}, u32[]{:S(2)}) collective-permute-start(bf16[8,24,128]{2,1,0:T(8,128)(2,1)S(1)} %get-tuple-element.18), channel_id=1, source_target_pairs={{0,2},{1,3},{2,0},{3,1},{4,6},{5,7},{6,4},{7,5},{8,10},{9,11},{10,... | collective-permute-start | bytes 147464 | tf_op jit(solution)/shard_map/ppermute | solution.py:34
  143.1 29.2 %collective-permute-start.6 = (bf16[16,8,24,128]{3,2,1,0:T(8,128)(2,1)S(1)}, bf16[16,8,24,128]{3,2,1,0:T(8,128)(2,1)S(1)}, u32[]{:S(2)}, u32[]{:S(2)}) collective-permute-start(bf16[16,8,24,128]{3,2,1,0:T(8,128)(2,1)S(1)} %bitcast.12), channel_id=1, source_target_pairs={{0,2},{1,3},{2,0},{3,1},{4,6},{5,7},{6,4},{7,5},{8,10},{9,11},{10,... | collective-permute-start | bytes 2359304 | tf_op jit(solution)/shard_map/ppermute | solution.py:34
  146.0 47.1 %all-to-all-start.2 = ((bf16[16,24,128]{2,1,0:T(8,128)(2,1)}), bf16[16,24,128]{2,1,0:T(8,128)(2,1)S(1)}, u32[]{:S(2)}, u32[]{:S(2)}) async-start(bf16[16,24,128]{2,1,0:T(8,128)(2,1)} %pad_maximum_fusion.1), calls=%async_computation.2 | async-start | bytes 196608 | tf_op jit(solution)/shard_map/all_to_all | solution.py:348
  170.4 30.0 %collective-permute-start.7 = (bf16[16,8,24,128]{3,2,1,0:T(8,128)(2,1)S(1)}, bf16[16,8,24,128]{3,2,1,0:T(8,128)(2,1)S(1)}, u32[]{:S(2)}, u32[]{:S(2)}) collective-permute-start(bf16[16,8,24,128]{3,2,1,0:T(8,128)(2,1)S(1)} %bitcast.13), channel_id=1, source_target_pairs={{0,1},{1,0},{2,3},{3,2},{4,5},{5,4},{6,7},{7,6},{8,9},{9,8},{10,11... | collective-permute-start | bytes 2359304 | tf_op jit(solution)/shard_map/ppermute | solution.py:34
  172.4 28.1 %collective-permute-start.8 = (bf16[16,8,24,128]{3,2,1,0:T(8,128)(2,1)S(1)}, bf16[16,8,24,128]{3,2,1,0:T(8,128)(2,1)}, u32[]{:S(2)}, u32[]{:S(2)}) collective-permute-start(bf16[16,8,24,128]{3,2,1,0:T(8,128)(2,1)S(1)} %collective-permute-done.6.refs_1_), channel_id=1, source_target_pairs={{0,1},{1,0},{2,3},{3,2},{4,5},{5,4},{6,7},{7,6},{8,9},{9,8},{10,11... | collective-permute-start | bytes 2359304 | tf_op jit(solution)/shard_map/ppermute | solution.py:34
  193.1 0.6 copy-start.6
  195.3 12.9 %all-to-all-start.3 = ((bf16[16,24,128]{2,1,0:T(8,128)(2,1)}), bf16[16,24,128]{2,1,0:T(8,128)(2,1)S(1)}, u32[]{:S(2)}, u32[]{:S(2)}) async-start(bf16[16,24,128]{2,1,0:T(8,128)(2,1)} %depth_sum.1), calls=%async_computation.3 | async-start | bytes 196608 | tf_op jit(solution)/shard_map/all_to_all | solution.py:325
  208.2 0.6 copy-start.7

commit v3 on v2

--- a/solution.py
+++ b/solution.py
@@ -47,9 +47,6 @@
 def message_kernel(block, q_ref, k_ref, c_ref, *out_refs):
     for section, out_ref in enumerate(out_refs):
         low = section * block
-        copies_ref = None
-        if section == 0:
-            copies_ref, out_ref = out_ref, out_ref.at[0]
         out_ref[:, :FEATURES] = c_ref[low + LEAST : low + block, :]
         pad = jnp.zeros((HD - GROUP * LEAST, HD), BF16)
         for h in range(KVH):
@@ -74,8 +71,6 @@
             at = SUMS + h * HD
             out_ref[:, at : at + HD] = coarse
             out_ref[:, at + WIDTH : at + WIDTH + HD] = (sums - coarse.astype(F32)).astype(BF16)
-        if copies_ref is not None:
-            copies_ref[1] = copies_ref[0]
 
 
 def messages(queries, key_rows, context_grad, tok, block):
@@ -87,9 +82,9 @@
         functools.partial(message_kernel, block),
         grid=(1,),
         in_specs=specs,
-        out_specs=[pl.BlockSpec((2, *shape), lambda i: (0, 0, 0)), pl.BlockSpec(shape, lambda i: (0, 0))],
-        out_shape=[jax.ShapeDtypeStruct((2, *shape), BF16), jax.ShapeDtypeStruct(shape, BF16)],
-        compiler_params=pltpu.CompilerParams(vmem_limit_bytes=24 * 2**20),
+        out_specs=[pl.BlockSpec(shape, lambda i: (0, 0))] * SECTIONS,
+        out_shape=[jax.ShapeDtypeStruct(shape, BF16)] * SECTIONS,
+        compiler_params=pltpu.CompilerParams(vmem_limit_bytes=56 * 2**20),
         name="messages",
     )(queries, key_rows, context_grad)
 
@@ -112,8 +107,7 @@
     return jnp.concatenate(heads, axis=1).astype(BF16)
 
 
-def attend_kernel(col_ref, row_ref, q_ref, k_ref, c_ref, behind_ref, out_ref):
-    del behind_ref
+def attend_kernel(col_ref, row_ref, q_ref, k_ref, c_ref, out_ref):
     tok = q_ref.shape[0]
     query = jnp.concatenate([q_ref[:, g * HD : (g + 1) * HD] for g in range(GROUP)], axis=0)
     context = jnp.concatenate([c_ref[:, g * HD : (g + 1) * HD] for g in range(GROUP)], axis=0)
@@ -126,7 +120,7 @@
     out_ref[...] = jnp.dot(probs, context, preferred_element_type=F32).astype(BF16)
 
 
-def attend(queries, key_rows, context_grad, segment, behind):
+def attend(queries, key_rows, context_grad, segment):
     tok = segment.shape[0]
     wide = pl.BlockSpec((tok, GROUP * HD), lambda h: (0, h))
     thin = pl.BlockSpec((tok, HD), lambda h: (0, h))
@@ -139,22 +133,21 @@
             wide,
             thin,
             wide,
-            pl.BlockSpec(memory_space=pl.ANY),
         ],
         out_specs=thin,
         out_shape=jax.ShapeDtypeStruct((tok, WIDTH), BF16),
         name="attend",
-    )(segment.reshape(tok, 1), segment.reshape(1, tok), queries, key_rows, context_grad, behind)
-
-
-def gradient_kernel(block, core_ref, half_ref, slot_ref, main_ref, first_ref, second_ref, act_ref, rows_ref, keep_ref, send_ref, whole):
+    )(segment.reshape(tok, 1), segment.reshape(1, tok), queries, key_rows, context_grad)
+
+
+def gradient_kernel(block, core_ref, slot_ref, main_ref, first_ref, second_ref, act_ref, behind_ref, rows_ref, keep_ref, send_ref, whole):
+    del behind_ref
     tok = slot_ref.shape[0]
 
     @pl.when(pl.program_id(0) == 0)
     def _():
         slot = slot_ref[...]
-        refs = (first_ref.at[1 - half_ref[0]], second_ref)
-        parts = [sent_block(slot, ref, tok + s * block, block) for s, ref in enumerate(refs)]
+        parts = [sent_block(slot, ref, tok + s * block, block) for s, ref in enumerate((first_ref, second_ref))]
         held = jnp.concatenate([main_ref[...], *parts], axis=0)
         chosen = (slot == iota((tok, held.shape[0]), 1)).astype(F32).astype(BF16)
         rows_ref[...] = jnp.dot(chosen, held, preferred_element_type=F32).astype(BF16)
@@ -182,23 +175,25 @@
                     target[cut * CUTS + k, pair] = piece[:, k * HD : (k + 1) * HD]
 
 
-def gradient_pieces(core, half, send_slot, main, first, second, activations, block):
+def gradient_pieces(core, send_slot, main, first, second, activations, behind, block):
     tok, features = activations.shape
     steps = 4
     held = pl.BlockSpec((tok, WIDTH), lambda m, *_: (0, 0))
-    message = [pl.BlockSpec(x.shape, lambda m, *_, rank=x.ndim: (0,) * rank) for x in (first, second)]
+    message = pl.BlockSpec(first.shape, lambda m, *_: (0, 0))
     pieces = pl.BlockSpec((CUTS * CUTS, DEPTH // 2 // steps, 40, HD), lambda m, *_: (0, m, 0, 0))
     shape = jax.ShapeDtypeStruct((CUTS * CUTS, DEPTH // 2, 40, HD), BF16)
     return pl.pallas_call(
         functools.partial(gradient_kernel, block),
         grid_spec=pltpu.PrefetchScalarGridSpec(
-            num_scalar_prefetch=2,
+            num_scalar_prefetch=1,
             grid=(steps,),
             in_specs=[
                 pl.BlockSpec((tok, 1), lambda m, *_: (0, 0)),
                 held,
-                *message,
+                message,
+                message,
                 pl.BlockSpec((tok, features // steps), lambda m, *_: (0, m)),
+                pl.BlockSpec(memory_space=pl.ANY),
             ],
             out_specs=[held, pieces, pieces],
             scratch_shapes=[pltpu.VMEM((features // steps, WIDTH), F32)],
@@ -206,7 +201,7 @@
         out_shape=[jax.ShapeDtypeStruct((tok, WIDTH), BF16), shape, shape],
         compiler_params=pltpu.CompilerParams(vmem_limit_bytes=24 * 2**20),
         name="gradient_pieces",
-    )(core, half, send_slot.reshape(tok, 1), main, first, second, activations)
+    )(core, send_slot.reshape(tok, 1), main, first, second, activations, behind)
 
 
 def plane_sum_kernel(odd_ref, parts_ref, keep_ref, send_ref, whole):
@@ -282,42 +277,39 @@
     )(odd, pieces)
 
 
-def project_kernel(core_ref, odd_ref, pair_ref, rows_ref, *refs):
-    *source_refs, out_ref, whole = refs
-    core, odd, swap = core_ref[0], odd_ref[0], pair_ref[0] % 2
-    pairs = source_refs[0].shape[1]
-    shard = whole.shape[0] // (4 * pairs)
-    places = [(a, b) for b in (core, 1 - core) for a in (odd, 1 - odd)]
-    for source, (z_parity, core_parity) in zip(source_refs, places, strict=True):
-        for pair in range(pairs):
+def project_kernel(core_ref, rows_ref, own_ref, other_ref, out_ref, whole):
+    core = core_ref[0]
+    shard = whole.shape[0] // (2 * own_ref.shape[1])
+    for source, parity in ((own_ref, core), (other_ref, 1 - core)):
+        for z in range(own_ref.shape[1]):
             for cut in range(CUTS):
                 size = min(ROWS, shard - cut * ROWS)
-                at = (4 * pair + 2 * z_parity + core_parity) * shard + cut * ROWS
+                start = pl.multiple_of(z * 2 * shard + parity * shard + cut * ROWS, 8)
                 for k in range(CUTS):
-                    part = source[cut * CUTS + k, pair ^ swap].astype(F32)
-                    whole[pl.ds(pl.multiple_of(at, 8), size), k * HD : (k + 1) * HD] = part[:size]
+                    part = source[cut * CUTS + k, z].astype(F32)
+                    whole[pl.ds(start, size), k * HD : (k + 1) * HD] = part[:size]
     out_ref[...] = lax.dot_general(
         rows_ref[...], whole[...].astype(BF16), ON_COLUMNS, preferred_element_type=F32
     ).astype(BF16)
 
 
-def project_back(core, odd, pair, row_grads, sources, features):
+def project_back(core, row_grads, own, other, features):
     tok, width = row_grads.shape
     steps = 4
-    pieces = pl.BlockSpec((CUTS * CUTS, DEPTH // 2 // steps, ROWS, HD), lambda m, c, o, p: (0, m ^ (p[0] // 2), 0, 0))
+    pieces = pl.BlockSpec((CUTS * CUTS, DEPTH // steps, ROWS, HD), lambda m, *_: (0, m, 0, 0))
     return pl.pallas_call(
         project_kernel,
         grid_spec=pltpu.PrefetchScalarGridSpec(
-            num_scalar_prefetch=3,
+            num_scalar_prefetch=1,
             grid=(steps,),
-            in_specs=[pl.BlockSpec((tok, width), lambda m, *_: (0, 0))] + [pieces] * len(sources),
+            in_specs=[pl.BlockSpec((tok, width), lambda m, *_: (0, 0)), pieces, pieces],
             out_specs=pl.BlockSpec((tok, features // steps), lambda m, *_: (0, m)),
             scratch_shapes=[pltpu.VMEM((features // steps, width), F32)],
         ),
         out_shape=jax.ShapeDtypeStruct((tok, features), BF16),
         compiler_params=pltpu.CompilerParams(vmem_limit_bytes=24 * 2**20),
         name="project_back",
-    )(core, odd, pair, row_grads, *sources)
+    )(core, row_grads, own, other)
 
 
 def plane_exchange(pieces):
@@ -326,15 +318,15 @@
 
 
 def depth_gather(piece):
-    pieces = piece[None]
-    for bit in range(1, DEPTH.bit_length() - 1):
-        pieces = jnp.concatenate([pieces, swapped(pieces, "fsdp", 2 << bit)], axis=0)
-    return pieces.reshape(DEPTH // 2 * ROWS, HD)
-
-
-def halves_exchange(copies):
-    groups = [[at, at + PLANE] for at in range(PLANE)]
-    return lax.all_to_all(copies, "dp", 0, 0, axis_index_groups=groups)
+    groups = [[2 * z + core for z in range(DEPTH)] for core in range(2)]
+    copies = jnp.broadcast_to(piece[None], (DEPTH, *piece.shape))
+    return lax.all_to_all(copies, "fsdp", 0, 0, axis_index_groups=groups)
+
+
+def plane_gather(pieces):
+    rounds = 1 + lax.axis_index("dp") // lax.axis_size("dp")
+    copies = jnp.broadcast_to(pieces[None], (PLANE, *pieces.shape))
+    return lax.fori_loop(0, rounds, lambda _, held: plane_exchange(held), copies)
 
 
 def depth_exchange(pieces):
@@ -362,41 +354,30 @@
     block = (queries.shape[0] - tok) // SECTIONS
     half = lax.axis_size("dp") // 2
     place = lax.axis_index("dp") % PLANE
-    core, odd, pair, upper = (
-        x.astype(jnp.int32).reshape(1)
-        for x in (
-            lax.axis_index("fsdp") % 2,
-            lax.axis_index("fsdp") // 2 % 2,
-            lax.axis_index("fsdp") // 4,
-            lax.axis_index("dp") // half,
-        )
-    )
+    core = (lax.axis_index("fsdp") % 2).astype(jnp.int32).reshape(1)
+    odd = (lax.axis_index("fsdp") // 2 % 2).astype(jnp.int32).reshape(1)
 
     piece = lax.dynamic_index_in_dim(cut_up(value_weight), place, 0, keepdims=False)
     first, second = messages(queries, key_rows, context_grad, tok, block)
-    first = halves_exchange(first)
+    first = swapped(first, "dp", half)
     second = swapped(second, "dp", half // 2)
-    depth_weight = depth_gather(piece)
-    main = attend(queries, key_rows, context_grad, segment, depth_weight)
-
-    row_grads, keep, send = gradient_pieces(core, upper, send_slot, main, first, second, activations, block)
+    own_weight = plane_gather(depth_gather(piece))
+    main = attend(queries, key_rows, context_grad, segment)
+    main, own_weight = lax.optimization_barrier((main, own_weight))
+
+    row_grads, keep, send = gradient_pieces(core, send_slot, main, first, second, activations, own_weight, block)
     came = swapped(send, "fsdp", 1)
     _, pairs, rows, _ = keep.shape
-    gradient = added(keep, came).reshape(PLANE, pairs * rows, HD)
-    weight = jnp.broadcast_to(depth_weight[None], (PLANE, *depth_weight.shape))
-    parts = plane_exchange(jnp.concatenate([gradient, weight], axis=1))
+    parts = plane_exchange(added(keep, came).reshape(PLANE, pairs * rows, HD))
+    other_weight = swapped(own_weight, "fsdp", 1)
 
     keep, send = plane_sum(odd, parts, pairs, rows)
     came = swapped(send, "fsdp", 2)
-    depth_part, parts = lax.optimization_barrier((added(keep, came), parts))
+    depth_part = added(keep, came)
     depth_parts = depth_exchange(jnp.concatenate([depth_part, depth_part], axis=0))
-
-    weight = parts[:, pairs * rows :].reshape(CUTS * CUTS, DEPTH // 2, ROWS, HD)
-    weights = [weight, swapped(weight, "fsdp", 2)]
-    weights += [swapped(x, "fsdp", 1) for x in weights]
+    input_grad = project_back(core, row_grads, own_weight, other_weight, features)
+    depth_parts, input_grad = lax.optimization_barrier((depth_parts, input_grad))
     finished = plane_exchange(depth_sum(depth_parts))
-    input_grad = project_back(core, odd, pair, row_grads, weights, features)
-    finished, input_grad = lax.optimization_barrier((finished, input_grad))
     weight_grad = join(odd, finished, value_weight.shape[0])
     return (input_grad, weight_grad)
 

time: 211 us -> 183 us (0.87)
  the two profiles are of different devices: /device:TPU:32 before, /device:TPU:2 now
where the time goes in v3:
time: 183 us; the launch traced here: 182 us
  starting transfers between devices  80.2 us (44%)
  waiting for transfers between devices  63 us (34%)
  Pallas kernels  17.5 us (10%)
  blocking collectives  12.9 us (7%)
  local copies, waits for them, and re-layouts  5.75 us (3%)
  other arithmetic  2.07 us (1%)
    all_to_all x2, waiting for transfers between devices, plane_exchange(): return lax.all_to_all(pieces, 'dp', 0, 0, axis_index_groups=groups)  37.3 us
    all_to_all x1, starting transfers between devices, depth_gather(): return lax.all_to_all(copies, 'fsdp', 0, 0, axis_index_groups=groups)  25.9 us
    ppermute x5, starting transfers between devices, swapped(): return lax.ppermute(block, axis, route)  23.1 us
    all_to_all x1, waiting for transfers between devices, depth_exchange(): return lax.all_to_all(pieces, BOTH, 0, 0, axis_index_groups=groups)  20.2 us
    all_to_all x1, starting transfers between devices, depth_exchange(): return lax.all_to_all(pieces, BOTH, 0, 0, axis_index_groups=groups)  18.2 us
    all_to_all x2, starting transfers between devices, plane_exchange(): return lax.all_to_all(pieces, 'dp', 0, 0, axis_index_groups=groups)  12.9 us
    all_to_all x1, blocking collectives, plane_exchange(): return lax.all_to_all(pieces, 'dp', 0, 0, axis_index_groups=groups)  12.9 us
    ppermute x5, waiting for transfers between devices, swapped(): return lax.ppermute(block, axis, route)  5.56 us
  transfers between devices with their start and end apart: 9, of which 5 were waited for; matrix products, arithmetic and copies ran while one was open for 2% of the time, Pallas kernels for 7%

profile of v3, /device:TPU:2, one launch (start us, length us, event | category | flops | bytes accessed | tf_op | source)
XLA Modules:
  0.0 182.2 jit_solution(4082363671385703005)
XLA Ops:
  0.7 0.9 pad.4
  1.6 0.7 broadcast_in_dim.7
  2.3 25.9 %all-to-all-start.1 = ((bf16[16,24,128]{2,1,0:T(8,128)(2,1)}), bf16[16,24,128]{2,1,0:T(8,128)(2,1)S(1)}, u32[]{:S(2)}, u32[]{:S(2)}) async-start(bf16[16,24,128]{2,1,0:T(8,128)(2,1)} %broadcast_in_dim.7), calls=%async_computation.1 | async-start | bytes 196608 | tf_op jit(solution)/shard_map/all_to_all | solution.py:323
  28.2 3.2 %messages.1 = (bf16[16,4608]{1,0:T(8,128)(2,1)}, bf16[16,4608]{1,0:T(8,128)(2,1)}) custom-call(bf16[192,2560]{1,0:T(8,128)(2,1)} %q_ref.3, bf16[192,512]{1,0:T(8,128)(2,1)} %k_ref.3, bf16[192,2560]{1,0:T(8,128)(2,1)} %c_ref.3), custom_call_target="tpu_custom_call" | custom-call | tf_op jit(solution)/shard_map/messages/pallas_call | solution.py:81
  31.4 11.8 %collective-permute-start = (bf16[16,4608]{1,0:T(8,128)(2,1)}, bf16[16,4608]{1,0:T(8,128)(2,1)S(1)}, u32[]{:S(2)}, u32[]{:S(2)}) collective-permute-start(bf16[16,4608]{1,0:T(8,128)(2,1)} %get-tuple-element.33), channel_id=1, source_target_pairs={{0,512},{32,544},{64,576},{96,608},{128,640},{160,672},{192,704},{... | collective-permute-start | bytes 442376 | tf_op jit(solution)/shard_map/ppermute | solution.py:34
  43.3 4.0 %collective-permute-start.1 = (bf16[16,4608]{1,0:T(8,128)(2,1)}, bf16[16,4608]{1,0:T(8,128)(2,1)S(1)}, u32[]{:S(2)}, u32[]{:S(2)}) collective-permute-start(bf16[16,4608]{1,0:T(8,128)(2,1)} %get-tuple-element.34), channel_id=1, source_target_pairs={{0,256},{32,288},{64,320},{96,352},{128,384},{160,416},{192,448},{... | collective-permute-start | bytes 442376 | tf_op jit(solution)/shard_map/ppermute | solution.py:34
  47.4 0.1 copy.15.slot_ref
  47.5 0.7 copy.13.col_ref
  48.2 4.2 %attend.1.main_ref = bf16[128,512]{1,0:T(8,128)(2,1)} custom-call(s32[128,1]{1,0:T(8,128)} %copy.13.col_ref, s32[1,128]{1,0:T(1,128)} %bitcast.12, bf16[192,2560]{1,0:T(8,128)(2,1)} %q_ref.3, bf16[192,512]{1,0:T(8,128)(2,1)} %k_ref.3, bf16[192,2560]{1,0:T(8,128)(2,1)} %c_ref.3), custom_call_target="tpu_custom_call" | custom-call | tf_op jit(solution)/shard_map/attend/pallas_call | solution.py:127
  52.4 1.5 broadcast_in_dim.16
  53.9 28.0 %while.10 = (s32[]{:T(128)}, bf16[16,16,24,128]{3,2,1,0:T(8,128)(2,1)}, s32[]{:T(128)}, s32[]{:T(128)}) while((s32[]{:T(128)}, bf16[16,16,24,128]{3,2,1,0:T(8,128)(2,1)}, s32[]{:T(128)}, s32[]{:T(128)}) %tuple.26), condition=%wide.region_1.2_spmd, body=%wide.region_0.1_spmd.sunk | while | flops 2 | bytes 7864405 | solution.py:329
  53.9 6.6 %all-to-all-start = ((bf16[16,16,24,128]{3,2,1,0:T(8,128)(2,1)}), bf16[16,16,24,128]{3,2,1,0:T(8,128)(2,1)S(1)}, u32[]{:S(2)}, u32[]{:S(2)}) async-start(bf16[16,16,24,128]{3,2,1,0:T(8,128)(2,1)} %get-tuple-element.74), calls=%async_computation | async-start | bytes 3145728 | tf_op jit(solution)/shard_map/while/body/all_to_all | solution.py:317
  60.5 20.2 %all-to-all-done = bf16[16,16,24,128]{3,2,1,0:T(8,128)(2,1)S(1)} async-done(((bf16[16,16,24,128]{3,2,1,0:T(8,128)(2,1)}), bf16[16,16,24,128]{3,2,1,0:T(8,128)(2,1)S(1)}, u32[]{:S(2)}, u32[]{:S(2)}) %all-to-all-start) | async-done | bytes 1572896 | tf_op jit(solution)/shard_map/while/body/all_to_all | solution.py:317
  80.8 1.2 copy.21
  82.0 2.5 %gradient_pieces.1 = (bf16[128,512]{1,0:T(8,128)(2,1)S(1)}, bf16[16,8,40,128]{3,2,1,0:T(8,128)(2,1)S(1)}, bf16[16,8,40,128]{3,2,1,0:T(8,128)(2,1)S(1)}) custom-call(s32[1]{0:T(128)} %bitcast.1.core_ref, s32[128,1]{1,0:T(8,128)S(1)} %copy.15.slot_ref, bf16[128,512]{1,0:T(8,128)(2,1)S(1)} %copy-done.1, bf16[16,4608]{1,0:T(8,128)(2,1)S(1)} %collective-permute-done.first_ref, ...), custom_call_target="tpu_custom_call" | custom-call | tf_op jit(solution)/shard_map/gradient_pieces/pallas_call | solution.py:185
  84.4 1.9 %collective-permute-start.2 = (bf16[16,8,40,128]{3,2,1,0:T(8,128)(2,1)S(1)}, bf16[16,8,40,128]{3,2,1,0:T(8,128)(2,1)S(1)}, u32[]{:S(2)}, u32[]{:S(2)}) collective-permute-start(bf16[16,8,40,128]{3,2,1,0:T(8,128)(2,1)S(1)} %get-tuple-element.37), channel_id=1, source_target_pairs={{0,1},{1,0},{2,3},{3,2},{4,5},{5,4},{6,7},{7,6},{8,9},{9,8},{10,11... | collective-permute-start | bytes 3932168 | tf_op jit(solution)/shard_map/ppermute | solution.py:34
  86.4 3.0 %collective-permute-done.2 = bf16[16,8,40,128]{3,2,1,0:T(8,128)(2,1)S(1)} collective-permute-done((bf16[16,8,40,128]{3,2,1,0:T(8,128)(2,1)S(1)}, bf16[16,8,40,128]{3,2,1,0:T(8,128)(2,1)S(1)}, u32[]{:S(2)}, u32[]{:S(2)}) %collective-permute-start.2) | collective-permute-done | bytes 1310752 | tf_op jit(solution)/shard_map/ppermute | solution.py:34
  89.4 1.4 add_convert_fusion
  90.8 6.3 %all-to-all-start.2 = ((bf16[16,320,128]{2,1,0:T(8,128)(2,1)}), bf16[16,320,128]{2,1,0:T(8,128)(2,1)S(1)}, u32[]{:S(2)}, u32[]{:S(2)}) async-start(bf16[16,320,128]{2,1,0:T(8,128)(2,1)} %bitcast.8), calls=%async_computation.2 | async-start | bytes 2621440 | tf_op jit(solution)/shard_map/all_to_all | solution.py:317
  97.1 1.9 %collective-permute-start.4 = (bf16[16,16,24,128]{3,2,1,0:T(8,128)(2,1)}, bf16[16,16,24,128]{3,2,1,0:T(8,128)(2,1)S(1)}, u32[]{:S(2)}, u32[]{:S(2)}) collective-permute-start(bf16[16,16,24,128]{3,2,1,0:T(8,128)(2,1)} %get-tuple-element.35.behind_ref.own_ref), channel_id=1, source_target_pairs={{0,1},{1,0},{2,3},{3,2},{4,5},{5,4},{6,7},{7,6},{8,9},{9,8},{10,11... | collective-permute-start | bytes 4718600 | tf_op jit(solution)/shard_map/ppermute | solution.py:34
  99.0 17.1 %all-to-all-done.2.parts_ref = bf16[16,320,128]{2,1,0:T(8,128)(2,1)S(1)} async-done(((bf16[16,320,128]{2,1,0:T(8,128)(2,1)}), bf16[16,320,128]{2,1,0:T(8,128)(2,1)S(1)}, u32[]{:S(2)}, u32[]{:S(2)}) %all-to-all-start.2) | async-done | bytes 1310752 | tf_op jit(solution)/shard_map/all_to_all | solution.py:317
  116.1 0.2 plane_sum.1
  116.3 3.4 %collective-permute-start.3 = (bf16[8,24,128]{2,1,0:T(8,128)(2,1)S(1)}, bf16[8,24,128]{2,1,0:T(8,128)(2,1)S(1)}, u32[]{:S(2)}, u32[]{:S(2)}) collective-permute-start(bf16[8,24,128]{2,1,0:T(8,128)(2,1)S(1)} %get-tuple-element.39), channel_id=1, source_target_pairs={{0,2},{1,3},{2,0},{3,1},{4,6},{5,7},{6,4},{7,5},{8,10},{9,11},{10,... | collective-permute-start | bytes 147464 | tf_op jit(solution)/shard_map/ppermute | solution.py:34
  119.7 2.6 %collective-permute-done.3 = bf16[8,24,128]{2,1,0:T(8,128)(2,1)S(1)} collective-permute-done((bf16[8,24,128]{2,1,0:T(8,128)(2,1)S(1)}, bf16[8,24,128]{2,1,0:T(8,128)(2,1)S(1)}, u32[]{:S(2)}, u32[]{:S(2)}) %collective-permute-start.3) | collective-permute-done | bytes 49184 | tf_op jit(solution)/shard_map/ppermute | solution.py:34
  122.3 0.6 pad_maximum_fusion
  122.9 18.2 %all-to-all-start.3 = ((bf16[16,24,128]{2,1,0:T(8,128)(2,1)}), bf16[16,24,128]{2,1,0:T(8,128)(2,1)S(1)}, u32[]{:S(2)}, u32[]{:S(2)}) async-start(bf16[16,24,128]{2,1,0:T(8,128)(2,1)} %pad_maximum_fusion), calls=%async_computation.3 | async-start | bytes 196608 | tf_op jit(solution)/shard_map/all_to_all | solution.py:340
  141.2 4.3 %project_back.1 = bf16[128,2560]{1,0:T(8,128)(2,1)} custom-call(s32[1]{0:T(128)} %bitcast.1.core_ref, bf16[128,512]{1,0:T(8,128)(2,1)S(1)} %get-tuple-element.40.rows_ref, bf16[16,16,24,128]{3,2,1,0:T(8,128)(2,1)} %get-tuple-element.35.behind_ref.own_ref, bf16[16,16,24,128]{3,2,1,0:T(8,128)(2,1)S(1)} %collective-permute-done.4.other_ref), custom_call_target="tpu_custom_call" | custom-call | tf_op jit(solution)/shard_map/project_back/pallas_call | solution.py:300
  145.4 20.2 %all-to-all-done.3.parts_ref = bf16[16,24,128]{2,1,0:T(8,128)(2,1)S(1)} async-done(((bf16[16,24,128]{2,1,0:T(8,128)(2,1)}), bf16[16,24,128]{2,1,0:T(8,128)(2,1)S(1)}, u32[]{:S(2)}, u32[]{:S(2)}) %all-to-all-start.3) | async-done | bytes 98336 | tf_op jit(solution)/shard_map/all_to_all | solution.py:340
  165.6 0.6 copy-done.2
  166.2 1.6 depth_sum.1
  167.8 12.9 %all_to_all.26.pieces_ref = bf16[16,24,128]{2,1,0:T(8,128)(2,1)} all-to-all(bf16[16,24,128]{2,1,0:T(8,128)(2,1)} %depth_sum.1), channel_id=1, replica_groups={{0,32,64,96,128,160,192,224,256,288,320,352,384,416,448,480},{512,544,5..., dimensions={0} | all-to-all | bytes 196608 | tf_op jit(solution)/shard_map/all_to_all | solution.py:317
  180.7 1.5 join.1
  (17 shorter events, 0.1 us)
Async XLA Ops:
  0.6 46.7 %copy-start.4 = (s32[128]{0:T(128)S(1)}, s32[128]{0:T(128)}, u32[]{:S(2)}) copy-start(s32[128]{0:T(128)} %param.15) | copy-start | bytes 1540
  0.7 46.8 %copy-start.3 = (s32[128]{0:T(128)S(1)}, s32[128]{0:T(128)}, u32[]{:S(2)}) copy-start(s32[128]{0:T(128)} %param.14) | copy-start | bytes 1540
  2.3 50.1 %all-to-all-start.1 = ((bf16[16,24,128]{2,1,0:T(8,128)(2,1)}), bf16[16,24,128]{2,1,0:T(8,128)(2,1)S(1)}, u32[]{:S(2)}, u32[]{:S(2)}) async-start(bf16[16,24,128]{2,1,0:T(8,128)(2,1)} %broadcast_in_dim.7), calls=%async_computation.1 | async-start | bytes 196608 | tf_op jit(solution)/shard_map/all_to_all | solution.py:323
  31.4 50.5 %collective-permute-start = (bf16[16,4608]{1,0:T(8,128)(2,1)}, bf16[16,4608]{1,0:T(8,128)(2,1)S(1)}, u32[]{:S(2)}, u32[]{:S(2)}) collective-permute-start(bf16[16,4608]{1,0:T(8,128)(2,1)} %get-tuple-element.33), channel_id=1, source_target_pairs={{0,512},{32,544},{64,576},{96,608},{128,640},{160,672},{192,704},{... | collective-permute-start | bytes 442376 | tf_op jit(solution)/shard_map/ppermute | solution.py:34
  43.3 38.7 %collective-permute-start.1 = (bf16[16,4608]{1,0:T(8,128)(2,1)}, bf16[16,4608]{1,0:T(8,128)(2,1)S(1)}, u32[]{:S(2)}, u32[]{:S(2)}) collective-permute-start(bf16[16,4608]{1,0:T(8,128)(2,1)} %get-tuple-element.34), channel_id=1, source_target_pairs={{0,256},{32,288},{64,320},{96,352},{128,384},{160,416},{192,448},{... | collective-permute-start | bytes 442376 | tf_op jit(solution)/shard_map/ppermute | solution.py:34
  53.9 28.0 %copy-start = (bf16[128,2560]{1,0:T(8,128)(2,1)S(1)}, bf16[128,2560]{1,0:T(8,128)(2,1)}, u32[]{:S(2)}) copy-start(bf16[128,2560]{1,0:T(8,128)(2,1)} %act_ref.1) | copy-start | bytes 1966084
  53.9 28.1 %copy-start.1 = (bf16[128,512]{1,0:T(8,128)(2,1)S(1)}, bf16[128,512]{1,0:T(8,128)(2,1)}, u32[]{:S(2)}) copy-start(bf16[128,512]{1,0:T(8,128)(2,1)} %attend.1.main_ref) | copy-start | bytes 393220
  53.9 26.9 %all-to-all-start = ((bf16[16,16,24,128]{3,2,1,0:T(8,128)(2,1)}), bf16[16,16,24,128]{3,2,1,0:T(8,128)(2,1)S(1)}, u32[]{:S(2)}, u32[]{:S(2)}) async-start(bf16[16,16,24,128]{3,2,1,0:T(8,128)(2,1)} %get-tuple-element.74), calls=%async_computation | async-start | bytes 3145728 | tf_op jit(solution)/shard_map/while/body/all_to_all | solution.py:317
  84.4 4.9 %collective-permute-start.2 = (bf16[16,8,40,128]{3,2,1,0:T(8,128)(2,1)S(1)}, bf16[16,8,40,128]{3,2,1,0:T(8,128)(2,1)S(1)}, u32[]{:S(2)}, u32[]{:S(2)}) collective-permute-start(bf16[16,8,40,128]{3,2,1,0:T(8,128)(2,1)S(1)} %get-tuple-element.37), channel_id=1, source_target_pairs={{0,1},{1,0},{2,3},{3,2},{4,5},{5,4},{6,7},{7,6},{8,9},{9,8},{10,11... | collective-permute-start | bytes 3932168 | tf_op jit(solution)/shard_map/ppermute | solution.py:34
  90.8 25.3 %all-to-all-start.2 = ((bf16[16,320,128]{2,1,0:T(8,128)(2,1)}), bf16[16,320,128]{2,1,0:T(8,128)(2,1)S(1)}, u32[]{:S(2)}, u32[]{:S(2)}) async-start(bf16[16,320,128]{2,1,0:T(8,128)(2,1)} %bitcast.8), calls=%async_computation.2 | async-start | bytes 2621440 | tf_op jit(solution)/shard_map/all_to_all | solution.py:317
  97.1 44.1 %collective-permute-start.4 = (bf16[16,16,24,128]{3,2,1,0:T(8,128)(2,1)}, bf16[16,16,24,128]{3,2,1,0:T(8,128)(2,1)S(1)}, u32[]{:S(2)}, u32[]{:S(2)}) collective-permute-start(bf16[16,16,24,128]{3,2,1,0:T(8,128)(2,1)} %get-tuple-element.35.behind_ref.own_ref), channel_id=1, source_target_pairs={{0,1},{1,0},{2,3},{3,2},{4,5},{5,4},{6,7},{7,6},{8,9},{9,8},{10,11... | collective-permute-start | bytes 4718600 | tf_op jit(solution)/shard_map/ppermute | solution.py:34
  116.3 6.0 %collective-permute-start.3 = (bf16[8,24,128]{2,1,0:T(8,128)(2,1)S(1)}, bf16[8,24,128]{2,1,0:T(8,128)(2,1)S(1)}, u32[]{:S(2)}, u32[]{:S(2)}) collective-permute-start(bf16[8,24,128]{2,1,0:T(8,128)(2,1)S(1)} %get-tuple-element.39), channel_id=1, source_target_pairs={{0,2},{1,3},{2,0},{3,1},{4,6},{5,7},{6,4},{7,5},{8,10},{9,11},{10,... | collective-permute-start | bytes 147464 | tf_op jit(solution)/shard_map/ppermute | solution.py:34
  122.9 42.6 %all-to-all-start.3 = ((bf16[16,24,128]{2,1,0:T(8,128)(2,1)}), bf16[16,24,128]{2,1,0:T(8,128)(2,1)S(1)}, u32[]{:S(2)}, u32[]{:S(2)}) async-start(bf16[16,24,128]{2,1,0:T(8,128)(2,1)} %pad_maximum_fusion), calls=%async_computation.3 | async-start | bytes 196608 | tf_op jit(solution)/shard_map/all_to_all | solution.py:340
  165.6 0.6 copy-start.2

commit v4 on v3

--- a/solution.py
+++ b/solution.py
@@ -107,7 +107,8 @@
     return jnp.concatenate(heads, axis=1).astype(BF16)
 
 
-def attend_kernel(col_ref, row_ref, q_ref, k_ref, c_ref, out_ref):
+def attend_kernel(col_ref, row_ref, q_ref, k_ref, c_ref, behind_ref, out_ref):
+    del behind_ref
     tok = q_ref.shape[0]
     query = jnp.concatenate([q_ref[:, g * HD : (g + 1) * HD] for g in range(GROUP)], axis=0)
     context = jnp.concatenate([c_ref[:, g * HD : (g + 1) * HD] for g in range(GROUP)], axis=0)
@@ -120,7 +121,7 @@
     out_ref[...] = jnp.dot(probs, context, preferred_element_type=F32).astype(BF16)
 
 
-def attend(queries, key_rows, context_grad, segment):
+def attend(queries, key_rows, context_grad, segment, behind):
     tok = segment.shape[0]
     wide = pl.BlockSpec((tok, GROUP * HD), lambda h: (0, h))
     thin = pl.BlockSpec((tok, HD), lambda h: (0, h))
@@ -133,11 +134,12 @@
             wide,
             thin,
             wide,
+            pl.BlockSpec(memory_space=pl.ANY),
         ],
         out_specs=thin,
         out_shape=jax.ShapeDtypeStruct((tok, WIDTH), BF16),
         name="attend",
-    )(segment.reshape(tok, 1), segment.reshape(1, tok), queries, key_rows, context_grad)
+    )(segment.reshape(tok, 1), segment.reshape(1, tok), queries, key_rows, context_grad, behind)
 
 
 def gradient_kernel(block, core_ref, slot_ref, main_ref, first_ref, second_ref, act_ref, behind_ref, rows_ref, keep_ref, send_ref, whole):
@@ -277,26 +279,81 @@
     )(odd, pieces)
 
 
+def cut_out(shard, place):
+    cut, k = place // CUTS, place % CUTS
+    rows = lax.dynamic_slice(shard, (16 * cut, HD * k), (16, HD))
+    tile = lax.dynamic_slice(shard, (16 * CUTS + 8 * (cut // 2), HD * k), (8, HD))
+    return jnp.concatenate([rows, tile], axis=0)
+
+
+def spread_kernel(place_ref, pieces_ref, out_ref, paired):
+    count = pieces_ref.shape[0]
+
+    @pl.when(pl.program_id(0) == 0)
+    def _():
+        flip = place_ref[0] // CUTS % 2
+        upper = iota((8, HD), 0) // 4 == flip
+        for z in range(0, count, 2):
+            even, odd = ((z + i + count // 2) % count for i in range(2))
+            turned = pltpu.roll(pieces_ref[odd, 16:, :].astype(F32), 4, 0)
+            mixed = jnp.where(upper, pieces_ref[even, 16:, :].astype(F32), turned)
+            part = [pieces_ref[even, :16, :].astype(F32), pieces_ref[odd, :16, :].astype(F32), mixed]
+            paired[20 * z : 20 * z + 40, :] = jnp.concatenate(part, axis=0)
+
+    for at in range(out_ref.shape[0]):
+        out_ref[at] = paired[...].astype(BF16)
+
+
+def spread(place, pieces):
+    steps = 4
+    rows = pieces.shape[0] * 20
+    return pl.pallas_call(
+        spread_kernel,
+        grid_spec=pltpu.PrefetchScalarGridSpec(
+            num_scalar_prefetch=1,
+            grid=(steps,),
+            in_specs=[pl.BlockSpec(pieces.shape, lambda m, *_: (0, 0, 0))],
+            out_specs=pl.BlockSpec((PLANE // steps, rows, HD), lambda m, *_: (m, 0, 0)),
+            scratch_shapes=[pltpu.VMEM((rows, HD), F32)],
+        ),
+        out_shape=jax.ShapeDtypeStruct((PLANE, rows, HD), BF16),
+        compiler_params=pltpu.CompilerParams(vmem_limit_bytes=24 * 2**20),
+        name="spread",
+    )(place, pieces)
+
+
 def project_kernel(core_ref, rows_ref, own_ref, other_ref, out_ref, whole):
     core = core_ref[0]
-    shard = whole.shape[0] // (2 * own_ref.shape[1])
+    pairs = own_ref.shape[1] // 40
+    shard = whole.shape[0] // (4 * pairs)
+    upper = iota((8, HD), 0) < 4
     for source, parity in ((own_ref, core), (other_ref, 1 - core)):
-        for z in range(own_ref.shape[1]):
-            for cut in range(CUTS):
-                size = min(ROWS, shard - cut * ROWS)
-                start = pl.multiple_of(z * 2 * shard + parity * shard + cut * ROWS, 8)
-                for k in range(CUTS):
-                    part = source[cut * CUTS + k, z].astype(F32)
-                    whole[pl.ds(start, size), k * HD : (k + 1) * HD] = part[:size]
+        for pair in range(pairs):
+
+            def put(odd, start, k, value):
+                at = pl.multiple_of((4 * pair + 2 * odd + parity) * shard + start, 16)
+                whole[pl.ds(at, 16), k * HD : (k + 1) * HD] = value
+
+            for k in range(CUTS):
+                tiles = []
+                for cut in range(CUTS):
+                    piece = source[cut * CUTS + k, 40 * pair : 40 * pair + 32, :]
+                    put(0, 16 * cut, k, piece[:16])
+                    put(1, 16 * cut, k, piece[16:])
+                    tiles.append(source[cut * CUTS + k, 40 * pair + 32 : 40 * pair + 40, :].astype(F32))
+                evens = [jnp.where(upper, tiles[i], tiles[i + 1]) for i in (0, 2)]
+                odds = [pltpu.roll(jnp.where(upper, tiles[i + 1], tiles[i]), 4, 0) for i in (0, 2)]
+                put(0, 16 * CUTS, k, jnp.concatenate(evens, axis=0).astype(BF16))
+                put(1, 16 * CUTS, k, jnp.concatenate(odds, axis=0).astype(BF16))
     out_ref[...] = lax.dot_general(
-        rows_ref[...], whole[...].astype(BF16), ON_COLUMNS, preferred_element_type=F32
+        rows_ref[...], whole[...], ON_COLUMNS, preferred_element_type=F32
     ).astype(BF16)
 
 
 def project_back(core, row_grads, own, other, features):
     tok, width = row_grads.shape
     steps = 4
-    pieces = pl.BlockSpec((CUTS * CUTS, DEPTH // steps, ROWS, HD), lambda m, *_: (0, m, 0, 0))
+    pieces = pl.BlockSpec((PLANE, own.shape[1] // steps, HD), lambda m, *_: (0, m, 0))
     return pl.pallas_call(
         project_kernel,
         grid_spec=pltpu.PrefetchScalarGridSpec(
@@ -304,7 +361,7 @@
             grid=(steps,),
             in_specs=[pl.BlockSpec((tok, width), lambda m, *_: (0, 0)), pieces, pieces],
             out_specs=pl.BlockSpec((tok, features // steps), lambda m, *_: (0, m)),
-            scratch_shapes=[pltpu.VMEM((features // steps, width), F32)],
+            scratch_shapes=[pltpu.VMEM((features // steps, width), BF16)],
         ),
         out_shape=jax.ShapeDtypeStruct((tok, features), BF16),
         compiler_params=pltpu.CompilerParams(vmem_limit_bytes=24 * 2**20),
@@ -318,15 +375,9 @@
 
 
 def depth_gather(piece):
-    groups = [[2 * z + core for z in range(DEPTH)] for core in range(2)]
+    groups = [[2 * ((z + DEPTH // 2) % DEPTH) + core for z in range(DEPTH)] for core in range(2)]
     copies = jnp.broadcast_to(piece[None], (DEPTH, *piece.shape))
     return lax.all_to_all(copies, "fsdp", 0, 0, axis_index_groups=groups)
-
-
-def plane_gather(pieces):
-    rounds = 1 + lax.axis_index("dp") // lax.axis_size("dp")
-    copies = jnp.broadcast_to(pieces[None], (PLANE, *pieces.shape))
-    return lax.fori_loop(0, rounds, lambda _, held: plane_exchange(held), copies)
 
 
 def depth_exchange(pieces):
@@ -344,11 +395,6 @@
     return (one.astype(F32) + two.astype(F32)).astype(BF16)
 
 
-def cut_up(shard):
-    padded = jnp.pad(shard, ((0, CUTS * ROWS - shard.shape[0]), (0, 0)))
-    return padded.reshape(CUTS, ROWS, CUTS, HD).transpose(0, 2, 1, 3).reshape(CUTS * CUTS, ROWS, HD)
-
-
 def local(activations, value_weight, queries, key_rows, context_grad, segment, send_slot):
     tok, features = activations.shape
     block = (queries.shape[0] - tok) // SECTIONS
@@ -357,12 +403,17 @@
     core = (lax.axis_index("fsdp") % 2).astype(jnp.int32).reshape(1)
     odd = (lax.axis_index("fsdp") // 2 % 2).astype(jnp.int32).reshape(1)
 
-    piece = lax.dynamic_index_in_dim(cut_up(value_weight), place, 0, keepdims=False)
     first, second = messages(queries, key_rows, context_grad, tok, block)
     first = swapped(first, "dp", half)
-    second = swapped(second, "dp", half // 2)
-    own_weight = plane_gather(depth_gather(piece))
-    main = attend(queries, key_rows, context_grad, segment)
+    copies = spread(place.astype(jnp.int32).reshape(1), depth_gather(cut_out(value_weight, place)))
+
+    def beside(held):
+        copies, second, _ = held
+        main = attend(queries, key_rows, context_grad, segment, second)
+        return plane_exchange(copies), swapped(second, "dp", half // 2), main
+
+    held = (copies, second, jnp.zeros((tok, WIDTH), BF16))
+    own_weight, second, main = lax.cond(lax.axis_index("dp") < lax.axis_size("dp"), beside, lambda held: held, held)
     main, own_weight = lax.optimization_barrier((main, own_weight))
 
     row_grads, keep, send = gradient_pieces(core, send_slot, main, first, second, activations, own_weight, block)

time: 183 us -> 178 us (0.973)
  the two profiles are of different devices: /device:TPU:2 before, /device:TPU:32 now
where the time goes in v4:
time: 178 us; the launch traced here: 177 us
  starting transfers between devices  79 us (44%)
  waiting for transfers between devices  56.3 us (32%)
  Pallas kernels  19.7 us (11%)
  blocking collectives  13.1 us (7%)
  local copies, waits for them, and re-layouts  5.54 us (3%)
  other arithmetic  2.09 us (1%)
    ppermute x5, starting transfers between devices, swapped(): return lax.ppermute(block, axis, route)  25.7 us
    all_to_all x1, starting transfers between devices, depth_gather(): return lax.all_to_all(copies, 'fsdp', 0, 0, axis_index_groups=groups)  25 us
    all_to_all x2, waiting for transfers between devices, plane_exchange(): return lax.all_to_all(pieces, 'dp', 0, 0, axis_index_groups=groups)  19.1 us
    ppermute x5, waiting for transfers between devices, swapped(): return lax.ppermute(block, axis, route)  18.9 us
    all_to_all x1, waiting for transfers between devices, depth_exchange(): return lax.all_to_all(pieces, BOTH, 0, 0, axis_index_groups=groups)  18.2 us
    all_to_all x2, starting transfers between devices, plane_exchange(): return lax.all_to_all(pieces, 'dp', 0, 0, axis_index_groups=groups)  14.2 us
    all_to_all x1, starting transfers between devices, depth_exchange(): return lax.all_to_all(pieces, BOTH, 0, 0, axis_index_groups=groups)  14.1 us
    all_to_all x1, blocking collectives, plane_exchange(): return lax.all_to_all(pieces, 'dp', 0, 0, axis_index_groups=groups)  13.1 us
  transfers between devices with their start and end apart: 9, of which 6 were waited for; matrix products, arithmetic and copies ran while one was open for 2% of the time, Pallas kernels for 8%

profile of v4, /device:TPU:32, one launch (start us, length us, event | category | flops | bytes accessed | tf_op | source)
XLA Modules:
  0.0 176.7 jit_solution(6353889901318509375)
XLA Ops:
  0.7 0.7 dynamic_slice.7
  1.4 0.7 dynamic_slice.6
  2.1 0.7 broadcast_in_dim.4
  2.8 25.0 %all-to-all-start.1 = ((bf16[16,24,128]{2,1,0:T(8,128)(2,1)}), bf16[16,24,128]{2,1,0:T(8,128)(2,1)S(1)}, u32[]{:S(2)}, u32[]{:S(2)}) async-start(bf16[16,24,128]{2,1,0:T(8,128)(2,1)} %broadcast_in_dim.4), calls=%async_computation.1 | async-start | bytes 196608 | tf_op jit(solution)/shard_map/all_to_all | solution.py:380
  27.8 3.2 %messages.1 = (bf16[16,4608]{1,0:T(8,128)(2,1)}, bf16[16,4608]{1,0:T(8,128)(2,1)S(1)}) custom-call(bf16[192,2560]{1,0:T(8,128)(2,1)} %q_ref.1, bf16[192,512]{1,0:T(8,128)(2,1)} %k_ref.1, bf16[192,2560]{1,0:T(8,128)(2,1)} %c_ref.1), custom_call_target="tpu_custom_call" | custom-call | tf_op jit(solution)/shard_map/messages/pallas_call | solution.py:81
  30.9 14.6 %collective-permute-start.1 = (bf16[16,4608]{1,0:T(8,128)(2,1)}, bf16[16,4608]{1,0:T(8,128)(2,1)S(1)}, u32[]{:S(2)}, u32[]{:S(2)}) collective-permute-start(bf16[16,4608]{1,0:T(8,128)(2,1)} %get-tuple-element.44), channel_id=1, source_target_pairs={{0,512},{32,544},{64,576},{96,608},{128,640},{160,672},{192,704},{... | collective-permute-start | bytes 442376 | tf_op jit(solution)/shard_map/ppermute | solution.py:34
  45.7 1.7 spread.1
  47.5 29.5 %conditional.1 = (bf16[16,320,128]{2,1,0:T(8,128)(2,1)}, bf16[16,4608]{1,0:T(8,128)(2,1)S(1)}, bf16[128,512]{1,0:T(8,128)(2,1)}) conditional(s32[]{:T(128)} %convert_element_type.21, (bf16[16,320,128]{2,1,0:T(8,128)(2,1)}, bf16[16,4608]{1,0:T(8,128)(2,1)S(1)}) %tuple.18, (bf16[16,320,128]{2,1,0:T(8,128)(2,1)}, bf16[16,4608]{1,0:T(8,128)(2,1)S(1)}, ...), branch_computations={%region_0.1_spmd, %region_1.2_spmd} | conditional | bytes 7439456 | solution.py:416
  47.5 7.2 %all-to-all-start = ((bf16[16,320,128]{2,1,0:T(8,128)(2,1)}), bf16[16,320,128]{2,1,0:T(8,128)(2,1)S(1)}, u32[]{:S(2)}, u32[]{:S(2)}) async-start(bf16[16,320,128]{2,1,0:T(8,128)(2,1)} %get-tuple-element.18), calls=%async_computation | async-start | bytes 2621440 | tf_op jit(solution)/shard_map/cond/branch_1_fun/all_to_all | solution.py:374
  54.6 5.3 %collective-permute-start = (bf16[16,4608]{1,0:T(8,128)(2,1)S(1)}, bf16[16,4608]{1,0:T(8,128)(2,1)}, u32[]{:S(2)}, u32[]{:S(2)}) collective-permute-start(bf16[16,4608]{1,0:T(8,128)(2,1)S(1)} %get-tuple-element.19.behind_ref), channel_id=1, source_target_pairs={{0,256},{32,288},{64,320},{96,352},{128,384},{160,416},{192,448},{... | collective-permute-start | bytes 442376 | tf_op jit(solution)/shard_map/cond/branch_1_fun/ppermute | solution.py:34
  60.0 0.7 copy.10.col_ref
  60.7 4.0 %attend.1 = bf16[128,512]{1,0:T(8,128)(2,1)} custom-call(s32[128,1]{1,0:T(8,128)} %copy.10.col_ref, s32[1,128]{1,0:T(1,128)S(1)} %bitcast.8, bf16[192,2560]{1,0:T(8,128)(2,1)S(1)} %get-tuple-element.21.q_ref, bf16[192,512]{1,0:T(8,128)(2,1)S(1)} %get-tuple-element.22.k_ref, bf16[192,2560]{1,0:T(8,128)(2,1)} %get-tuple-element.23.c_ref, ...), custom_call_target="tpu_custom_call" | custom-call | tf_op jit(solution)/shard_map/cond/branch_1_fun/attend/pallas_call | solution.py:128
  64.7 10.3 %collective-permute-done = bf16[16,4608]{1,0:T(8,128)(2,1)} collective-permute-done((bf16[16,4608]{1,0:T(8,128)(2,1)S(1)}, bf16[16,4608]{1,0:T(8,128)(2,1)}, u32[]{:S(2)}, u32[]{:S(2)}) %collective-permute-start) | collective-permute-done | bytes 147488 | tf_op jit(solution)/shard_map/cond/branch_1_fun/ppermute | solution.py:34
  75.0 0.9 copy.16
  75.9 1.1 copy.15
  77.0 1.6 collective-permute-done.1.first_ref
  78.6 3.3 %gradient_pieces.1 = (bf16[128,512]{1,0:T(8,128)(2,1)S(1)}, bf16[16,8,40,128]{3,2,1,0:T(8,128)(2,1)S(1)}, bf16[16,8,40,128]{3,2,1,0:T(8,128)(2,1)S(1)}) custom-call(s32[1]{0:T(128)} %bitcast.3.core_ref, s32[128,1]{1,0:T(8,128)S(1)} %copy.11.slot_ref, bf16[128,512]{1,0:T(8,128)(2,1)} %get-tuple-element.43.main_ref, ...), custom_call_target="tpu_custom_call" | custom-call | tf_op jit(solution)/shard_map/gradient_pieces/pallas_call | solution.py:187
  81.9 1.9 %collective-permute-start.2 = (bf16[16,8,40,128]{3,2,1,0:T(8,128)(2,1)S(1)}, bf16[16,8,40,128]{3,2,1,0:T(8,128)(2,1)S(1)}, u32[]{:S(2)}, u32[]{:S(2)}) collective-permute-start(bf16[16,8,40,128]{3,2,1,0:T(8,128)(2,1)S(1)} %get-tuple-element.48), channel_id=1, source_target_pairs={{0,1},{1,0},{2,3},{3,2},{4,5},{5,4},{6,7},{7,6},{8,9},{9,8},{10,11... | collective-permute-start | bytes 3932168 | tf_op jit(solution)/shard_map/ppermute | solution.py:34
  83.8 3.0 %collective-permute-done.2 = bf16[16,8,40,128]{3,2,1,0:T(8,128)(2,1)S(1)} collective-permute-done((bf16[16,8,40,128]{3,2,1,0:T(8,128)(2,1)S(1)}, bf16[16,8,40,128]{3,2,1,0:T(8,128)(2,1)S(1)}, u32[]{:S(2)}, u32[]{:S(2)}) %collective-permute-start.2) | collective-permute-done | bytes 1310752 | tf_op jit(solution)/shard_map/ppermute | solution.py:34
  86.8 1.4 add_convert_fusion
  88.2 7.0 %all-to-all-start.2 = ((bf16[16,320,128]{2,1,0:T(8,128)(2,1)}), bf16[16,320,128]{2,1,0:T(8,128)(2,1)S(1)}, u32[]{:S(2)}, u32[]{:S(2)}) async-start(bf16[16,320,128]{2,1,0:T(8,128)(2,1)} %bitcast.6), calls=%async_computation.2 | async-start | bytes 2621440 | tf_op jit(solution)/shard_map/all_to_all | solution.py:374
  95.3 1.9 %collective-permute-start.4 = (bf16[16,320,128]{2,1,0:T(8,128)(2,1)}, bf16[16,320,128]{2,1,0:T(8,128)(2,1)S(1)}, u32[]{:S(2)}, u32[]{:S(2)}) collective-permute-start(bf16[16,320,128]{2,1,0:T(8,128)(2,1)} %get-tuple-element.46.behind_ref.own_ref), channel_id=1, source_target_pairs={{0,1},{1,0},{2,3},{3,2},{4,5},{5,4},{6,7},{7,6},{8,9},{9,8},{10,11... | collective-permute-start | bytes 3932168 | tf_op jit(solution)/shard_map/ppermute | solution.py:34
  97.2 19.1 %all-to-all-done.2.parts_ref = bf16[16,320,128]{2,1,0:T(8,128)(2,1)S(1)} async-done(((bf16[16,320,128]{2,1,0:T(8,128)(2,1)}), bf16[16,320,128]{2,1,0:T(8,128)(2,1)S(1)}, u32[]{:S(2)}, u32[]{:S(2)}) %all-to-all-start.2) | async-done | bytes 1310752 | tf_op jit(solution)/shard_map/all_to_all | solution.py:374
  116.6 1.9 %collective-permute-start.3 = (bf16[8,24,128]{2,1,0:T(8,128)(2,1)S(1)}, bf16[8,24,128]{2,1,0:T(8,128)(2,1)S(1)}, u32[]{:S(2)}, u32[]{:S(2)}) collective-permute-start(bf16[8,24,128]{2,1,0:T(8,128)(2,1)S(1)} %get-tuple-element.50), channel_id=1, source_target_pairs={{0,2},{1,3},{2,0},{3,1},{4,6},{5,7},{6,4},{7,5},{8,10},{9,11},{10,... | collective-permute-start | bytes 147464 | tf_op jit(solution)/shard_map/ppermute | solution.py:34
  118.5 4.1 %collective-permute-done.3 = bf16[8,24,128]{2,1,0:T(8,128)(2,1)S(1)} collective-permute-done((bf16[8,24,128]{2,1,0:T(8,128)(2,1)S(1)}, bf16[8,24,128]{2,1,0:T(8,128)(2,1)S(1)}, u32[]{:S(2)}, u32[]{:S(2)}) %collective-permute-start.3) | collective-permute-done | bytes 49184 | tf_op jit(solution)/shard_map/ppermute | solution.py:34
  122.6 0.7 pad_maximum_fusion
  123.2 14.1 %all-to-all-start.3 = ((bf16[16,24,128]{2,1,0:T(8,128)(2,1)}), bf16[16,24,128]{2,1,0:T(8,128)(2,1)S(1)}, u32[]{:S(2)}, u32[]{:S(2)}) async-start(bf16[16,24,128]{2,1,0:T(8,128)(2,1)} %pad_maximum_fusion), calls=%async_computation.3 | async-start | bytes 196608 | tf_op jit(solution)/shard_map/all_to_all | solution.py:391
  137.3 4.3 %project_back.1 = bf16[128,2560]{1,0:T(8,128)(2,1)} custom-call(s32[1]{0:T(128)} %bitcast.3.core_ref, bf16[128,512]{1,0:T(8,128)(2,1)S(1)} %get-tuple-element.51.rows_ref, bf16[16,320,128]{2,1,0:T(8,128)(2,1)} %get-tuple-element.46.behind_ref.own_ref, bf16[16,320,128]{2,1,0:T(8,128)(2,1)S(1)} %collective-permute-done.4.other_ref), custom_call_target="tpu_custom_call" | custom-call | tf_op jit(solution)/shard_map/project_back/pallas_call | solution.py:357
  141.6 18.2 %all-to-all-done.3.parts_ref = bf16[16,24,128]{2,1,0:T(8,128)(2,1)S(1)} async-done(((bf16[16,24,128]{2,1,0:T(8,128)(2,1)}), bf16[16,24,128]{2,1,0:T(8,128)(2,1)S(1)}, u32[]{:S(2)}, u32[]{:S(2)}) %all-to-all-start.3) | async-done | bytes 98336 | tf_op jit(solution)/shard_map/all_to_all | solution.py:391
  160.5 1.6 depth_sum.1
  162.0 13.1 %all_to_all.24.pieces_ref = bf16[16,24,128]{2,1,0:T(8,128)(2,1)} all-to-all(bf16[16,24,128]{2,1,0:T(8,128)(2,1)} %depth_sum.1), channel_id=1, replica_groups={{0,32,64,96,128,160,192,224,256,288,320,352,384,416,448,480},{512,544,5..., dimensions={0} | all-to-all | bytes 196608 | tf_op jit(solution)/shard_map/all_to_all | solution.py:374
  175.1 1.5 join.1
  (19 shorter events, 1.0 us)
Async XLA Ops:
  0.6 45.0 %copy-start.5 = (s32[128]{0:T(128)S(1)}, s32[128]{0:T(128)}, u32[]{:S(2)}) copy-start(s32[128]{0:T(128)} %param.15) | copy-start | bytes 1540
  2.8 43.0 %all-to-all-start.1 = ((bf16[16,24,128]{2,1,0:T(8,128)(2,1)}), bf16[16,24,128]{2,1,0:T(8,128)(2,1)S(1)}, u32[]{:S(2)}, u32[]{:S(2)}) async-start(bf16[16,24,128]{2,1,0:T(8,128)(2,1)} %broadcast_in_dim.4), calls=%async_computation.1 | async-start | bytes 196608 | tf_op jit(solution)/shard_map/all_to_all | solution.py:380
  27.8 19.7 %copy-start.1 = (bf16[192,2560]{1,0:T(8,128)(2,1)S(1)}, bf16[192,2560]{1,0:T(8,128)(2,1)}, u32[]{:S(2)}) copy-start(bf16[192,2560]{1,0:T(8,128)(2,1)} %q_ref.1) | copy-start | bytes 2949124
  27.8 19.7 %copy-start.2 = (bf16[192,512]{1,0:T(8,128)(2,1)S(1)}, bf16[192,512]{1,0:T(8,128)(2,1)}, u32[]{:S(2)}) copy-start(bf16[192,512]{1,0:T(8,128)(2,1)} %k_ref.1) | copy-start | bytes 589828
  27.8 19.7 %copy-start.4 = (s32[128]{0:T(128)S(1)}, s32[128]{0:T(128)}, u32[]{:S(2)}) copy-start(s32[128]{0:T(128)} %param.14) | copy-start | bytes 1540
  30.9 47.6 %collective-permute-start.1 = (bf16[16,4608]{1,0:T(8,128)(2,1)}, bf16[16,4608]{1,0:T(8,128)(2,1)S(1)}, u32[]{:S(2)}, u32[]{:S(2)}) collective-permute-start(bf16[16,4608]{1,0:T(8,128)(2,1)} %get-tuple-element.44), channel_id=1, source_target_pairs={{0,512},{32,544},{64,576},{96,608},{128,640},{160,672},{192,704},{... | collective-permute-start | bytes 442376 | tf_op jit(solution)/shard_map/ppermute | solution.py:34
  47.4 31.1 %copy-start = (bf16[128,2560]{1,0:T(8,128)(2,1)S(1)}, bf16[128,2560]{1,0:T(8,128)(2,1)}, u32[]{:S(2)}) copy-start(bf16[128,2560]{1,0:T(8,128)(2,1)} %act_ref.1) | copy-start | bytes 1966084
  47.5 28.5 %all-to-all-start = ((bf16[16,320,128]{2,1,0:T(8,128)(2,1)}), bf16[16,320,128]{2,1,0:T(8,128)(2,1)S(1)}, u32[]{:S(2)}, u32[]{:S(2)}) async-start(bf16[16,320,128]{2,1,0:T(8,128)(2,1)} %get-tuple-element.18), calls=%async_computation | async-start | bytes 2621440 | tf_op jit(solution)/shard_map/cond/branch_1_fun/all_to_all | solution.py:374
  54.6 20.4 %collective-permute-start = (bf16[16,4608]{1,0:T(8,128)(2,1)S(1)}, bf16[16,4608]{1,0:T(8,128)(2,1)}, u32[]{:S(2)}, u32[]{:S(2)}) collective-permute-start(bf16[16,4608]{1,0:T(8,128)(2,1)S(1)} %get-tuple-element.19.behind_ref), channel_id=1, source_target_pairs={{0,256},{32,288},{64,320},{96,352},{128,384},{160,416},{192,448},{... | collective-permute-start | bytes 442376 | tf_op jit(solution)/shard_map/cond/branch_1_fun/ppermute | solution.py:34
  81.9 4.9 %collective-permute-start.2 = (bf16[16,8,40,128]{3,2,1,0:T(8,128)(2,1)S(1)}, bf16[16,8,40,128]{3,2,1,0:T(8,128)(2,1)S(1)}, u32[]{:S(2)}, u32[]{:S(2)}) collective-permute-start(bf16[16,8,40,128]{3,2,1,0:T(8,128)(2,1)S(1)} %get-tuple-element.48), channel_id=1, source_target_pairs={{0,1},{1,0},{2,3},{3,2},{4,5},{5,4},{6,7},{7,6},{8,9},{9,8},{10,11... | collective-permute-start | bytes 3932168 | tf_op jit(solution)/shard_map/ppermute | solution.py:34
  88.2 28.1 %all-to-all-start.2 = ((bf16[16,320,128]{2,1,0:T(8,128)(2,1)}), bf16[16,320,128]{2,1,0:T(8,128)(2,1)S(1)}, u32[]{:S(2)}, u32[]{:S(2)}) async-start(bf16[16,320,128]{2,1,0:T(8,128)(2,1)} %bitcast.6), calls=%async_computation.2 | async-start | bytes 2621440 | tf_op jit(solution)/shard_map/all_to_all | solution.py:374
  95.3 42.0 %collective-permute-start.4 = (bf16[16,320,128]{2,1,0:T(8,128)(2,1)}, bf16[16,320,128]{2,1,0:T(8,128)(2,1)S(1)}, u32[]{:S(2)}, u32[]{:S(2)}) collective-permute-start(bf16[16,320,128]{2,1,0:T(8,128)(2,1)} %get-tuple-element.46.behind_ref.own_ref), channel_id=1, source_target_pairs={{0,1},{1,0},{2,3},{3,2},{4,5},{5,4},{6,7},{7,6},{8,9},{9,8},{10,11... | collective-permute-start | bytes 3932168 | tf_op jit(solution)/shard_map/ppermute | solution.py:34
  116.6 6.0 %collective-permute-start.3 = (bf16[8,24,128]{2,1,0:T(8,128)(2,1)S(1)}, bf16[8,24,128]{2,1,0:T(8,128)(2,1)S(1)}, u32[]{:S(2)}, u32[]{:S(2)}) collective-permute-start(bf16[8,24,128]{2,1,0:T(8,128)(2,1)S(1)} %get-tuple-element.50), channel_id=1, source_target_pairs={{0,2},{1,3},{2,0},{3,1},{4,6},{5,7},{6,4},{7,5},{8,10},{9,11},{10,... | collective-permute-start | bytes 147464 | tf_op jit(solution)/shard_map/ppermute | solution.py:34
  123.2 36.6 %all-to-all-start.3 = ((bf16[16,24,128]{2,1,0:T(8,128)(2,1)}), bf16[16,24,128]{2,1,0:T(8,128)(2,1)S(1)}, u32[]{:S(2)}, u32[]{:S(2)}) async-start(bf16[16,24,128]{2,1,0:T(8,128)(2,1)} %pad_maximum_fusion), calls=%async_computation.3 | async-start | bytes 196608 | tf_op jit(solution)/shard_map/all_to_all | solution.py:391
  159.8 0.6 copy-start.3

commit v5 on v4

--- a/solution.py
+++ b/solution.py
@@ -22,9 +22,10 @@
 F32 = jnp.float32
 WIDTH = KVH * HD
 FEATURES = KVH * GROUP * HD
+LATE = GROUP * LEAST
 SUMS = FEATURES
-PROBS = SUMS + 2 * WIDTH
-MESSAGE = PROBS + 2 * KVH * HD
+PROBS = SUMS + WIDTH
+MESSAGE = PROBS + 2 * KVH * LATE
 SCALE = 1.0 / math.sqrt(HD)
 ON_COLUMNS = (((1,), (1,)), ((), ()))
 
@@ -37,7 +38,7 @@
 def softmax_down(scores, allowed):
     masked = jnp.where(allowed, scores * SCALE, -jnp.inf)
     exponent = jnp.exp(masked - jnp.max(masked, axis=0, keepdims=True))
-    return (exponent * (1.0 / jnp.sum(exponent, axis=0, keepdims=True))).astype(BF16)
+    return exponent * (1.0 / jnp.sum(exponent, axis=0, keepdims=True))
 
 
 def iota(shape, dim):
@@ -48,7 +49,8 @@
     for section, out_ref in enumerate(out_refs):
         low = section * block
         out_ref[:, :FEATURES] = c_ref[low + LEAST : low + block, :]
-        pad = jnp.zeros((HD - GROUP * LEAST, HD), BF16)
+        pad = jnp.zeros((HD - LATE, HD), BF16)
+        late = []
         for h in range(KVH):
 
             def stacked(ref, start):
@@ -58,19 +60,15 @@
             keys = k_ref[low : low + block, h * HD : (h + 1) * HD]
             scores = lax.dot_general(keys, stacked(q_ref, low + LEAST), ON_COLUMNS, preferred_element_type=F32)
             allowed = iota((block, HD), 0) <= iota((block, HD), 1) % LEAST + LEAST
-            probs = softmax_down(scores, allowed)
-            at = PROBS + 2 * h * HD
-            out_ref[:, at : at + HD] = probs[:LEAST]
-            out_ref[:, at + HD : at + 2 * HD] = probs[LEAST:]
+            late.append(softmax_down(scores, allowed)[:, :LATE])
 
             scores = lax.dot_general(keys[:LEAST], stacked(q_ref, low), ON_COLUMNS, preferred_element_type=F32)
             allowed = iota((LEAST, HD), 0) <= iota((LEAST, HD), 1) % LEAST
-            probs = softmax_down(scores, allowed)
+            probs = softmax_down(scores, allowed).astype(BF16)
             sums = jnp.dot(probs, stacked(c_ref, low), preferred_element_type=F32)
-            coarse = sums.astype(BF16)
-            at = SUMS + h * HD
-            out_ref[:, at : at + HD] = coarse
-            out_ref[:, at + WIDTH : at + WIDTH + HD] = (sums - coarse.astype(F32)).astype(BF16)
+            out_ref[:, SUMS + h * HD : SUMS + (h + 1) * HD] = sums.astype(BF16)
+        late = [x[start : start + LEAST] for start in range(0, block, LEAST) for x in late]
+        out_ref[:, PROBS:] = jnp.concatenate(late, axis=1).astype(BF16)
 
 
 def messages(queries, key_rows, context_grad, tok, block):
@@ -84,7 +82,7 @@
         in_specs=specs,
         out_specs=[pl.BlockSpec(shape, lambda i: (0, 0))] * SECTIONS,
         out_shape=[jax.ShapeDtypeStruct(shape, BF16)] * SECTIONS,
-        compiler_params=pltpu.CompilerParams(vmem_limit_bytes=56 * 2**20),
+        compiler_params=pltpu.CompilerParams(vmem_limit_bytes=24 * 2**20),
         name="messages",
     )(queries, key_rows, context_grad)
 
@@ -92,18 +90,19 @@
 def sent_block(slot, message_ref, low, block):
     inside = (slot >= low) & (slot < low + block)
     count = jnp.sum(inside.astype(jnp.int32), axis=0, keepdims=True)
-    pad = jnp.zeros((HD - GROUP * LEAST, HD), BF16)
+    held = iota((block, HD), 1) % LEAST + LEAST < count
+    pad = jnp.zeros((HD - LATE, HD), BF16)
+    late = message_ref[:, PROBS:].astype(F32)
     heads = []
     for h in range(KVH):
-        at = PROBS + 2 * h * HD
-        probs = jnp.concatenate([message_ref[:, at : at + HD], message_ref[:, at + HD : at + 2 * HD]], axis=0)
-        held = iota(probs.shape, 1) % LEAST + LEAST < count
-        probs = jnp.where(held, probs.astype(F32), 0.0).astype(BF16)
+        parts = [late[:, (half * KVH + h) * LATE : (half * KVH + h + 1) * LATE] for half in range(block // LEAST)]
+        probs = jnp.concatenate(parts, axis=0)
+        probs = jnp.concatenate([probs, jnp.zeros((block, HD - LATE), F32)], axis=1)
+        probs = jnp.where(held, probs, 0.0).astype(BF16)
         rows = [message_ref[:, (h * GROUP + g) * HD : (h * GROUP + g + 1) * HD] for g in range(GROUP)]
-        late = jnp.dot(probs, jnp.concatenate([*rows, pad], axis=0), preferred_element_type=F32)
-        at = SUMS + h * HD
-        early = message_ref[:, at : at + HD].astype(F32) + message_ref[:, at + WIDTH : at + WIDTH + HD].astype(F32)
-        heads.append(late + jnp.concatenate([early, jnp.zeros((block - LEAST, HD), F32)], axis=0))
+        sums = jnp.dot(probs, jnp.concatenate([*rows, pad], axis=0), preferred_element_type=F32)
+        early = message_ref[:, SUMS + h * HD : SUMS + (h + 1) * HD].astype(F32)
+        heads.append(sums + jnp.concatenate([early, jnp.zeros((block - LEAST, HD), F32)], axis=0))
     return jnp.concatenate(heads, axis=1).astype(BF16)
 
 
@@ -142,68 +141,73 @@
     )(segment.reshape(tok, 1), segment.reshape(1, tok), queries, key_rows, context_grad, behind)
 
 
-def gradient_kernel(block, core_ref, slot_ref, main_ref, first_ref, second_ref, act_ref, behind_ref, rows_ref, keep_ref, send_ref, whole):
-    del behind_ref
-    tok = slot_ref.shape[0]
-
-    @pl.when(pl.program_id(0) == 0)
-    def _():
-        slot = slot_ref[...]
-        parts = [sent_block(slot, ref, tok + s * block, block) for s, ref in enumerate((first_ref, second_ref))]
-        held = jnp.concatenate([main_ref[...], *parts], axis=0)
-        chosen = (slot == iota((tok, held.shape[0]), 1)).astype(F32).astype(BF16)
-        rows_ref[...] = jnp.dot(chosen, held, preferred_element_type=F32).astype(BF16)
-
+def rows_kernel(block, slot_ref, main_ref, first_ref, second_ref, out_ref):
+    slot = slot_ref[...]
+    tok = slot.shape[0]
+    parts = [sent_block(slot, ref, tok + s * block, block) for s, ref in enumerate((first_ref, second_ref))]
+    held = jnp.concatenate([main_ref[...], *parts], axis=0)
+    chosen = (slot == iota((tok, held.shape[0]), 1)).astype(F32).astype(BF16)
+    out_ref[...] = jnp.dot(chosen, held, preferred_element_type=F32).astype(BF16)
+
+
+def own_rows(send_slot, main, first, second, block):
+    tok = main.shape[0]
+    operands = (send_slot.reshape(tok, 1), main, first, second)
+    return pl.pallas_call(
+        functools.partial(rows_kernel, block),
+        grid=(1,),
+        in_specs=[pl.BlockSpec(x.shape, lambda i: (0, 0)) for x in operands],
+        out_specs=pl.BlockSpec(main.shape, lambda i: (0, 0)),
+        out_shape=jax.ShapeDtypeStruct(main.shape, BF16),
+        compiler_params=pltpu.CompilerParams(vmem_limit_bytes=24 * 2**20),
+        name="own_rows",
+    )(*operands)
+
+
+def gradient_kernel(core_ref, rows_ref, other_rows_ref, act_ref, other_act_ref, out_ref, whole):
     whole[...] = lax.dot_general(
-        act_ref[...], rows_ref[...], (((0,), (0,)), ((), ())), preferred_element_type=F32
+        jnp.concatenate([act_ref[...], other_act_ref[...]], axis=0),
+        jnp.concatenate([rows_ref[...], other_rows_ref[...]], axis=0),
+        (((0,), (0,)), ((), ())),
+        preferred_element_type=F32,
     )
     core = core_ref[0]
-    pairs = keep_ref.shape[1]
+    pairs = out_ref.shape[1] // 40
     shard = whole.shape[0] // (4 * pairs)
     upper = iota((8, WIDTH), 0) < 4
-    for target, parity in ((keep_ref, core), (send_ref, 1 - core)):
-        for pair in range(pairs):
-
-            def rows(odd, start, size):
-                at = (4 * pair + 2 * odd + parity) * shard + start
-                return whole[pl.ds(pl.multiple_of(at, 8), size), :]
-
-            for cut in range(CUTS):
-                split = 16 * CUTS + 8 * (cut // 2)
-                even, odd = rows(0, split, 8), pltpu.roll(rows(1, split, 8), 4, 0)
-                mixed = jnp.where(upper, even, odd) if cut % 2 == 0 else jnp.where(upper, odd, even)
-                piece = jnp.concatenate([rows(0, 16 * cut, 16), rows(1, 16 * cut, 16), mixed], axis=0).astype(BF16)
-                for k in range(CUTS):
-                    target[cut * CUTS + k, pair] = piece[:, k * HD : (k + 1) * HD]
-
-
-def gradient_pieces(core, send_slot, main, first, second, activations, behind, block):
+    for pair in range(pairs):
+
+        def rows(odd, start, size):
+            at = (4 * pair + 2 * odd + core) * shard + start
+            return whole[pl.ds(pl.multiple_of(at, 8), size), :]
+
+        for cut in range(CUTS):
+            split = 16 * CUTS + 8 * (cut // 2)
+            even, odd = rows(0, split, 8), pltpu.roll(rows(1, split, 8), 4, 0)
+            mixed = jnp.where(upper, even, odd) if cut % 2 == 0 else jnp.where(upper, odd, even)
+            piece = jnp.concatenate([rows(0, 16 * cut, 16), rows(1, 16 * cut, 16), mixed], axis=0).astype(BF16)
+            for k in range(CUTS):
+                out_ref[cut * CUTS + k, 40 * pair : 40 * pair + 40, :] = piece[:, k * HD : (k + 1) * HD]
+
+
+def gradient_pieces(core, rows, other_rows, activations, other_activations):
     tok, features = activations.shape
     steps = 4
     held = pl.BlockSpec((tok, WIDTH), lambda m, *_: (0, 0))
-    message = pl.BlockSpec(first.shape, lambda m, *_: (0, 0))
-    pieces = pl.BlockSpec((CUTS * CUTS, DEPTH // 2 // steps, 40, HD), lambda m, *_: (0, m, 0, 0))
-    shape = jax.ShapeDtypeStruct((CUTS * CUTS, DEPTH // 2, 40, HD), BF16)
-    return pl.pallas_call(
-        functools.partial(gradient_kernel, block),
+    columns = pl.BlockSpec((tok, features // steps), lambda m, *_: (0, m))
+    return pl.pallas_call(
+        gradient_kernel,
         grid_spec=pltpu.PrefetchScalarGridSpec(
             num_scalar_prefetch=1,
             grid=(steps,),
-            in_specs=[
-                pl.BlockSpec((tok, 1), lambda m, *_: (0, 0)),
-                held,
-                message,
-                message,
-                pl.BlockSpec((tok, features // steps), lambda m, *_: (0, m)),
-                pl.BlockSpec(memory_space=pl.ANY),
-            ],
-            out_specs=[held, pieces, pieces],
+            in_specs=[held, held, columns, columns],
+            out_specs=pl.BlockSpec((CUTS * CUTS, 20 * DEPTH // steps, HD), lambda m, *_: (0, m, 0)),
             scratch_shapes=[pltpu.VMEM((features // steps, WIDTH), F32)],
         ),
-        out_shape=[jax.ShapeDtypeStruct((tok, WIDTH), BF16), shape, shape],
+        out_shape=jax.ShapeDtypeStruct((CUTS * CUTS, 20 * DEPTH, HD), BF16),
         compiler_params=pltpu.CompilerParams(vmem_limit_bytes=24 * 2**20),
         name="gradient_pieces",
-    )(core, send_slot.reshape(tok, 1), main, first, second, activations, behind)
+    )(core, rows, other_rows, activations, other_activations)
 
 
 def plane_sum_kernel(odd_ref, parts_ref, keep_ref, send_ref, whole):
@@ -217,8 +221,9 @@
             target[pair] = jnp.concatenate([own, whole[pair, 32:40, :]], axis=0).astype(BF16)
 
 
-def plane_sum(odd, parts, pairs, rows):
-    count, _, lanes = parts.shape
+def plane_sum(odd, parts):
+    count, rows, lanes = parts.shape
+    pairs, rows = rows // 40, 40
     out = pl.BlockSpec((pairs, ROWS, lanes), lambda i, *_: (0, 0, 0))
     return pl.pallas_call(
         plane_sum_kernel,
@@ -233,20 +238,6 @@
         compiler_params=pltpu.CompilerParams(vmem_limit_bytes=24 * 2**20),
         name="plane_sum",
     )(odd, parts)
-
-
-def depth_sum_kernel(parts_ref, out_ref):
-    total = jnp.sum(parts_ref[...].astype(F32), axis=0).astype(BF16)
-    for at in range(out_ref.shape[0]):
-        out_ref[at] = total
-
-
-def depth_sum(parts):
-    return pl.pallas_call(
-        depth_sum_kernel,
-        out_shape=jax.ShapeDtypeStruct((PLANE, *parts.shape[1:]), BF16),
-        name="depth_sum",
-    )(parts)
 
 
 def join_kernel(odd_ref, pieces_ref, out_ref):
@@ -408,27 +399,29 @@
     copies = spread(place.astype(jnp.int32).reshape(1), depth_gather(cut_out(value_weight, place)))
 
     def beside(held):
-        copies, second, _ = held
+        copies, second, _, act = held
         main = attend(queries, key_rows, context_grad, segment, second)
-        return plane_exchange(copies), swapped(second, "dp", half // 2), main
-
-    held = (copies, second, jnp.zeros((tok, WIDTH), BF16))
-    own_weight, second, main = lax.cond(lax.axis_index("dp") < lax.axis_size("dp"), beside, lambda held: held, held)
+        return plane_exchange(copies), swapped(second, "dp", half // 2), main, swapped(act, "fsdp", 1)
+
+    held = (copies, second, jnp.zeros((tok, WIDTH), BF16), activations)
+    own_weight, second, main, other_act = lax.cond(
+        lax.axis_index("dp") < lax.axis_size("dp"), beside, lambda held: held, held
+    )
     main, own_weight = lax.optimization_barrier((main, own_weight))
 
-    row_grads, keep, send = gradient_pieces(core, send_slot, main, first, second, activations, own_weight, block)
-    came = swapped(send, "fsdp", 1)
-    _, pairs, rows, _ = keep.shape
-    parts = plane_exchange(added(keep, came).reshape(PLANE, pairs * rows, HD))
+    row_grads = own_rows(send_slot, main, first, second, block)
+    other_rows = swapped(row_grads, "fsdp", 1)
+    parts = plane_exchange(gradient_pieces(core, row_grads, other_rows, activations, other_act))
     other_weight = swapped(own_weight, "fsdp", 1)
 
-    keep, send = plane_sum(odd, parts, pairs, rows)
+    keep, send = plane_sum(odd, parts)
     came = swapped(send, "fsdp", 2)
     depth_part = added(keep, came)
     depth_parts = depth_exchange(jnp.concatenate([depth_part, depth_part], axis=0))
     input_grad = project_back(core, row_grads, own_weight, other_weight, features)
     depth_parts, input_grad = lax.optimization_barrier((depth_parts, input_grad))
-    finished = plane_exchange(depth_sum(depth_parts))
+    finished = jnp.sum(depth_parts.astype(F32), axis=0).astype(BF16)
+    finished = plane_exchange(jnp.broadcast_to(finished[None], (PLANE, *finished.shape)))
     weight_grad = join(odd, finished, value_weight.shape[0])
     return (input_grad, weight_grad)
 

time: 178 us -> 169 us (0.949)
  the two profiles are of different devices: /device:TPU:32 before, /device:TPU:2 now
where the time goes in v5:
time: 169 us; the launch traced here: 168 us
  starting transfers between devices  77.9 us (46%)
  waiting for transfers between devices  49.7 us (29%)
  Pallas kernels  20.5 us (12%)
  blocking collectives  12.3 us (7%)
  local copies, waits for them, and re-layouts  5.57 us (3%)
    ppermute x6, starting transfers between devices, swapped(): return lax.ppermute(block, axis, route)  26.8 us
    all_to_all x1, starting transfers between devices, depth_gather(): return lax.all_to_all(copies, 'fsdp', 0, 0, axis_index_groups=groups)  26.4 us
    all_to_all x1, waiting for transfers between devices, depth_exchange(): return lax.all_to_all(pieces, BOTH, 0, 0, axis_index_groups=groups)  20.3 us
    all_to_all x2, waiting for transfers between devices, plane_exchange(): return lax.all_to_all(pieces, 'dp', 0, 0, axis_index_groups=groups)  16.5 us
    all_to_all x2, starting transfers between devices, plane_exchange(): return lax.all_to_all(pieces, 'dp', 0, 0, axis_index_groups=groups)  13.4 us
    ppermute x6, waiting for transfers between devices, swapped(): return lax.ppermute(block, axis, route)  12.9 us
    all_to_all x1, blocking collectives, plane_exchange(): return lax.all_to_all(pieces, 'dp', 0, 0, axis_index_groups=groups)  12.3 us
    all_to_all x1, starting transfers between devices, depth_exchange(): return lax.all_to_all(pieces, BOTH, 0, 0, axis_index_groups=groups)  11.3 us
  transfers between devices with their start and end apart: 10, of which 5 were waited for; matrix products, arithmetic and copies ran while one was open for 2% of the time, Pallas kernels for 8%

profile of v5, /device:TPU:2, one launch (start us, length us, event | category | flops | bytes accessed | tf_op | source)
XLA Modules:
  0.0 167.6 jit_solution(5993887616245376837)
XLA Ops:
  0.7 0.7 dynamic_slice.6
  1.4 0.7 dynamic_slice.7
  2.1 0.7 broadcast_in_dim.7
  2.8 26.4 %all-to-all-start.1 = ((bf16[16,24,128]{2,1,0:T(8,128)(2,1)}), bf16[16,24,128]{2,1,0:T(8,128)(2,1)S(1)}, u32[]{:S(2)}, u32[]{:S(2)}) async-start(bf16[16,24,128]{2,1,0:T(8,128)(2,1)} %broadcast_in_dim.7), calls=%async_computation.1 | async-start | bytes 196608 | tf_op jit(solution)/shard_map/all_to_all | solution.py:371
  29.2 3.3 %messages.1 = (bf16[16,3712]{1,0:T(8,128)(2,1)S(1)}, bf16[16,3712]{1,0:T(8,128)(2,1)}) custom-call(bf16[192,2560]{1,0:T(8,128)(2,1)} %q_ref.1, bf16[192,512]{1,0:T(8,128)(2,1)} %k_ref.1, bf16[192,2560]{1,0:T(8,128)(2,1)} %c_ref.1), custom_call_target="tpu_custom_call" | custom-call | tf_op jit(solution)/shard_map/messages/pallas_call | solution.py:79
  32.5 14.6 %collective-permute-start.2 = (bf16[16,3712]{1,0:T(8,128)(2,1)S(1)}, bf16[16,3712]{1,0:T(8,128)(2,1)S(1)}, u32[]{:S(2)}, u32[]{:S(2)}) collective-permute-start(bf16[16,3712]{1,0:T(8,128)(2,1)S(1)} %get-tuple-element.48), channel_id=1, source_target_pairs={{0,512},{32,544},{64,576},{96,608},{128,640},{160,672},{192,704},{... | collective-permute-start | bytes 356360 | tf_op jit(solution)/shard_map/ppermute | solution.py:35
  47.3 1.7 %spread.1 = bf16[16,320,128]{2,1,0:T(8,128)(2,1)} custom-call(s32[1]{0:T(128)} %bitcast.5.place_ref, bf16[16,24,128]{2,1,0:T(8,128)(2,1)S(1)} %all-to-all-done.1.pieces_ref), custom_call_target="tpu_custom_call" | custom-call | tf_op jit(solution)/shard_map/spread/pallas_call | solution.py:301
  49.0 28.9 %conditional.1 = (bf16[16,320,128]{2,1,0:T(8,128)(2,1)}, bf16[16,3712]{1,0:T(8,128)(2,1)}, bf16[128,512]{1,0:T(8,128)(2,1)S(1)}, bf16[128,2560]{1,0:T(8,128)(2,1)}) conditional(s32[]{:T(128)} %convert_element_type.14, (bf16[16,320,128]{2,1,0:T(8,128)(2,1)}, bf16[16,3712]{1,0:T(8,128)(2,1)}, bf16[128,2560]{1,0:T(8,128)(2,1)S(1)}) %tuple.26, ...), branch_computations={%region_0.1_spmd, %region_1.2_spmd} | conditional | bytes 10413228 | solution.py:407
  49.0 7.5 %all-to-all-start = ((bf16[16,320,128]{2,1,0:T(8,128)(2,1)}), bf16[16,320,128]{2,1,0:T(8,128)(2,1)S(1)}, u32[]{:S(2)}, u32[]{:S(2)}) async-start(bf16[16,320,128]{2,1,0:T(8,128)(2,1)} %get-tuple-element.23), calls=%async_computation | async-start | bytes 2621440 | tf_op jit(solution)/shard_map/cond/branch_1_fun/all_to_all | solution.py:365
  56.5 1.9 %collective-permute-start.1 = (bf16[128,2560]{1,0:T(8,128)(2,1)S(1)}, bf16[128,2560]{1,0:T(8,128)(2,1)}, u32[]{:S(2)}, u32[]{:S(2)}) collective-permute-start(bf16[128,2560]{1,0:T(8,128)(2,1)S(1)} %get-tuple-element.29), channel_id=1, source_target_pairs={{0,1},{1,0},{2,3},{3,2},{4,5},{5,4},{6,7},{7,6},{8,9},{9,8},{10,11... | collective-permute-start | bytes 1966088 | tf_op jit(solution)/shard_map/cond/branch_1_fun/ppermute | solution.py:35
  58.4 4.0 %collective-permute-start = (bf16[16,3712]{1,0:T(8,128)(2,1)}, bf16[16,3712]{1,0:T(8,128)(2,1)}, u32[]{:S(2)}, u32[]{:S(2)}) collective-permute-start(bf16[16,3712]{1,0:T(8,128)(2,1)} %get-tuple-element.24.behind_ref), channel_id=1, source_target_pairs={{0,256},{32,288},{64,320},{96,352},{128,384},{160,416},{192,448},{... | collective-permute-start | bytes 356360 | tf_op jit(solution)/shard_map/cond/branch_1_fun/ppermute | solution.py:35
  62.4 0.7 copy.10.col_ref
  63.1 4.0 %attend.1 = bf16[128,512]{1,0:T(8,128)(2,1)} custom-call(s32[128,1]{1,0:T(8,128)} %copy.10.col_ref, s32[1,128]{1,0:T(1,128)S(1)} %bitcast.7, bf16[192,2560]{1,0:T(8,128)(2,1)S(1)} %get-tuple-element.26.q_ref, bf16[192,512]{1,0:T(8,128)(2,1)S(1)} %get-tuple-element.27.k_ref, bf16[192,2560]{1,0:T(8,128)(2,1)} %get-tuple-element.28.c_ref, ...), custom_call_target="tpu_custom_call" | custom-call | tf_op jit(solution)/shard_map/cond/branch_1_fun/attend/pallas_call | solution.py:127
  67.1 8.1 %collective-permute-done = bf16[16,3712]{1,0:T(8,128)(2,1)} collective-permute-done((bf16[16,3712]{1,0:T(8,128)(2,1)}, bf16[16,3712]{1,0:T(8,128)(2,1)}, u32[]{:S(2)}, u32[]{:S(2)}) %collective-permute-start) | collective-permute-done | bytes 118816 | tf_op jit(solution)/shard_map/cond/branch_1_fun/ppermute | solution.py:35
  75.2 1.6 copy.17
  76.8 1.1 copy.16
  77.9 1.3 own_rows.1.rows_ref
  79.2 1.9 %collective-permute-start.3 = (bf16[128,512]{1,0:T(8,128)(2,1)S(1)}, bf16[128,512]{1,0:T(8,128)(2,1)S(1)}, u32[]{:S(2)}, u32[]{:S(2)}) collective-permute-start(bf16[128,512]{1,0:T(8,128)(2,1)S(1)} %own_rows.1.rows_ref), channel_id=1, source_target_pairs={{0,1},{1,0},{2,3},{3,2},{4,5},{5,4},{6,7},{7,6},{8,9},{9,8},{10,11... | collective-permute-start | bytes 393224 | tf_op jit(solution)/shard_map/ppermute | solution.py:35
  81.2 1.3 collective-permute-done.3.other_rows_ref
  82.5 4.2 %gradient_pieces.1 = bf16[16,320,128]{2,1,0:T(8,128)(2,1)} custom-call(s32[1]{0:T(128)} %bitcast.3.core_ref, bf16[128,512]{1,0:T(8,128)(2,1)S(1)} %own_rows.1.rows_ref, bf16[128,512]{1,0:T(8,128)(2,1)S(1)} %collective-permute-done.3.other_rows_ref, bf16[128,2560]{1,0:T(8,128)(2,1)S(1)} %copy-done.1, bf16[128,2560]{1,0:T(8,128)(2,1)} %get-tuple-element.50.other_act_ref), custom_call_target="tpu_custom_call" | custom-call | tf_op jit(solution)/shard_map/gradient_pieces/pallas_call | solution.py:198
  86.6 5.9 %all-to-all-start.2 = ((bf16[16,320,128]{2,1,0:T(8,128)(2,1)}), bf16[16,320,128]{2,1,0:T(8,128)(2,1)S(1)}, u32[]{:S(2)}, u32[]{:S(2)}) async-start(bf16[16,320,128]{2,1,0:T(8,128)(2,1)} %gradient_pieces.1), calls=%async_computation.2 | async-start | bytes 2621440 | tf_op jit(solution)/shard_map/all_to_all | solution.py:365
  92.5 1.9 %collective-permute-start.5 = (bf16[16,320,128]{2,1,0:T(8,128)(2,1)}, bf16[16,320,128]{2,1,0:T(8,128)(2,1)S(1)}, u32[]{:S(2)}, u32[]{:S(2)}) collective-permute-start(bf16[16,320,128]{2,1,0:T(8,128)(2,1)} %get-tuple-element.53.own_ref), channel_id=1, source_target_pairs={{0,1},{1,0},{2,3},{3,2},{4,5},{5,4},{6,7},{7,6},{8,9},{9,8},{10,11... | collective-permute-start | bytes 3932168 | tf_op jit(solution)/shard_map/ppermute | solution.py:35
  94.5 16.5 %all-to-all-done.2.parts_ref = bf16[16,320,128]{2,1,0:T(8,128)(2,1)S(1)} async-done(((bf16[16,320,128]{2,1,0:T(8,128)(2,1)}), bf16[16,320,128]{2,1,0:T(8,128)(2,1)S(1)}, u32[]{:S(2)}, u32[]{:S(2)}) %all-to-all-start.2) | async-done | bytes 1310752 | tf_op jit(solution)/shard_map/all_to_all | solution.py:365
  111.0 0.2 plane_sum.1
  111.2 2.5 %collective-permute-start.4 = (bf16[8,24,128]{2,1,0:T(8,128)(2,1)S(1)}, bf16[8,24,128]{2,1,0:T(8,128)(2,1)S(1)}, u32[]{:S(2)}, u32[]{:S(2)}) collective-permute-start(bf16[8,24,128]{2,1,0:T(8,128)(2,1)S(1)} %get-tuple-element.52), channel_id=1, source_target_pairs={{0,2},{1,3},{2,0},{3,1},{4,6},{5,7},{6,4},{7,5},{8,10},{9,11},{10,... | collective-permute-start | bytes 147464 | tf_op jit(solution)/shard_map/ppermute | solution.py:35
  113.7 3.5 %collective-permute-done.4 = bf16[8,24,128]{2,1,0:T(8,128)(2,1)S(1)} collective-permute-done((bf16[8,24,128]{2,1,0:T(8,128)(2,1)S(1)}, bf16[8,24,128]{2,1,0:T(8,128)(2,1)S(1)}, u32[]{:S(2)}, u32[]{:S(2)}) %collective-permute-start.4) | collective-permute-done | bytes 49184 | tf_op jit(solution)/shard_map/ppermute | solution.py:35
  117.2 0.7 pad_maximum_fusion
  117.8 11.3 %all-to-all-start.3 = ((bf16[16,24,128]{2,1,0:T(8,128)(2,1)}), bf16[16,24,128]{2,1,0:T(8,128)(2,1)S(1)}, u32[]{:S(2)}, u32[]{:S(2)}) async-start(bf16[16,24,128]{2,1,0:T(8,128)(2,1)} %pad_maximum_fusion), calls=%async_computation.3 | async-start | bytes 196608 | tf_op jit(solution)/shard_map/all_to_all | solution.py:382
  129.2 4.3 %project_back.1 = bf16[128,2560]{1,0:T(8,128)(2,1)} custom-call(s32[1]{0:T(128)} %bitcast.3.core_ref, bf16[128,512]{1,0:T(8,128)(2,1)S(1)} %own_rows.1.rows_ref, bf16[16,320,128]{2,1,0:T(8,128)(2,1)} %get-tuple-element.53.own_ref, bf16[16,320,128]{2,1,0:T(8,128)(2,1)S(1)} %collective-permute-done.5.other_ref), custom_call_target="tpu_custom_call" | custom-call | tf_op jit(solution)/shard_map/project_back/pallas_call | solution.py:348
  133.4 20.3 %all-to-all-done.3 = bf16[16,24,128]{2,1,0:T(8,128)(2,1)S(1)} async-done(((bf16[16,24,128]{2,1,0:T(8,128)(2,1)}), bf16[16,24,128]{2,1,0:T(8,128)(2,1)S(1)}, u32[]{:S(2)}, u32[]{:S(2)}) %all-to-all-start.3) | async-done | bytes 98336 | tf_op jit(solution)/shard_map/all_to_all | solution.py:382
  153.8 12.3 %all_to_all.24.pieces_ref = bf16[16,24,128]{2,1,0:T(8,128)(2,1)} all-to-all(bf16[16,24,128]{2,1,0:T(8,128)(2,1)S(1)} %broadcast_in_dim.8), channel_id=1, replica_groups={{0,32,64,96,128,160,192,224,256,288,320,352,384,416,448,480},{512,544,5..., dimensions={0} | all-to-all | bytes 196608 | tf_op jit(solution)/shard_map/all_to_all | solution.py:365
  166.1 1.5 join.1
  (22 shorter events, 0.2 us)
Async XLA Ops:
  0.6 46.5 %copy-start.5 = (s32[128]{0:T(128)S(1)}, s32[128]{0:T(128)}, u32[]{:S(2)}) copy-start(s32[128]{0:T(128)} %param.15) | copy-start | bytes 1540
  2.8 44.5 %all-to-all-start.1 = ((bf16[16,24,128]{2,1,0:T(8,128)(2,1)}), bf16[16,24,128]{2,1,0:T(8,128)(2,1)S(1)}, u32[]{:S(2)}, u32[]{:S(2)}) async-start(bf16[16,24,128]{2,1,0:T(8,128)(2,1)} %broadcast_in_dim.7), calls=%async_computation.1 | async-start | bytes 196608 | tf_op jit(solution)/shard_map/all_to_all | solution.py:371
  29.1 19.9 %copy-start = (bf16[192,2560]{1,0:T(8,128)(2,1)S(1)}, bf16[192,2560]{1,0:T(8,128)(2,1)}, u32[]{:S(2)}) copy-start(bf16[192,2560]{1,0:T(8,128)(2,1)} %q_ref.1) | copy-start | bytes 2949124
  29.1 19.9 %copy-start.1 = (bf16[128,2560]{1,0:T(8,128)(2,1)S(1)}, bf16[128,2560]{1,0:T(8,128)(2,1)}, u32[]{:S(2)}) copy-start(bf16[128,2560]{1,0:T(8,128)(2,1)} %act_ref.1) | copy-start | bytes 1966084
  29.1 19.8 %copy-start.2 = (bf16[192,512]{1,0:T(8,128)(2,1)S(1)}, bf16[192,512]{1,0:T(8,128)(2,1)}, u32[]{:S(2)}) copy-start(bf16[192,512]{1,0:T(8,128)(2,1)} %k_ref.1) | copy-start | bytes 589828
  29.1 19.8 %copy-start.4 = (s32[128]{0:T(128)S(1)}, s32[128]{0:T(128)}, u32[]{:S(2)}) copy-start(s32[128]{0:T(128)} %param.14) | copy-start | bytes 1540
  32.5 45.4 %collective-permute-start.2 = (bf16[16,3712]{1,0:T(8,128)(2,1)S(1)}, bf16[16,3712]{1,0:T(8,128)(2,1)S(1)}, u32[]{:S(2)}, u32[]{:S(2)}) collective-permute-start(bf16[16,3712]{1,0:T(8,128)(2,1)S(1)} %get-tuple-element.48), channel_id=1, source_target_pairs={{0,512},{32,544},{64,576},{96,608},{128,640},{160,672},{192,704},{... | collective-permute-start | bytes 356360 | tf_op jit(solution)/shard_map/ppermute | solution.py:35
  49.0 27.8 %all-to-all-start = ((bf16[16,320,128]{2,1,0:T(8,128)(2,1)}), bf16[16,320,128]{2,1,0:T(8,128)(2,1)S(1)}, u32[]{:S(2)}, u32[]{:S(2)}) async-start(bf16[16,320,128]{2,1,0:T(8,128)(2,1)} %get-tuple-element.23), calls=%async_computation | async-start | bytes 2621440 | tf_op jit(solution)/shard_map/cond/branch_1_fun/all_to_all | solution.py:365
  56.5 21.4 %collective-permute-start.1 = (bf16[128,2560]{1,0:T(8,128)(2,1)S(1)}, bf16[128,2560]{1,0:T(8,128)(2,1)}, u32[]{:S(2)}, u32[]{:S(2)}) collective-permute-start(bf16[128,2560]{1,0:T(8,128)(2,1)S(1)} %get-tuple-element.29), channel_id=1, source_target_pairs={{0,1},{1,0},{2,3},{3,2},{4,5},{5,4},{6,7},{7,6},{8,9},{9,8},{10,11... | collective-permute-start | bytes 1966088 | tf_op jit(solution)/shard_map/cond/branch_1_fun/ppermute | solution.py:35
  58.4 16.8 %collective-permute-start = (bf16[16,3712]{1,0:T(8,128)(2,1)}, bf16[16,3712]{1,0:T(8,128)(2,1)}, u32[]{:S(2)}, u32[]{:S(2)}) collective-permute-start(bf16[16,3712]{1,0:T(8,128)(2,1)} %get-tuple-element.24.behind_ref), channel_id=1, source_target_pairs={{0,256},{32,288},{64,320},{96,352},{128,384},{160,416},{192,448},{... | collective-permute-start | bytes 356360 | tf_op jit(solution)/shard_map/cond/branch_1_fun/ppermute | solution.py:35
  76.8 1.1 copy-start.3
  79.2 3.2 %collective-permute-start.3 = (bf16[128,512]{1,0:T(8,128)(2,1)S(1)}, bf16[128,512]{1,0:T(8,128)(2,1)S(1)}, u32[]{:S(2)}, u32[]{:S(2)}) collective-permute-start(bf16[128,512]{1,0:T(8,128)(2,1)S(1)} %own_rows.1.rows_ref), channel_id=1, source_target_pairs={{0,1},{1,0},{2,3},{3,2},{4,5},{5,4},{6,7},{7,6},{8,9},{9,8},{10,11... | collective-permute-start | bytes 393224 | tf_op jit(solution)/shard_map/ppermute | solution.py:35
  86.6 24.4 %all-to-all-start.2 = ((bf16[16,320,128]{2,1,0:T(8,128)(2,1)}), bf16[16,320,128]{2,1,0:T(8,128)(2,1)S(1)}, u32[]{:S(2)}, u32[]{:S(2)}) async-start(bf16[16,320,128]{2,1,0:T(8,128)(2,1)} %gradient_pieces.1), calls=%async_computation.2 | async-start | bytes 2621440 | tf_op jit(solution)/shard_map/all_to_all | solution.py:365
  92.5 36.6 %collective-permute-start.5 = (bf16[16,320,128]{2,1,0:T(8,128)(2,1)}, bf16[16,320,128]{2,1,0:T(8,128)(2,1)S(1)}, u32[]{:S(2)}, u32[]{:S(2)}) collective-permute-start(bf16[16,320,128]{2,1,0:T(8,128)(2,1)} %get-tuple-element.53.own_ref), channel_id=1, source_target_pairs={{0,1},{1,0},{2,3},{3,2},{4,5},{5,4},{6,7},{7,6},{8,9},{9,8},{10,11... | collective-permute-start | bytes 3932168 | tf_op jit(solution)/shard_map/ppermute | solution.py:35
  111.2 6.0 %collective-permute-start.4 = (bf16[8,24,128]{2,1,0:T(8,128)(2,1)S(1)}, bf16[8,24,128]{2,1,0:T(8,128)(2,1)S(1)}, u32[]{:S(2)}, u32[]{:S(2)}) collective-permute-start(bf16[8,24,128]{2,1,0:T(8,128)(2,1)S(1)} %get-tuple-element.52), channel_id=1, source_target_pairs={{0,2},{1,3},{2,0},{3,1},{4,6},{5,7},{6,4},{7,5},{8,10},{9,11},{10,... | collective-permute-start | bytes 147464 | tf_op jit(solution)/shard_map/ppermute | solution.py:35
  117.8 35.9 %all-to-all-start.3 = ((bf16[16,24,128]{2,1,0:T(8,128)(2,1)}), bf16[16,24,128]{2,1,0:T(8,128)(2,1)S(1)}, u32[]{:S(2)}, u32[]{:S(2)}) async-start(bf16[16,24,128]{2,1,0:T(8,128)(2,1)} %pad_maximum_fusion), calls=%async_computation.3 | async-start | bytes 196608 | tf_op jit(solution)/shard_map/all_to_all | solution.py:382

commit v6 on v5

--- a/solution.py
+++ b/solution.py
@@ -106,8 +106,7 @@
     return jnp.concatenate(heads, axis=1).astype(BF16)
 
 
-def attend_kernel(col_ref, row_ref, q_ref, k_ref, c_ref, behind_ref, out_ref):
-    del behind_ref
+def attend_kernel(col_ref, row_ref, q_ref, k_ref, c_ref, out_ref):
     tok = q_ref.shape[0]
     query = jnp.concatenate([q_ref[:, g * HD : (g + 1) * HD] for g in range(GROUP)], axis=0)
     context = jnp.concatenate([c_ref[:, g * HD : (g + 1) * HD] for g in range(GROUP)], axis=0)
@@ -120,7 +119,7 @@
     out_ref[...] = jnp.dot(probs, context, preferred_element_type=F32).astype(BF16)
 
 
-def attend(queries, key_rows, context_grad, segment, behind):
+def attend(queries, key_rows, context_grad, segment):
     tok = segment.shape[0]
     wide = pl.BlockSpec((tok, GROUP * HD), lambda h: (0, h))
     thin = pl.BlockSpec((tok, HD), lambda h: (0, h))
@@ -133,12 +132,11 @@
             wide,
             thin,
             wide,
-            pl.BlockSpec(memory_space=pl.ANY),
         ],
         out_specs=thin,
         out_shape=jax.ShapeDtypeStruct((tok, WIDTH), BF16),
         name="attend",
-    )(segment.reshape(tok, 1), segment.reshape(1, tok), queries, key_rows, context_grad, behind)
+    )(segment.reshape(tok, 1), segment.reshape(1, tok), queries, key_rows, context_grad)
 
 
 def rows_kernel(block, slot_ref, main_ref, first_ref, second_ref, out_ref):
@@ -192,7 +190,7 @@
 
 def gradient_pieces(core, rows, other_rows, activations, other_activations):
     tok, features = activations.shape
-    steps = 4
+    steps = 2
     held = pl.BlockSpec((tok, WIDTH), lambda m, *_: (0, 0))
     columns = pl.BlockSpec((tok, features // steps), lambda m, *_: (0, m))
     return pl.pallas_call(
@@ -270,11 +268,28 @@
     )(odd, pieces)
 
 
+def cut_kernel(place_ref, rows_ref, tile_ref, out_ref):
+    del place_ref
+    for at in range(out_ref.shape[0]):
+        out_ref[at, :16, :] = rows_ref[...]
+        out_ref[at, 16:, :] = tile_ref[...]
+
+
 def cut_out(shard, place):
-    cut, k = place // CUTS, place % CUTS
-    rows = lax.dynamic_slice(shard, (16 * cut, HD * k), (16, HD))
-    tile = lax.dynamic_slice(shard, (16 * CUTS + 8 * (cut // 2), HD * k), (8, HD))
-    return jnp.concatenate([rows, tile], axis=0)
+    return pl.pallas_call(
+        cut_kernel,
+        grid_spec=pltpu.PrefetchScalarGridSpec(
+            num_scalar_prefetch=1,
+            grid=(1,),
+            in_specs=[
+                pl.BlockSpec((16, HD), lambda i, p: (p[0] // CUTS, p[0] % CUTS)),
+                pl.BlockSpec((8, HD), lambda i, p: (2 * CUTS + p[0] // (2 * CUTS), p[0] % CUTS)),
+            ],
+            out_specs=pl.BlockSpec((DEPTH, ROWS, HD), lambda i, p: (0, 0, 0)),
+        ),
+        out_shape=jax.ShapeDtypeStruct((DEPTH, ROWS, HD), BF16),
+        name="cut_out",
+    )(place, shard, shard)
 
 
 def spread_kernel(place_ref, pieces_ref, out_ref, paired):
@@ -365,9 +380,8 @@
     return lax.all_to_all(pieces, "dp", 0, 0, axis_index_groups=groups)
 
 
-def depth_gather(piece):
+def depth_gather(copies):
     groups = [[2 * ((z + DEPTH // 2) % DEPTH) + core for z in range(DEPTH)] for core in range(2)]
-    copies = jnp.broadcast_to(piece[None], (DEPTH, *piece.shape))
     return lax.all_to_all(copies, "fsdp", 0, 0, axis_index_groups=groups)
 
 
@@ -390,21 +404,21 @@
     tok, features = activations.shape
     block = (queries.shape[0] - tok) // SECTIONS
     half = lax.axis_size("dp") // 2
-    place = lax.axis_index("dp") % PLANE
+    place = (lax.axis_index("dp") % PLANE).astype(jnp.int32).reshape(1)
     core = (lax.axis_index("fsdp") % 2).astype(jnp.int32).reshape(1)
     odd = (lax.axis_index("fsdp") // 2 % 2).astype(jnp.int32).reshape(1)
 
     first, second = messages(queries, key_rows, context_grad, tok, block)
     first = swapped(first, "dp", half)
-    copies = spread(place.astype(jnp.int32).reshape(1), depth_gather(cut_out(value_weight, place)))
+    second = swapped(second, "dp", half // 2)
+    copies = spread(place, depth_gather(cut_out(value_weight, place)))
 
     def beside(held):
-        copies, second, _, act = held
-        main = attend(queries, key_rows, context_grad, segment, second)
-        return plane_exchange(copies), swapped(second, "dp", half // 2), main, swapped(act, "fsdp", 1)
-
-    held = (copies, second, jnp.zeros((tok, WIDTH), BF16), activations)
-    own_weight, second, main, other_act = lax.cond(
+        copies, _, act = held
+        return plane_exchange(copies), attend(queries, key_rows, context_grad, segment), swapped(act, "fsdp", 1)
+
+    held = (copies, jnp.zeros((tok, WIDTH), BF16), activations)
+    own_weight, main, other_act = lax.cond(
         lax.axis_index("dp") < lax.axis_size("dp"), beside, lambda held: held, held
     )
     main, own_weight = lax.optimization_barrier((main, own_weight))

time: 169 us -> 167 us (0.988)
  the two profiles are of different devices: /device:TPU:2 before, /device:TPU:32 now
where the time goes in v6:
time: 167 us; the launch traced here: 166 us
  starting transfers between devices  75.2 us (45%)
  waiting for transfers between devices  54.2 us (32%)
  Pallas kernels  20.2 us (12%)
  blocking collectives  12.9 us (8%)
  local copies, waits for them, and re-layouts  1.97 us (1%)
    all_to_all x2, waiting for transfers between devices, plane_exchange(): return lax.all_to_all(pieces, 'dp', 0, 0, axis_index_groups=groups)  32 us
    ppermute x6, starting transfers between devices, swapped(): return lax.ppermute(block, axis, route)  28.9 us
    all_to_all x1, starting transfers between devices, depth_gather(): return lax.all_to_all(copies, 'fsdp', 0, 0, axis_index_groups=groups)  25 us
    all_to_all x1, waiting for transfers between devices, depth_exchange(): return lax.all_to_all(pieces, BOTH, 0, 0, axis_index_groups=groups)  18.3 us
    all_to_all x1, blocking collectives, plane_exchange(): return lax.all_to_all(pieces, 'dp', 0, 0, axis_index_groups=groups)  12.9 us
    all_to_all x1, starting transfers between devices, depth_exchange(): return lax.all_to_all(pieces, BOTH, 0, 0, axis_index_groups=groups)  12.5 us
    all_to_all x2, starting transfers between devices, plane_exchange(): return lax.all_to_all(pieces, 'dp', 0, 0, axis_index_groups=groups)  8.86 us
    pallas_call x1, Pallas kernels, project_back(): pl.pallas_call(project_kernel, grid_spec=pltpu.PrefetchScalarGridSpec(num...  4.26 us
  transfers between devices with their start and end apart: 10, of which 5 were waited for; matrix products, arithmetic and copies ran while one was open for 2% of the time, Pallas kernels for 8%

profile of v6, /device:TPU:32, one launch (start us, length us, event | category | flops | bytes accessed | tf_op | source)
XLA Modules:
  0.0 166.0 jit_solution(23612427619086193)
XLA Ops:
  0.7 1.4 cut_out.1
  2.0 25.0 %all-to-all-start.1 = ((bf16[16,24,128]{2,1,0:T(8,128)(2,1)}), bf16[16,24,128]{2,1,0:T(8,128)(2,1)S(1)}, u32[]{:S(2)}, u32[]{:S(2)}) async-start(bf16[16,24,128]{2,1,0:T(8,128)(2,1)} %cut_out.1), calls=%async_computation.1 | async-start | bytes 196608 | tf_op jit(solution)/shard_map/all_to_all | solution.py:385
  27.0 0.0 copy-start.1
  27.0 0.0 copy-start.2
  27.1 2.7 %messages.1 = (bf16[16,3712]{1,0:T(8,128)(2,1)S(1)}, bf16[16,3712]{1,0:T(8,128)(2,1)S(1)}) custom-call(bf16[192,2560]{1,0:T(8,128)(2,1)} %q_ref.1, bf16[192,512]{1,0:T(8,128)(2,1)} %k_ref.1, bf16[192,2560]{1,0:T(8,128)(2,1)} %c_ref.1), custom_call_target="tpu_custom_call" | custom-call | tf_op jit(solution)/shard_map/messages/pallas_call | solution.py:79
  29.7 14.7 %collective-permute-start.1 = (bf16[16,3712]{1,0:T(8,128)(2,1)S(1)}, bf16[16,3712]{1,0:T(8,128)(2,1)S(1)}, u32[]{:S(2)}, u32[]{:S(2)}) collective-permute-start(bf16[16,3712]{1,0:T(8,128)(2,1)S(1)} %get-tuple-element.40), channel_id=1, source_target_pairs={{0,512},{32,544},{64,576},{96,608},{128,640},{160,672},{192,704},{... | collective-permute-start | bytes 356360 | tf_op jit(solution)/shard_map/ppermute | solution.py:35
  44.4 4.9 %collective-permute-start.2 = (bf16[16,3712]{1,0:T(8,128)(2,1)S(1)}, bf16[16,3712]{1,0:T(8,128)(2,1)S(1)}, u32[]{:S(2)}, u32[]{:S(2)}) collective-permute-start(bf16[16,3712]{1,0:T(8,128)(2,1)S(1)} %get-tuple-element.41), channel_id=1, source_target_pairs={{0,256},{32,288},{64,320},{96,352},{128,384},{160,416},{192,448},{... | collective-permute-start | bytes 356360 | tf_op jit(solution)/shard_map/ppermute | solution.py:35
  49.3 0.1 copy.11.slot_ref
  49.5 1.7 %spread.1 = bf16[16,320,128]{2,1,0:T(8,128)(2,1)} custom-call(s32[1]{0:T(128)} %bitcast.5.place_ref, bf16[16,24,128]{2,1,0:T(8,128)(2,1)S(1)} %all-to-all-done.1.pieces_ref), custom_call_target="tpu_custom_call" | custom-call | tf_op jit(solution)/shard_map/spread/pallas_call | solution.py:316
  51.2 25.6 %conditional.1 = (bf16[16,320,128]{2,1,0:T(8,128)(2,1)}, bf16[128,512]{1,0:T(8,128)(2,1)}, bf16[128,2560]{1,0:T(8,128)(2,1)}) conditional(s32[]{:T(128)} %convert_element_type.14, (bf16[16,320,128]{2,1,0:T(8,128)(2,1)}, bf16[128,2560]{1,0:T(8,128)(2,1)S(1)}) %tuple.26, (bf16[16,320,128]{2,1,0:T(8,128)(2,1)}, s32[128]{0:T(128)S(1)}, ...), branch_computations={%region_0.1_spmd, %region_1.2_spmd} | conditional | bytes 9176160 | solution.py:421
  51.2 5.2 %all-to-all-start = ((bf16[16,320,128]{2,1,0:T(8,128)(2,1)}), bf16[16,320,128]{2,1,0:T(8,128)(2,1)S(1)}, u32[]{:S(2)}, u32[]{:S(2)}) async-start(bf16[16,320,128]{2,1,0:T(8,128)(2,1)} %get-tuple-element.18), calls=%async_computation | async-start | bytes 2621440 | tf_op jit(solution)/shard_map/cond/branch_1_fun/all_to_all | solution.py:380
  56.3 1.9 %collective-permute-start = (bf16[128,2560]{1,0:T(8,128)(2,1)S(1)}, bf16[128,2560]{1,0:T(8,128)(2,1)}, u32[]{:S(2)}, u32[]{:S(2)}) collective-permute-start(bf16[128,2560]{1,0:T(8,128)(2,1)S(1)} %get-tuple-element.23), channel_id=1, source_target_pairs={{0,1},{1,0},{2,3},{3,2},{4,5},{5,4},{6,7},{7,6},{8,9},{9,8},{10,11... | collective-permute-start | bytes 1966088 | tf_op jit(solution)/shard_map/cond/branch_1_fun/ppermute | solution.py:35
  58.3 0.7 copy.10.col_ref
  59.0 4.0 %attend.1 = bf16[128,512]{1,0:T(8,128)(2,1)} custom-call(s32[128,1]{1,0:T(8,128)} %copy.10.col_ref, s32[1,128]{1,0:T(1,128)S(1)} %bitcast.7, bf16[192,2560]{1,0:T(8,128)(2,1)S(1)} %get-tuple-element.20.q_ref, bf16[192,512]{1,0:T(8,128)(2,1)} %get-tuple-element.21.k_ref, bf16[192,2560]{1,0:T(8,128)(2,1)} %get-tuple-element.22.c_ref), custom_call_target="tpu_custom_call" | custom-call | tf_op jit(solution)/shard_map/cond/branch_1_fun/attend/pallas_call | solution.py:126
  63.0 12.6 %all-to-all-done = bf16[16,320,128]{2,1,0:T(8,128)(2,1)S(1)} async-done(((bf16[16,320,128]{2,1,0:T(8,128)(2,1)}), bf16[16,320,128]{2,1,0:T(8,128)(2,1)S(1)}, u32[]{:S(2)}, u32[]{:S(2)}) %all-to-all-start) | async-done | bytes 1310752 | tf_op jit(solution)/shard_map/cond/branch_1_fun/all_to_all | solution.py:380
  75.6 1.1 copy.15
  76.7 1.4 own_rows.1.rows_ref
  78.1 1.9 %collective-permute-start.3 = (bf16[128,512]{1,0:T(8,128)(2,1)S(1)}, bf16[128,512]{1,0:T(8,128)(2,1)S(1)}, u32[]{:S(2)}, u32[]{:S(2)}) collective-permute-start(bf16[128,512]{1,0:T(8,128)(2,1)S(1)} %own_rows.1.rows_ref), channel_id=1, source_target_pairs={{0,1},{1,0},{2,3},{3,2},{4,5},{5,4},{6,7},{7,6},{8,9},{9,8},{10,11... | collective-permute-start | bytes 393224 | tf_op jit(solution)/shard_map/ppermute | solution.py:35
  80.0 1.3 collective-permute-done.3.other_rows_ref
  81.3 3.1 %gradient_pieces.1 = bf16[16,320,128]{2,1,0:T(8,128)(2,1)} custom-call(s32[1]{0:T(128)} %bitcast.3.core_ref, bf16[128,512]{1,0:T(8,128)(2,1)S(1)} %own_rows.1.rows_ref, bf16[128,512]{1,0:T(8,128)(2,1)S(1)} %collective-permute-done.3.other_rows_ref, bf16[128,2560]{1,0:T(8,128)(2,1)S(1)} %copy-done.1, bf16[128,2560]{1,0:T(8,128)(2,1)} %get-tuple-element.42.other_act_ref), custom_call_target="tpu_custom_call" | custom-call | tf_op jit(solution)/shard_map/gradient_pieces/pallas_call | solution.py:196
  84.4 3.7 %all-to-all-start.2 = ((bf16[16,320,128]{2,1,0:T(8,128)(2,1)}), bf16[16,320,128]{2,1,0:T(8,128)(2,1)S(1)}, u32[]{:S(2)}, u32[]{:S(2)}) async-start(bf16[16,320,128]{2,1,0:T(8,128)(2,1)} %gradient_pieces.1), calls=%async_computation.2 | async-start | bytes 2621440 | tf_op jit(solution)/shard_map/all_to_all | solution.py:380
  88.1 2.1 %collective-permute-start.5 = (bf16[16,320,128]{2,1,0:T(8,128)(2,1)}, bf16[16,320,128]{2,1,0:T(8,128)(2,1)S(1)}, u32[]{:S(2)}, u32[]{:S(2)}) collective-permute-start(bf16[16,320,128]{2,1,0:T(8,128)(2,1)} %get-tuple-element.45.own_ref), channel_id=1, source_target_pairs={{0,1},{1,0},{2,3},{3,2},{4,5},{5,4},{6,7},{7,6},{8,9},{9,8},{10,11... | collective-permute-start | bytes 3932168 | tf_op jit(solution)/shard_map/ppermute | solution.py:35
  90.2 19.4 %all-to-all-done.2.parts_ref = bf16[16,320,128]{2,1,0:T(8,128)(2,1)S(1)} async-done(((bf16[16,320,128]{2,1,0:T(8,128)(2,1)}), bf16[16,320,128]{2,1,0:T(8,128)(2,1)S(1)}, u32[]{:S(2)}, u32[]{:S(2)}) %all-to-all-start.2) | async-done | bytes 1310752 | tf_op jit(solution)/shard_map/all_to_all | solution.py:380
  109.6 0.2 plane_sum.1
  109.8 3.4 %collective-permute-start.4 = (bf16[8,24,128]{2,1,0:T(8,128)(2,1)S(1)}, bf16[8,24,128]{2,1,0:T(8,128)(2,1)S(1)}, u32[]{:S(2)}, u32[]{:S(2)}) collective-permute-start(bf16[8,24,128]{2,1,0:T(8,128)(2,1)S(1)} %get-tuple-element.44), channel_id=1, source_target_pairs={{0,2},{1,3},{2,0},{3,1},{4,6},{5,7},{6,4},{7,5},{8,10},{9,11},{10,... | collective-permute-start | bytes 147464 | tf_op jit(solution)/shard_map/ppermute | solution.py:35
  113.2 2.6 %collective-permute-done.4 = bf16[8,24,128]{2,1,0:T(8,128)(2,1)S(1)} collective-permute-done((bf16[8,24,128]{2,1,0:T(8,128)(2,1)S(1)}, bf16[8,24,128]{2,1,0:T(8,128)(2,1)S(1)}, u32[]{:S(2)}, u32[]{:S(2)}) %collective-permute-start.4) | collective-permute-done | bytes 49184 | tf_op jit(solution)/shard_map/ppermute | solution.py:35
  115.8 0.6 pad_maximum_fusion
  116.5 12.5 %all-to-all-start.3 = ((bf16[16,24,128]{2,1,0:T(8,128)(2,1)}), bf16[16,24,128]{2,1,0:T(8,128)(2,1)S(1)}, u32[]{:S(2)}, u32[]{:S(2)}) async-start(bf16[16,24,128]{2,1,0:T(8,128)(2,1)} %pad_maximum_fusion), calls=%async_computation.3 | async-start | bytes 196608 | tf_op jit(solution)/shard_map/all_to_all | solution.py:396
  129.0 4.3 %project_back.1 = bf16[128,2560]{1,0:T(8,128)(2,1)} custom-call(s32[1]{0:T(128)} %bitcast.3.core_ref, bf16[128,512]{1,0:T(8,128)(2,1)S(1)} %own_rows.1.rows_ref, bf16[16,320,128]{2,1,0:T(8,128)(2,1)} %get-tuple-element.45.own_ref, bf16[16,320,128]{2,1,0:T(8,128)(2,1)S(1)} %collective-permute-done.5.other_ref), custom_call_target="tpu_custom_call" | custom-call | tf_op jit(solution)/shard_map/project_back/pallas_call | solution.py:363
  133.3 18.3 %all-to-all-done.3 = bf16[16,24,128]{2,1,0:T(8,128)(2,1)S(1)} async-done(((bf16[16,24,128]{2,1,0:T(8,128)(2,1)}), bf16[16,24,128]{2,1,0:T(8,128)(2,1)S(1)}, u32[]{:S(2)}, u32[]{:S(2)}) %all-to-all-start.3) | async-done | bytes 98336 | tf_op jit(solution)/shard_map/all_to_all | solution.py:396
  151.6 12.9 %all_to_all.24.pieces_ref = bf16[16,24,128]{2,1,0:T(8,128)(2,1)} all-to-all(bf16[16,24,128]{2,1,0:T(8,128)(2,1)S(1)} %broadcast_in_dim.5), channel_id=1, replica_groups={{0,32,64,96,128,160,192,224,256,288,320,352,384,416,448,480},{512,544,5..., dimensions={0} | all-to-all | bytes 196608 | tf_op jit(solution)/shard_map/all_to_all | solution.py:380
  164.4 1.5 join.1
  (14 shorter events, 0.1 us)
Async XLA Ops:
  0.6 48.7 %copy-start.3 = (s32[128]{0:T(128)S(1)}, s32[128]{0:T(128)}, u32[]{:S(2)}) copy-start(s32[128]{0:T(128)} %param.15) | copy-start | bytes 1540
  2.0 47.4 %all-to-all-start.1 = ((bf16[16,24,128]{2,1,0:T(8,128)(2,1)}), bf16[16,24,128]{2,1,0:T(8,128)(2,1)S(1)}, u32[]{:S(2)}, u32[]{:S(2)}) async-start(bf16[16,24,128]{2,1,0:T(8,128)(2,1)} %cut_out.1), calls=%async_computation.1 | async-start | bytes 196608 | tf_op jit(solution)/shard_map/all_to_all | solution.py:385
  27.0 24.1 %copy-start = (bf16[192,2560]{1,0:T(8,128)(2,1)S(1)}, bf16[192,2560]{1,0:T(8,128)(2,1)}, u32[]{:S(2)}) copy-start(bf16[192,2560]{1,0:T(8,128)(2,1)} %q_ref.1) | copy-start | bytes 2949124
  27.0 24.1 %copy-start.1 = (bf16[128,2560]{1,0:T(8,128)(2,1)S(1)}, bf16[128,2560]{1,0:T(8,128)(2,1)}, u32[]{:S(2)}) copy-start(bf16[128,2560]{1,0:T(8,128)(2,1)} %act_ref.1) | copy-start | bytes 1966084
  27.0 24.1 %copy-start.2 = (s32[128]{0:T(128)S(1)}, s32[128]{0:T(128)}, u32[]{:S(2)}) copy-start(s32[128]{0:T(128)} %param.14) | copy-start | bytes 1540
  29.7 47.0 %collective-permute-start.1 = (bf16[16,3712]{1,0:T(8,128)(2,1)S(1)}, bf16[16,3712]{1,0:T(8,128)(2,1)S(1)}, u32[]{:S(2)}, u32[]{:S(2)}) collective-permute-start(bf16[16,3712]{1,0:T(8,128)(2,1)S(1)} %get-tuple-element.40), channel_id=1, source_target_pairs={{0,512},{32,544},{64,576},{96,608},{128,640},{160,672},{192,704},{... | collective-permute-start | bytes 356360 | tf_op jit(solution)/shard_map/ppermute | solution.py:35
  44.4 32.3 %collective-permute-start.2 = (bf16[16,3712]{1,0:T(8,128)(2,1)S(1)}, bf16[16,3712]{1,0:T(8,128)(2,1)S(1)}, u32[]{:S(2)}, u32[]{:S(2)}) collective-permute-start(bf16[16,3712]{1,0:T(8,128)(2,1)S(1)} %get-tuple-element.41), channel_id=1, source_target_pairs={{0,256},{32,288},{64,320},{96,352},{128,384},{160,416},{192,448},{... | collective-permute-start | bytes 356360 | tf_op jit(solution)/shard_map/ppermute | solution.py:35
  51.2 24.5 %all-to-all-start = ((bf16[16,320,128]{2,1,0:T(8,128)(2,1)}), bf16[16,320,128]{2,1,0:T(8,128)(2,1)S(1)}, u32[]{:S(2)}, u32[]{:S(2)}) async-start(bf16[16,320,128]{2,1,0:T(8,128)(2,1)} %get-tuple-element.18), calls=%async_computation | async-start | bytes 2621440 | tf_op jit(solution)/shard_map/cond/branch_1_fun/all_to_all | solution.py:380
  56.3 20.4 %collective-permute-start = (bf16[128,2560]{1,0:T(8,128)(2,1)S(1)}, bf16[128,2560]{1,0:T(8,128)(2,1)}, u32[]{:S(2)}, u32[]{:S(2)}) collective-permute-start(bf16[128,2560]{1,0:T(8,128)(2,1)S(1)} %get-tuple-element.23), channel_id=1, source_target_pairs={{0,1},{1,0},{2,3},{3,2},{4,5},{5,4},{6,7},{7,6},{8,9},{9,8},{10,11... | collective-permute-start | bytes 1966088 | tf_op jit(solution)/shard_map/cond/branch_1_fun/ppermute | solution.py:35
  78.1 3.2 %collective-permute-start.3 = (bf16[128,512]{1,0:T(8,128)(2,1)S(1)}, bf16[128,512]{1,0:T(8,128)(2,1)S(1)}, u32[]{:S(2)}, u32[]{:S(2)}) collective-permute-start(bf16[128,512]{1,0:T(8,128)(2,1)S(1)} %own_rows.1.rows_ref), channel_id=1, source_target_pairs={{0,1},{1,0},{2,3},{3,2},{4,5},{5,4},{6,7},{7,6},{8,9},{9,8},{10,11... | collective-permute-start | bytes 393224 | tf_op jit(solution)/shard_map/ppermute | solution.py:35
  84.4 25.2 %all-to-all-start.2 = ((bf16[16,320,128]{2,1,0:T(8,128)(2,1)}), bf16[16,320,128]{2,1,0:T(8,128)(2,1)S(1)}, u32[]{:S(2)}, u32[]{:S(2)}) async-start(bf16[16,320,128]{2,1,0:T(8,128)(2,1)} %gradient_pieces.1), calls=%async_computation.2 | async-start | bytes 2621440 | tf_op jit(solution)/shard_map/all_to_all | solution.py:380
  88.1 40.9 %collective-permute-start.5 = (bf16[16,320,128]{2,1,0:T(8,128)(2,1)}, bf16[16,320,128]{2,1,0:T(8,128)(2,1)S(1)}, u32[]{:S(2)}, u32[]{:S(2)}) collective-permute-start(bf16[16,320,128]{2,1,0:T(8,128)(2,1)} %get-tuple-element.45.own_ref), channel_id=1, source_target_pairs={{0,1},{1,0},{2,3},{3,2},{4,5},{5,4},{6,7},{7,6},{8,9},{9,8},{10,11... | collective-permute-start | bytes 3932168 | tf_op jit(solution)/shard_map/ppermute | solution.py:35
  109.8 6.0 %collective-permute-start.4 = (bf16[8,24,128]{2,1,0:T(8,128)(2,1)S(1)}, bf16[8,24,128]{2,1,0:T(8,128)(2,1)S(1)}, u32[]{:S(2)}, u32[]{:S(2)}) collective-permute-start(bf16[8,24,128]{2,1,0:T(8,128)(2,1)S(1)} %get-tuple-element.44), channel_id=1, source_target_pairs={{0,2},{1,3},{2,0},{3,1},{4,6},{5,7},{6,4},{7,5},{8,10},{9,11},{10,... | collective-permute-start | bytes 147464 | tf_op jit(solution)/shard_map/ppermute | solution.py:35
  116.5 35.1 %all-to-all-start.3 = ((bf16[16,24,128]{2,1,0:T(8,128)(2,1)}), bf16[16,24,128]{2,1,0:T(8,128)(2,1)S(1)}, u32[]{:S(2)}, u32[]{:S(2)}) async-start(bf16[16,24,128]{2,1,0:T(8,128)(2,1)} %pad_maximum_fusion), calls=%async_computation.3 | async-start | bytes 196608 | tf_op jit(solution)/shard_map/all_to_all | solution.py:396

commit v7 on v6

--- a/solution.py
+++ b/solution.py
@@ -388,7 +388,7 @@
 def depth_exchange(pieces):
     count = 2 * DEPTH
     groups = [
-        [(half * PLANE + at) * count + 2 * z + core for half in range(2) for z in range(odd, DEPTH, 2)]
+        [(half * PLANE + at) * count + 2 * z + core for half in (1, 0) for z in range(odd, DEPTH, 2)]
         for at in range(PLANE)
         for odd in range(2)
         for core in range(2)

time: 167 us -> 159 us (0.952)
  the two profiles are of different devices: /device:TPU:32 before, /device:TPU:2 now
where the time goes in v7:
time: 159 us; the launch traced here: 158 us
  starting transfers between devices  87.1 us (55%)
  waiting for transfers between devices  34.7 us (22%)
  Pallas kernels  20.2 us (13%)
  blocking collectives  12.9 us (8%)
  local copies, waits for them, and re-layouts  1.97 us (1%)
    all_to_all x2, waiting for transfers between devices, plane_exchange(): return lax.all_to_all(pieces, 'dp', 0, 0, axis_index_groups=groups)  27.6 us
    ppermute x6, starting transfers between devices, swapped(): return lax.ppermute(block, axis, route)  26.9 us
    all_to_all x1, starting transfers between devices, depth_gather(): return lax.all_to_all(copies, 'fsdp', 0, 0, axis_index_groups=groups)  26.4 us
    all_to_all x1, starting transfers between devices, depth_exchange(): return lax.all_to_all(pieces, BOTH, 0, 0, axis_index_groups=groups)  21.6 us
    all_to_all x1, blocking collectives, plane_exchange(): return lax.all_to_all(pieces, 'dp', 0, 0, axis_index_groups=groups)  12.9 us
    all_to_all x2, starting transfers between devices, plane_exchange(): return lax.all_to_all(pieces, 'dp', 0, 0, axis_index_groups=groups)  12.2 us
    ppermute x6, waiting for transfers between devices, swapped(): return lax.ppermute(block, axis, route)  4.81 us
    pallas_call x1, Pallas kernels, project_back(): pl.pallas_call(project_kernel, grid_spec=pltpu.PrefetchScalarGridSpec(num...  4.26 us
  transfers between devices with their start and end apart: 10, of which 5 were waited for; matrix products, arithmetic and copies ran while one was open for 2% of the time, Pallas kernels for 8%

profile of v7, /device:TPU:2, one launch (start us, length us, event | category | flops | bytes accessed | tf_op | source)
XLA Modules:
  0.0 158.4 jit_solution(9124489590201946232)
XLA Ops:
  0.7 1.4 cut_out.1
  2.0 26.4 %all-to-all-start.1 = ((bf16[16,24,128]{2,1,0:T(8,128)(2,1)}), bf16[16,24,128]{2,1,0:T(8,128)(2,1)S(1)}, u32[]{:S(2)}, u32[]{:S(2)}) async-start(bf16[16,24,128]{2,1,0:T(8,128)(2,1)} %cut_out.1), calls=%async_computation.1 | async-start | bytes 196608 | tf_op jit(solution)/shard_map/all_to_all | solution.py:385
  28.4 0.0 copy-start.1
  28.4 0.0 copy-start.2
  28.4 2.7 %messages.1 = (bf16[16,3712]{1,0:T(8,128)(2,1)S(1)}, bf16[16,3712]{1,0:T(8,128)(2,1)S(1)}) custom-call(bf16[192,2560]{1,0:T(8,128)(2,1)} %q_ref.1, bf16[192,512]{1,0:T(8,128)(2,1)} %k_ref.1, bf16[192,2560]{1,0:T(8,128)(2,1)} %c_ref.1), custom_call_target="tpu_custom_call" | custom-call | tf_op jit(solution)/shard_map/messages/pallas_call | solution.py:79
  31.1 14.7 %collective-permute-start.1 = (bf16[16,3712]{1,0:T(8,128)(2,1)S(1)}, bf16[16,3712]{1,0:T(8,128)(2,1)S(1)}, u32[]{:S(2)}, u32[]{:S(2)}) collective-permute-start(bf16[16,3712]{1,0:T(8,128)(2,1)S(1)} %get-tuple-element.40), channel_id=1, source_target_pairs={{0,512},{32,544},{64,576},{96,608},{128,640},{160,672},{192,704},{... | collective-permute-start | bytes 356360 | tf_op jit(solution)/shard_map/ppermute | solution.py:35
  45.7 4.0 %collective-permute-start.2 = (bf16[16,3712]{1,0:T(8,128)(2,1)S(1)}, bf16[16,3712]{1,0:T(8,128)(2,1)S(1)}, u32[]{:S(2)}, u32[]{:S(2)}) collective-permute-start(bf16[16,3712]{1,0:T(8,128)(2,1)S(1)} %get-tuple-element.41), channel_id=1, source_target_pairs={{0,256},{32,288},{64,320},{96,352},{128,384},{160,416},{192,448},{... | collective-permute-start | bytes 356360 | tf_op jit(solution)/shard_map/ppermute | solution.py:35
  49.8 0.1 copy.11.slot_ref
  49.9 1.7 %spread.1 = bf16[16,320,128]{2,1,0:T(8,128)(2,1)} custom-call(s32[1]{0:T(128)} %bitcast.5.place_ref, bf16[16,24,128]{2,1,0:T(8,128)(2,1)S(1)} %all-to-all-done.1.pieces_ref), custom_call_target="tpu_custom_call" | custom-call | tf_op jit(solution)/shard_map/spread/pallas_call | solution.py:316
  51.6 24.8 %conditional.1 = (bf16[16,320,128]{2,1,0:T(8,128)(2,1)}, bf16[128,512]{1,0:T(8,128)(2,1)}, bf16[128,2560]{1,0:T(8,128)(2,1)}) conditional(s32[]{:T(128)} %convert_element_type.14, (bf16[16,320,128]{2,1,0:T(8,128)(2,1)}, bf16[128,2560]{1,0:T(8,128)(2,1)S(1)}) %tuple.26, (bf16[16,320,128]{2,1,0:T(8,128)(2,1)}, s32[128]{0:T(128)S(1)}, ...), branch_computations={%region_0.1_spmd, %region_1.2_spmd} | conditional | bytes 9176160 | solution.py:421
  51.6 6.5 %all-to-all-start = ((bf16[16,320,128]{2,1,0:T(8,128)(2,1)}), bf16[16,320,128]{2,1,0:T(8,128)(2,1)S(1)}, u32[]{:S(2)}, u32[]{:S(2)}) async-start(bf16[16,320,128]{2,1,0:T(8,128)(2,1)} %get-tuple-element.18), calls=%async_computation | async-start | bytes 2621440 | tf_op jit(solution)/shard_map/cond/branch_1_fun/all_to_all | solution.py:380
  58.1 1.9 %collective-permute-start = (bf16[128,2560]{1,0:T(8,128)(2,1)S(1)}, bf16[128,2560]{1,0:T(8,128)(2,1)}, u32[]{:S(2)}, u32[]{:S(2)}) collective-permute-start(bf16[128,2560]{1,0:T(8,128)(2,1)S(1)} %get-tuple-element.23), channel_id=1, source_target_pairs={{0,1},{1,0},{2,3},{3,2},{4,5},{5,4},{6,7},{7,6},{8,9},{9,8},{10,11... | collective-permute-start | bytes 1966088 | tf_op jit(solution)/shard_map/cond/branch_1_fun/ppermute | solution.py:35
  60.0 0.7 copy.10.col_ref
  60.8 4.0 %attend.1 = bf16[128,512]{1,0:T(8,128)(2,1)} custom-call(s32[128,1]{1,0:T(8,128)} %copy.10.col_ref, s32[1,128]{1,0:T(1,128)S(1)} %bitcast.7, bf16[192,2560]{1,0:T(8,128)(2,1)S(1)} %get-tuple-element.20.q_ref, bf16[192,512]{1,0:T(8,128)(2,1)} %get-tuple-element.21.k_ref, bf16[192,2560]{1,0:T(8,128)(2,1)} %get-tuple-element.22.c_ref), custom_call_target="tpu_custom_call" | custom-call | tf_op jit(solution)/shard_map/cond/branch_1_fun/attend/pallas_call | solution.py:126
  64.8 10.5 %all-to-all-done = bf16[16,320,128]{2,1,0:T(8,128)(2,1)S(1)} async-done(((bf16[16,320,128]{2,1,0:T(8,128)(2,1)}), bf16[16,320,128]{2,1,0:T(8,128)(2,1)S(1)}, u32[]{:S(2)}, u32[]{:S(2)}) %all-to-all-start) | async-done | bytes 1310752 | tf_op jit(solution)/shard_map/cond/branch_1_fun/all_to_all | solution.py:380
  75.3 1.1 copy.15
  76.4 1.4 own_rows.1.rows_ref
  77.8 1.9 %collective-permute-start.3 = (bf16[128,512]{1,0:T(8,128)(2,1)S(1)}, bf16[128,512]{1,0:T(8,128)(2,1)S(1)}, u32[]{:S(2)}, u32[]{:S(2)}) collective-permute-start(bf16[128,512]{1,0:T(8,128)(2,1)S(1)} %own_rows.1.rows_ref), channel_id=1, source_target_pairs={{0,1},{1,0},{2,3},{3,2},{4,5},{5,4},{6,7},{7,6},{8,9},{9,8},{10,11... | collective-permute-start | bytes 393224 | tf_op jit(solution)/shard_map/ppermute | solution.py:35
  79.7 1.3 collective-permute-done.3.other_rows_ref
  81.0 3.1 %gradient_pieces.1 = bf16[16,320,128]{2,1,0:T(8,128)(2,1)} custom-call(s32[1]{0:T(128)} %bitcast.3.core_ref, bf16[128,512]{1,0:T(8,128)(2,1)S(1)} %own_rows.1.rows_ref, bf16[128,512]{1,0:T(8,128)(2,1)S(1)} %collective-permute-done.3.other_rows_ref, bf16[128,2560]{1,0:T(8,128)(2,1)S(1)} %copy-done.1, bf16[128,2560]{1,0:T(8,128)(2,1)} %get-tuple-element.42.other_act_ref), custom_call_target="tpu_custom_call" | custom-call | tf_op jit(solution)/shard_map/gradient_pieces/pallas_call | solution.py:196
  84.1 5.7 %all-to-all-start.2 = ((bf16[16,320,128]{2,1,0:T(8,128)(2,1)}), bf16[16,320,128]{2,1,0:T(8,128)(2,1)S(1)}, u32[]{:S(2)}, u32[]{:S(2)}) async-start(bf16[16,320,128]{2,1,0:T(8,128)(2,1)} %gradient_pieces.1), calls=%async_computation.2 | async-start | bytes 2621440 | tf_op jit(solution)/shard_map/all_to_all | solution.py:380
  89.8 1.9 %collective-permute-start.5 = (bf16[16,320,128]{2,1,0:T(8,128)(2,1)}, bf16[16,320,128]{2,1,0:T(8,128)(2,1)S(1)}, u32[]{:S(2)}, u32[]{:S(2)}) collective-permute-start(bf16[16,320,128]{2,1,0:T(8,128)(2,1)} %get-tuple-element.45.own_ref), channel_id=1, source_target_pairs={{0,1},{1,0},{2,3},{3,2},{4,5},{5,4},{6,7},{7,6},{8,9},{9,8},{10,11... | collective-permute-start | bytes 3932168 | tf_op jit(solution)/shard_map/ppermute | solution.py:35
  91.8 17.1 %all-to-all-done.2.parts_ref = bf16[16,320,128]{2,1,0:T(8,128)(2,1)S(1)} async-done(((bf16[16,320,128]{2,1,0:T(8,128)(2,1)}), bf16[16,320,128]{2,1,0:T(8,128)(2,1)S(1)}, u32[]{:S(2)}, u32[]{:S(2)}) %all-to-all-start.2) | async-done | bytes 1310752 | tf_op jit(solution)/shard_map/all_to_all | solution.py:380
  108.8 0.2 plane_sum.1
  109.0 2.5 %collective-permute-start.4 = (bf16[8,24,128]{2,1,0:T(8,128)(2,1)S(1)}, bf16[8,24,128]{2,1,0:T(8,128)(2,1)S(1)}, u32[]{:S(2)}, u32[]{:S(2)}) collective-permute-start(bf16[8,24,128]{2,1,0:T(8,128)(2,1)S(1)} %get-tuple-element.44), channel_id=1, source_target_pairs={{0,2},{1,3},{2,0},{3,1},{4,6},{5,7},{6,4},{7,5},{8,10},{9,11},{10,... | collective-permute-start | bytes 147464 | tf_op jit(solution)/shard_map/ppermute | solution.py:35
  111.5 3.5 %collective-permute-done.4 = bf16[8,24,128]{2,1,0:T(8,128)(2,1)S(1)} collective-permute-done((bf16[8,24,128]{2,1,0:T(8,128)(2,1)S(1)}, bf16[8,24,128]{2,1,0:T(8,128)(2,1)S(1)}, u32[]{:S(2)}, u32[]{:S(2)}) %collective-permute-start.4) | collective-permute-done | bytes 49184 | tf_op jit(solution)/shard_map/ppermute | solution.py:35
  115.0 0.6 pad_maximum_fusion
  115.7 21.6 %all-to-all-start.3 = ((bf16[16,24,128]{2,1,0:T(8,128)(2,1)}), bf16[16,24,128]{2,1,0:T(8,128)(2,1)S(1)}, u32[]{:S(2)}, u32[]{:S(2)}) async-start(bf16[16,24,128]{2,1,0:T(8,128)(2,1)} %pad_maximum_fusion), calls=%async_computation.3 | async-start | bytes 196608 | tf_op jit(solution)/shard_map/all_to_all | solution.py:396
  137.3 4.3 %project_back.1 = bf16[128,2560]{1,0:T(8,128)(2,1)} custom-call(s32[1]{0:T(128)} %bitcast.3.core_ref, bf16[128,512]{1,0:T(8,128)(2,1)S(1)} %own_rows.1.rows_ref, bf16[16,320,128]{2,1,0:T(8,128)(2,1)} %get-tuple-element.45.own_ref, bf16[16,320,128]{2,1,0:T(8,128)(2,1)S(1)} %collective-permute-done.5.other_ref), custom_call_target="tpu_custom_call" | custom-call | tf_op jit(solution)/shard_map/project_back/pallas_call | solution.py:363
  141.6 2.3 %all-to-all-done.3 = bf16[16,24,128]{2,1,0:T(8,128)(2,1)S(1)} async-done(((bf16[16,24,128]{2,1,0:T(8,128)(2,1)}), bf16[16,24,128]{2,1,0:T(8,128)(2,1)S(1)}, u32[]{:S(2)}, u32[]{:S(2)}) %all-to-all-start.3) | async-done | bytes 98336 | tf_op jit(solution)/shard_map/all_to_all | solution.py:396
  144.0 12.9 %all_to_all.24.pieces_ref = bf16[16,24,128]{2,1,0:T(8,128)(2,1)} all-to-all(bf16[16,24,128]{2,1,0:T(8,128)(2,1)S(1)} %broadcast_in_dim.5), channel_id=1, replica_groups={{0,32,64,96,128,160,192,224,256,288,320,352,384,416,448,480},{512,544,5..., dimensions={0} | all-to-all | bytes 196608 | tf_op jit(solution)/shard_map/all_to_all | solution.py:380
  156.9 1.5 join.1
  (14 shorter events, 0.1 us)
Async XLA Ops:
  0.6 49.1 %copy-start.3 = (s32[128]{0:T(128)S(1)}, s32[128]{0:T(128)}, u32[]{:S(2)}) copy-start(s32[128]{0:T(128)} %param.15) | copy-start | bytes 1540
  2.0 47.9 %all-to-all-start.1 = ((bf16[16,24,128]{2,1,0:T(8,128)(2,1)}), bf16[16,24,128]{2,1,0:T(8,128)(2,1)S(1)}, u32[]{:S(2)}, u32[]{:S(2)}) async-start(bf16[16,24,128]{2,1,0:T(8,128)(2,1)} %cut_out.1), calls=%async_computation.1 | async-start | bytes 196608 | tf_op jit(solution)/shard_map/all_to_all | solution.py:385
  28.4 23.2 %copy-start = (bf16[192,2560]{1,0:T(8,128)(2,1)S(1)}, bf16[192,2560]{1,0:T(8,128)(2,1)}, u32[]{:S(2)}) copy-start(bf16[192,2560]{1,0:T(8,128)(2,1)} %q_ref.1) | copy-start | bytes 2949124
  28.4 23.2 %copy-start.1 = (bf16[128,2560]{1,0:T(8,128)(2,1)S(1)}, bf16[128,2560]{1,0:T(8,128)(2,1)}, u32[]{:S(2)}) copy-start(bf16[128,2560]{1,0:T(8,128)(2,1)} %act_ref.1) | copy-start | bytes 1966084
  28.4 23.2 %copy-start.2 = (s32[128]{0:T(128)S(1)}, s32[128]{0:T(128)}, u32[]{:S(2)}) copy-start(s32[128]{0:T(128)} %param.14) | copy-start | bytes 1540
  31.1 45.3 %collective-permute-start.1 = (bf16[16,3712]{1,0:T(8,128)(2,1)S(1)}, bf16[16,3712]{1,0:T(8,128)(2,1)S(1)}, u32[]{:S(2)}, u32[]{:S(2)}) collective-permute-start(bf16[16,3712]{1,0:T(8,128)(2,1)S(1)} %get-tuple-element.40), channel_id=1, source_target_pairs={{0,512},{32,544},{64,576},{96,608},{128,640},{160,672},{192,704},{... | collective-permute-start | bytes 356360 | tf_op jit(solution)/shard_map/ppermute | solution.py:35
  45.7 30.7 %collective-permute-start.2 = (bf16[16,3712]{1,0:T(8,128)(2,1)S(1)}, bf16[16,3712]{1,0:T(8,128)(2,1)S(1)}, u32[]{:S(2)}, u32[]{:S(2)}) collective-permute-start(bf16[16,3712]{1,0:T(8,128)(2,1)S(1)} %get-tuple-element.41), channel_id=1, source_target_pairs={{0,256},{32,288},{64,320},{96,352},{128,384},{160,416},{192,448},{... | collective-permute-start | bytes 356360 | tf_op jit(solution)/shard_map/ppermute | solution.py:35
  51.6 23.7 %all-to-all-start = ((bf16[16,320,128]{2,1,0:T(8,128)(2,1)}), bf16[16,320,128]{2,1,0:T(8,128)(2,1)S(1)}, u32[]{:S(2)}, u32[]{:S(2)}) async-start(bf16[16,320,128]{2,1,0:T(8,128)(2,1)} %get-tuple-element.18), calls=%async_computation | async-start | bytes 2621440 | tf_op jit(solution)/shard_map/cond/branch_1_fun/all_to_all | solution.py:380
  58.1 18.3 %collective-permute-start = (bf16[128,2560]{1,0:T(8,128)(2,1)S(1)}, bf16[128,2560]{1,0:T(8,128)(2,1)}, u32[]{:S(2)}, u32[]{:S(2)}) collective-permute-start(bf16[128,2560]{1,0:T(8,128)(2,1)S(1)} %get-tuple-element.23), channel_id=1, source_target_pairs={{0,1},{1,0},{2,3},{3,2},{4,5},{5,4},{6,7},{7,6},{8,9},{9,8},{10,11... | collective-permute-start | bytes 1966088 | tf_op jit(solution)/shard_map/cond/branch_1_fun/ppermute | solution.py:35
  77.8 3.2 %collective-permute-start.3 = (bf16[128,512]{1,0:T(8,128)(2,1)S(1)}, bf16[128,512]{1,0:T(8,128)(2,1)S(1)}, u32[]{:S(2)}, u32[]{:S(2)}) collective-permute-start(bf16[128,512]{1,0:T(8,128)(2,1)S(1)} %own_rows.1.rows_ref), channel_id=1, source_target_pairs={{0,1},{1,0},{2,3},{3,2},{4,5},{5,4},{6,7},{7,6},{8,9},{9,8},{10,11... | collective-permute-start | bytes 393224 | tf_op jit(solution)/shard_map/ppermute | solution.py:35
  84.1 24.7 %all-to-all-start.2 = ((bf16[16,320,128]{2,1,0:T(8,128)(2,1)}), bf16[16,320,128]{2,1,0:T(8,128)(2,1)S(1)}, u32[]{:S(2)}, u32[]{:S(2)}) async-start(bf16[16,320,128]{2,1,0:T(8,128)(2,1)} %gradient_pieces.1), calls=%async_computation.2 | async-start | bytes 2621440 | tf_op jit(solution)/shard_map/all_to_all | solution.py:380
  89.8 47.5 %collective-permute-start.5 = (bf16[16,320,128]{2,1,0:T(8,128)(2,1)}, bf16[16,320,128]{2,1,0:T(8,128)(2,1)S(1)}, u32[]{:S(2)}, u32[]{:S(2)}) collective-permute-start(bf16[16,320,128]{2,1,0:T(8,128)(2,1)} %get-tuple-element.45.own_ref), channel_id=1, source_target_pairs={{0,1},{1,0},{2,3},{3,2},{4,5},{5,4},{6,7},{7,6},{8,9},{9,8},{10,11... | collective-permute-start | bytes 3932168 | tf_op jit(solution)/shard_map/ppermute | solution.py:35
  109.0 6.0 %collective-permute-start.4 = (bf16[8,24,128]{2,1,0:T(8,128)(2,1)S(1)}, bf16[8,24,128]{2,1,0:T(8,128)(2,1)S(1)}, u32[]{:S(2)}, u32[]{:S(2)}) collective-permute-start(bf16[8,24,128]{2,1,0:T(8,128)(2,1)S(1)} %get-tuple-element.44), channel_id=1, source_target_pairs={{0,2},{1,3},{2,0},{3,1},{4,6},{5,7},{6,4},{7,5},{8,10},{9,11},{10,... | collective-permute-start | bytes 147464 | tf_op jit(solution)/shard_map/ppermute | solution.py:35
  115.7 28.3 %all-to-all-start.3 = ((bf16[16,24,128]{2,1,0:T(8,128)(2,1)}), bf16[16,24,128]{2,1,0:T(8,128)(2,1)S(1)}, u32[]{:S(2)}, u32[]{:S(2)}) async-start(bf16[16,24,128]{2,1,0:T(8,128)(2,1)} %pad_maximum_fusion), calls=%async_computation.3 | async-start | bytes 196608 | tf_op jit(solution)/shard_map/all_to_all | solution.py:396

commit v8 on v7

--- a/solution.py
+++ b/solution.py
@@ -170,22 +170,24 @@
         preferred_element_type=F32,
     )
     core = core_ref[0]
-    pairs = out_ref.shape[1] // 40
-    shard = whole.shape[0] // (4 * pairs)
+    quads = out_ref.shape[1] // 40
+    shard = whole.shape[0] // (8 * quads)
     upper = iota((8, WIDTH), 0) < 4
-    for pair in range(pairs):
-
-        def rows(odd, start, size):
-            at = (4 * pair + 2 * odd + core) * shard + start
-            return whole[pl.ds(pl.multiple_of(at, 8), size), :]
-
-        for cut in range(CUTS):
-            split = 16 * CUTS + 8 * (cut // 2)
-            even, odd = rows(0, split, 8), pltpu.roll(rows(1, split, 8), 4, 0)
-            mixed = jnp.where(upper, even, odd) if cut % 2 == 0 else jnp.where(upper, odd, even)
-            piece = jnp.concatenate([rows(0, 16 * cut, 16), rows(1, 16 * cut, 16), mixed], axis=0).astype(BF16)
-            for k in range(CUTS):
-                out_ref[cut * CUTS + k, 40 * pair : 40 * pair + 40, :] = piece[:, k * HD : (k + 1) * HD]
+    for quad in range(quads):
+        for parity in range(2):
+
+            def rows(later, start, size):
+                at = (2 * (4 * quad + 2 * later + parity) + core) * shard + start
+                return whole[pl.ds(pl.multiple_of(at, 8), size), :]
+
+            for cut in range(CUTS):
+                split = 16 * CUTS + 8 * (cut // 2)
+                one, two = rows(0, split, 8), pltpu.roll(rows(1, split, 8), 4, 0)
+                mixed = jnp.where(upper, one, two) if cut % 2 == 0 else jnp.where(upper, two, one)
+                piece = jnp.concatenate([rows(0, 16 * cut, 16), rows(1, 16 * cut, 16), mixed], axis=0).astype(BF16)
+                for k in range(CUTS):
+                    target = 2 * (cut * CUTS + k) + parity
+                    out_ref[target, 40 * quad : 40 * quad + 40, :] = piece[:, k * HD : (k + 1) * HD]
 
 
 def gradient_pieces(core, rows, other_rows, activations, other_activations):
@@ -199,47 +201,41 @@
             num_scalar_prefetch=1,
             grid=(steps,),
             in_specs=[held, held, columns, columns],
-            out_specs=pl.BlockSpec((CUTS * CUTS, 20 * DEPTH // steps, HD), lambda m, *_: (0, m, 0)),
+            out_specs=pl.BlockSpec((2 * PLANE, 10 * DEPTH // steps, HD), lambda m, *_: (0, m, 0)),
             scratch_shapes=[pltpu.VMEM((features // steps, WIDTH), F32)],
         ),
-        out_shape=jax.ShapeDtypeStruct((CUTS * CUTS, 20 * DEPTH, HD), BF16),
+        out_shape=jax.ShapeDtypeStruct((2 * PLANE, 10 * DEPTH, HD), BF16),
         compiler_params=pltpu.CompilerParams(vmem_limit_bytes=24 * 2**20),
         name="gradient_pieces",
     )(core, rows, other_rows, activations, other_activations)
 
 
-def plane_sum_kernel(odd_ref, parts_ref, keep_ref, send_ref, whole):
-    pairs, rows, _ = whole.shape
-    for pair in range(pairs):
-        whole[pair] = jnp.sum(parts_ref[:, pair * rows : (pair + 1) * rows, :].astype(F32), axis=0)
-    odd = odd_ref[0]
-    for target, parity in ((keep_ref, odd), (send_ref, 1 - odd)):
-        for pair in range(whole.shape[0]):
-            own = whole[pair, pl.ds(pl.multiple_of(parity * 16, 8), 16), :]
-            target[pair] = jnp.concatenate([own, whole[pair, 32:40, :]], axis=0).astype(BF16)
-
-
-def plane_sum(odd, parts):
-    count, rows, lanes = parts.shape
-    pairs, rows = rows // 40, 40
-    out = pl.BlockSpec((pairs, ROWS, lanes), lambda i, *_: (0, 0, 0))
+def plane_sum_kernel(parts_ref, out_ref):
+    count = out_ref.shape[0] // 2
+    for pair in range(count // 2):
+        total = jnp.sum(parts_ref[:, 40 * pair : 40 * pair + 40, :].astype(F32), axis=0)
+        for later in range(2):
+            piece = jnp.concatenate([total[16 * later : 16 * later + 16], total[32:]], axis=0).astype(BF16)
+            for half in range(2):
+                out_ref[half * count + 2 * pair + later] = piece
+
+
+def plane_sum(parts):
+    _, rows, lanes = parts.shape
+    out = (rows // 10, ROWS, lanes)
     return pl.pallas_call(
         plane_sum_kernel,
-        grid_spec=pltpu.PrefetchScalarGridSpec(
-            num_scalar_prefetch=1,
-            grid=(1,),
-            in_specs=[pl.BlockSpec((count, pairs * rows, lanes), lambda i, *_: (0, 0, 0))],
-            out_specs=[out, out],
-            scratch_shapes=[pltpu.VMEM((pairs, rows, lanes), F32)],
-        ),
-        out_shape=[jax.ShapeDtypeStruct((pairs, ROWS, lanes), BF16)] * 2,
+        grid=(1,),
+        in_specs=[pl.BlockSpec(parts.shape, lambda i: (0, 0, 0))],
+        out_specs=pl.BlockSpec(out, lambda i: (0, 0, 0)),
+        out_shape=jax.ShapeDtypeStruct(out, BF16),
         compiler_params=pltpu.CompilerParams(vmem_limit_bytes=24 * 2**20),
         name="plane_sum",
-    )(odd, parts)
-
-
-def join_kernel(odd_ref, pieces_ref, out_ref):
-    odd = odd_ref[0]
+    )(parts)
+
+
+def join_kernel(later_ref, pieces_ref, out_ref):
+    later = later_ref[0]
     upper = iota((8, HD), 0) < 4
     for k in range(CUTS):
         lanes = slice(k * HD, (k + 1) * HD)
@@ -249,12 +245,12 @@
             tiles.append(pieces_ref[cut * CUTS + k, 16:, :].astype(F32))
         last = []
         for low, high in ((tiles[0], tiles[1]), (tiles[2], tiles[3])):
-            from_odd = pltpu.roll(jnp.where(upper, high, low), 4, 0)
-            last.append(jnp.where(odd == 1, from_odd, jnp.where(upper, low, high)))
+            turned = pltpu.roll(jnp.where(upper, high, low), 4, 0)
+            last.append(jnp.where(later == 1, turned, jnp.where(upper, low, high)))
         out_ref[16 * CUTS :, lanes] = jnp.concatenate(last, axis=0).astype(BF16)
 
 
-def join(odd, pieces, rows):
+def join(later, pieces, rows):
     return pl.pallas_call(
         join_kernel,
         grid_spec=pltpu.PrefetchScalarGridSpec(
@@ -265,7 +261,7 @@
         ),
         out_shape=jax.ShapeDtypeStruct((rows, WIDTH), BF16),
         name="join",
-    )(odd, pieces)
+    )(later, pieces)
 
 
 def cut_kernel(place_ref, rows_ref, tile_ref, out_ref):
@@ -385,6 +381,17 @@
     return lax.all_to_all(copies, "fsdp", 0, 0, axis_index_groups=groups)
 
 
+def planes_exchange(pieces):
+    count = 2 * DEPTH
+    groups = [
+        [(half * PLANE + at) * count + 2 * (z + odd) + core for at in range(PLANE) for odd in range(2)]
+        for half in range(2)
+        for z in range(0, DEPTH, 2)
+        for core in range(2)
+    ]
+    return lax.all_to_all(pieces, BOTH, 0, 0, axis_index_groups=groups)
+
+
 def depth_exchange(pieces):
     count = 2 * DEPTH
     groups = [
@@ -396,17 +403,13 @@
     return lax.all_to_all(pieces, BOTH, 0, 0, axis_index_groups=groups)
 
 
-def added(one, two):
-    return (one.astype(F32) + two.astype(F32)).astype(BF16)
-
-
 def local(activations, value_weight, queries, key_rows, context_grad, segment, send_slot):
     tok, features = activations.shape
     block = (queries.shape[0] - tok) // SECTIONS
     half = lax.axis_size("dp") // 2
     place = (lax.axis_index("dp") % PLANE).astype(jnp.int32).reshape(1)
     core = (lax.axis_index("fsdp") % 2).astype(jnp.int32).reshape(1)
-    odd = (lax.axis_index("fsdp") // 2 % 2).astype(jnp.int32).reshape(1)
+    later = (lax.axis_index("fsdp") // 4 % 2).astype(jnp.int32).reshape(1)
 
     first, second = messages(queries, key_rows, context_grad, tok, block)
     first = swapped(first, "dp", half)
@@ -425,18 +428,14 @@
 
     row_grads = own_rows(send_slot, main, first, second, block)
     other_rows = swapped(row_grads, "fsdp", 1)
-    parts = plane_exchange(gradient_pieces(core, row_grads, other_rows, activations, other_act))
+    parts = planes_exchange(gradient_pieces(core, row_grads, other_rows, activations, other_act))
     other_weight = swapped(own_weight, "fsdp", 1)
-
-    keep, send = plane_sum(odd, parts)
-    came = swapped(send, "fsdp", 2)
-    depth_part = added(keep, came)
-    depth_parts = depth_exchange(jnp.concatenate([depth_part, depth_part], axis=0))
+    depth_parts = depth_exchange(plane_sum(parts))
     input_grad = project_back(core, row_grads, own_weight, other_weight, features)
     depth_parts, input_grad = lax.optimization_barrier((depth_parts, input_grad))
     finished = jnp.sum(depth_parts.astype(F32), axis=0).astype(BF16)
     finished = plane_exchange(jnp.broadcast_to(finished[None], (PLANE, *finished.shape)))
-    weight_grad = join(odd, finished, value_weight.shape[0])
+    weight_grad = join(later, finished, value_weight.shape[0])
     return (input_grad, weight_grad)
 
 

time: 159 us -> 156 us (0.981)
  blocking collectives: 12.9 us -> 0 us
  waiting for transfers between devices: 34.7 us -> 39.5 us
  starting transfers between devices: 87.1 us -> 90.7 us
    all_to_all x0 -> x1, waiting for transfers between devices: none -> 17.1 us  [planes_exchange(): return lax.all_to_all(pieces, BOTH, 0, 0, axis_index_groups=groups)]
    all_to_all x1 -> x0, blocking collectives: 12.9 us -> none  [plane_exchange(): return lax.all_to_all(pieces, 'dp', 0, 0, axis_index_groups=groups)]
    all_to_all x2, waiting for transfers between devices: 27.6 us -> 16.9 us  [plane_exchange(): return lax.all_to_all(pieces, 'dp', 0, 0, axis_index_groups=groups)]
    all_to_all x0 -> x1, starting transfers between devices: none -> 5.84 us  [planes_exchange(): return lax.all_to_all(pieces, BOTH, 0, 0, axis_index_groups=groups)]
    ppermute x6 -> x5, waiting for transfers between devices: 4.81 us -> 1.31 us  [swapped(): return lax.ppermute(block, axis, route)]
    ppermute x6 -> x5, starting transfers between devices: 26.9 us -> 24.4 us  [swapped(): return lax.ppermute(block, axis, route)]
    all_to_all x1, waiting for transfers between devices: 2.34 us -> 4.13 us  [depth_exchange(): return lax.all_to_all(pieces, BOTH, 0, 0, axis_index_groups=groups)]
  transfers between devices with their start and end apart: 10 -> 10, of which waited for: 5 -> 5; matrix products, arithmetic and copies ran while one was open for 2% -> 1% of each run, Pallas kernels for 8% -> 9%
where the time goes in v8:
time: 156 us; the launch traced here: 155 us
  starting transfers between devices  90.7 us (58%)
  waiting for transfers between devices  39.5 us (25%)
  Pallas kernels  20.8 us (13%)
  local copies, waits for them, and re-layouts  3.25 us (2%)
    all_to_all x1, starting transfers between devices, depth_gather(): return lax.all_to_all(copies, 'fsdp', 0, 0, axis_index_groups=groups)  26.4 us
    ppermute x5, starting transfers between devices, swapped(): return lax.ppermute(block, axis, route)  24.4 us
    all_to_all x1, starting transfers between devices, depth_exchange(): return lax.all_to_all(pieces, BOTH, 0, 0, axis_index_groups=groups)  21.6 us
    all_to_all x1, waiting for transfers between devices, planes_exchange(): return lax.all_to_all(pieces, BOTH, 0, 0, axis_index_groups=groups)  17.1 us
    all_to_all x2, waiting for transfers between devices, plane_exchange(): return lax.all_to_all(pieces, 'dp', 0, 0, axis_index_groups=groups)  16.9 us
    all_to_all x2, starting transfers between devices, plane_exchange(): return lax.all_to_all(pieces, 'dp', 0, 0, axis_index_groups=groups)  12.4 us
    all_to_all x1, starting transfers between devices, planes_exchange(): return lax.all_to_all(pieces, BOTH, 0, 0, axis_index_groups=groups)  5.84 us
    pallas_call x1, Pallas kernels, project_back(): pl.pallas_call(project_kernel, grid_spec=pltpu.PrefetchScalarGridSpec(num...  4.26 us
  transfers between devices with their start and end apart: 10, of which 5 were waited for; matrix products, arithmetic and copies ran while one was open for 1% of the time, Pallas kernels for 9%

profile of v8, /device:TPU:2, one launch (start us, length us, event | category | flops | bytes accessed | tf_op | source)
XLA Modules:
  0.0 155.1 jit_solution(9944274759501819009)
XLA Ops:
  0.7 1.4 cut_out.1
  2.0 26.4 %all-to-all-start.1 = ((bf16[16,24,128]{2,1,0:T(8,128)(2,1)}), bf16[16,24,128]{2,1,0:T(8,128)(2,1)S(1)}, u32[]{:S(2)}, u32[]{:S(2)}) async-start(bf16[16,24,128]{2,1,0:T(8,128)(2,1)} %cut_out.1), calls=%async_computation.1 | async-start | bytes 196608 | tf_op jit(solution)/shard_map/all_to_all | solution.py:381
  28.4 0.0 copy-start.1
  28.4 0.0 copy-start.3
  28.4 2.7 %messages.1 = (bf16[16,3712]{1,0:T(8,128)(2,1)S(1)}, bf16[16,3712]{1,0:T(8,128)(2,1)S(1)}) custom-call(bf16[192,2560]{1,0:T(8,128)(2,1)} %q_ref.1, bf16[192,512]{1,0:T(8,128)(2,1)} %k_ref.1, bf16[192,2560]{1,0:T(8,128)(2,1)} %c_ref.1), custom_call_target="tpu_custom_call" | custom-call | tf_op jit(solution)/shard_map/messages/pallas_call | solution.py:79
  31.1 14.7 %collective-permute-start.1 = (bf16[16,3712]{1,0:T(8,128)(2,1)S(1)}, bf16[16,3712]{1,0:T(8,128)(2,1)S(1)}, u32[]{:S(2)}, u32[]{:S(2)}) collective-permute-start(bf16[16,3712]{1,0:T(8,128)(2,1)S(1)} %get-tuple-element.38), channel_id=1, source_target_pairs={{0,512},{32,544},{64,576},{96,608},{128,640},{160,672},{192,704},{... | collective-permute-start | bytes 356360 | tf_op jit(solution)/shard_map/ppermute | solution.py:35
  45.7 4.0 %collective-permute-start.2 = (bf16[16,3712]{1,0:T(8,128)(2,1)S(1)}, bf16[16,3712]{1,0:T(8,128)(2,1)S(1)}, u32[]{:S(2)}, u32[]{:S(2)}) collective-permute-start(bf16[16,3712]{1,0:T(8,128)(2,1)S(1)} %get-tuple-element.39), channel_id=1, source_target_pairs={{0,256},{32,288},{64,320},{96,352},{128,384},{160,416},{192,448},{... | collective-permute-start | bytes 356360 | tf_op jit(solution)/shard_map/ppermute | solution.py:35
  49.8 0.1 copy.11.slot_ref
  49.9 1.7 %spread.1 = bf16[16,320,128]{2,1,0:T(8,128)(2,1)} custom-call(s32[1]{0:T(128)} %bitcast.4.place_ref, bf16[16,24,128]{2,1,0:T(8,128)(2,1)S(1)} %all-to-all-done.1.pieces_ref), custom_call_target="tpu_custom_call" | custom-call | tf_op jit(solution)/shard_map/spread/pallas_call | solution.py:312
  51.6 24.8 %conditional.1 = (bf16[16,320,128]{2,1,0:T(8,128)(2,1)}, bf16[128,512]{1,0:T(8,128)(2,1)}, bf16[128,2560]{1,0:T(8,128)(2,1)}) conditional(s32[]{:T(128)} %convert_element_type.2, (bf16[16,320,128]{2,1,0:T(8,128)(2,1)}, bf16[128,2560]{1,0:T(8,128)(2,1)S(1)}) %tuple.26, (bf16[16,320,128]{2,1,0:T(8,128)(2,1)}, s32[128]{0:T(128)S(1)}, ...), branch_computations={%region_0.1_spmd, %region_1.2_spmd} | conditional | bytes 9176160 | solution.py:424
  51.6 6.5 %all-to-all-start = ((bf16[16,320,128]{2,1,0:T(8,128)(2,1)}), bf16[16,320,128]{2,1,0:T(8,128)(2,1)S(1)}, u32[]{:S(2)}, u32[]{:S(2)}) async-start(bf16[16,320,128]{2,1,0:T(8,128)(2,1)} %get-tuple-element.18), calls=%async_computation | async-start | bytes 2621440 | tf_op jit(solution)/shard_map/cond/branch_1_fun/all_to_all | solution.py:376
  58.1 1.9 %collective-permute-start = (bf16[128,2560]{1,0:T(8,128)(2,1)S(1)}, bf16[128,2560]{1,0:T(8,128)(2,1)}, u32[]{:S(2)}, u32[]{:S(2)}) collective-permute-start(bf16[128,2560]{1,0:T(8,128)(2,1)S(1)} %get-tuple-element.23), channel_id=1, source_target_pairs={{0,1},{1,0},{2,3},{3,2},{4,5},{5,4},{6,7},{7,6},{8,9},{9,8},{10,11... | collective-permute-start | bytes 1966088 | tf_op jit(solution)/shard_map/cond/branch_1_fun/ppermute | solution.py:35
  60.0 0.7 copy.10.col_ref
  60.8 4.0 %attend.1 = bf16[128,512]{1,0:T(8,128)(2,1)} custom-call(s32[128,1]{1,0:T(8,128)} %copy.10.col_ref, s32[1,128]{1,0:T(1,128)S(1)} %bitcast.7, bf16[192,2560]{1,0:T(8,128)(2,1)S(1)} %get-tuple-element.20.q_ref, bf16[192,512]{1,0:T(8,128)(2,1)} %get-tuple-element.21.k_ref, bf16[192,2560]{1,0:T(8,128)(2,1)} %get-tuple-element.22.c_ref), custom_call_target="tpu_custom_call" | custom-call | tf_op jit(solution)/shard_map/cond/branch_1_fun/attend/pallas_call | solution.py:126
  64.8 10.5 %all-to-all-done = bf16[16,320,128]{2,1,0:T(8,128)(2,1)S(1)} async-done(((bf16[16,320,128]{2,1,0:T(8,128)(2,1)}), bf16[16,320,128]{2,1,0:T(8,128)(2,1)S(1)}, u32[]{:S(2)}, u32[]{:S(2)}) %all-to-all-start) | async-done | bytes 1310752 | tf_op jit(solution)/shard_map/cond/branch_1_fun/all_to_all | solution.py:376
  75.3 1.1 copy.15
  76.4 1.4 own_rows.1.rows_ref
  77.8 1.9 %collective-permute-start.3 = (bf16[128,512]{1,0:T(8,128)(2,1)S(1)}, bf16[128,512]{1,0:T(8,128)(2,1)S(1)}, u32[]{:S(2)}, u32[]{:S(2)}) collective-permute-start(bf16[128,512]{1,0:T(8,128)(2,1)S(1)} %own_rows.1.rows_ref), channel_id=1, source_target_pairs={{0,1},{1,0},{2,3},{3,2},{4,5},{5,4},{6,7},{7,6},{8,9},{9,8},{10,11... | collective-permute-start | bytes 393224 | tf_op jit(solution)/shard_map/ppermute | solution.py:35
  79.7 1.3 collective-permute-done.3.other_rows_ref
  81.0 3.1 %gradient_pieces.1 = bf16[32,160,128]{2,1,0:T(8,128)(2,1)} custom-call(s32[1]{0:T(128)} %bitcast.2.core_ref, bf16[128,512]{1,0:T(8,128)(2,1)S(1)} %own_rows.1.rows_ref, bf16[128,512]{1,0:T(8,128)(2,1)S(1)} %collective-permute-done.3.other_rows_ref, bf16[128,2560]{1,0:T(8,128)(2,1)S(1)} %copy-done.1, bf16[128,2560]{1,0:T(8,128)(2,1)} %get-tuple-element.40.other_act_ref), custom_call_target="tpu_custom_call" | custom-call | tf_op jit(solution)/shard_map/gradient_pieces/pallas_call | solution.py:198
  84.1 5.8 %all-to-all-start.2 = ((bf16[32,160,128]{2,1,0:T(8,128)(2,1)}), bf16[32,160,128]{2,1,0:T(8,128)(2,1)S(1)}, u32[]{:S(2)}, u32[]{:S(2)}) async-start(bf16[32,160,128]{2,1,0:T(8,128)(2,1)} %gradient_pieces.1), calls=%async_computation.2 | async-start | bytes 2621440 | tf_op jit(solution)/shard_map/all_to_all | solution.py:392
  90.0 1.9 %collective-permute-start.4 = (bf16[16,320,128]{2,1,0:T(8,128)(2,1)}, bf16[16,320,128]{2,1,0:T(8,128)(2,1)S(1)}, u32[]{:S(2)}, u32[]{:S(2)}) collective-permute-start(bf16[16,320,128]{2,1,0:T(8,128)(2,1)} %get-tuple-element.41.own_ref), channel_id=1, source_target_pairs={{0,1},{1,0},{2,3},{3,2},{4,5},{5,4},{6,7},{7,6},{8,9},{9,8},{10,11... | collective-permute-start | bytes 3932168 | tf_op jit(solution)/shard_map/ppermute | solution.py:35
  91.9 17.1 %all-to-all-done.2.parts_ref = bf16[32,160,128]{2,1,0:T(8,128)(2,1)S(1)} async-done(((bf16[32,160,128]{2,1,0:T(8,128)(2,1)}), bf16[32,160,128]{2,1,0:T(8,128)(2,1)S(1)}, u32[]{:S(2)}, u32[]{:S(2)}) %all-to-all-start.2) | async-done | bytes 1310752 | tf_op jit(solution)/shard_map/all_to_all | solution.py:392
  109.0 0.8 plane_sum.1
  109.8 21.6 %all-to-all-start.3 = ((bf16[16,24,128]{2,1,0:T(8,128)(2,1)}), bf16[16,24,128]{2,1,0:T(8,128)(2,1)S(1)}, u32[]{:S(2)}, u32[]{:S(2)}) async-start(bf16[16,24,128]{2,1,0:T(8,128)(2,1)} %plane_sum.1), calls=%async_computation.3 | async-start | bytes 196608 | tf_op jit(solution)/shard_map/all_to_all | solution.py:403
  131.5 4.3 %project_back.1 = bf16[128,2560]{1,0:T(8,128)(2,1)} custom-call(s32[1]{0:T(128)} %bitcast.2.core_ref, bf16[128,512]{1,0:T(8,128)(2,1)S(1)} %own_rows.1.rows_ref, bf16[16,320,128]{2,1,0:T(8,128)(2,1)} %get-tuple-element.41.own_ref, bf16[16,320,128]{2,1,0:T(8,128)(2,1)S(1)} %collective-permute-done.4.other_ref), custom_call_target="tpu_custom_call" | custom-call | tf_op jit(solution)/shard_map/project_back/pallas_call | solution.py:359
  135.8 4.1 %all-to-all-done.3 = bf16[16,24,128]{2,1,0:T(8,128)(2,1)S(1)} async-done(((bf16[16,24,128]{2,1,0:T(8,128)(2,1)}), bf16[16,24,128]{2,1,0:T(8,128)(2,1)S(1)}, u32[]{:S(2)}, u32[]{:S(2)}) %all-to-all-start.3) | async-done | bytes 98336 | tf_op jit(solution)/shard_map/all_to_all | solution.py:403
  139.9 0.7 broadcast_in_dim.5
  140.6 5.9 %all-to-all-start.4 = ((bf16[16,24,128]{2,1,0:T(8,128)(2,1)}), bf16[16,24,128]{2,1,0:T(8,128)(2,1)S(1)}, u32[]{:S(2)}, u32[]{:S(2)}) async-start(bf16[16,24,128]{2,1,0:T(8,128)(2,1)} %broadcast_in_dim.5), calls=%async_computation.4 | async-start | bytes 196608 | tf_op jit(solution)/shard_map/all_to_all | solution.py:376
  146.5 6.4 %all-to-all-done.4.pieces_ref = bf16[16,24,128]{2,1,0:T(8,128)(2,1)S(1)} async-done(((bf16[16,24,128]{2,1,0:T(8,128)(2,1)}), bf16[16,24,128]{2,1,0:T(8,128)(2,1)S(1)}, u32[]{:S(2)}, u32[]{:S(2)}) %all-to-all-start.4) | async-done | bytes 98336 | tf_op jit(solution)/shard_map/all_to_all | solution.py:376
  152.9 0.6 copy-done.2
  153.5 1.5 join.1
  (13 shorter events, 0.0 us)
Async XLA Ops:
  0.6 49.1 %copy-start.4 = (s32[128]{0:T(128)S(1)}, s32[128]{0:T(128)}, u32[]{:S(2)}) copy-start(s32[128]{0:T(128)} %param.15) | copy-start | bytes 1540
  2.0 47.9 %all-to-all-start.1 = ((bf16[16,24,128]{2,1,0:T(8,128)(2,1)}), bf16[16,24,128]{2,1,0:T(8,128)(2,1)S(1)}, u32[]{:S(2)}, u32[]{:S(2)}) async-start(bf16[16,24,128]{2,1,0:T(8,128)(2,1)} %cut_out.1), calls=%async_computation.1 | async-start | bytes 196608 | tf_op jit(solution)/shard_map/all_to_all | solution.py:381
  28.4 23.2 %copy-start = (bf16[192,2560]{1,0:T(8,128)(2,1)S(1)}, bf16[192,2560]{1,0:T(8,128)(2,1)}, u32[]{:S(2)}) copy-start(bf16[192,2560]{1,0:T(8,128)(2,1)} %q_ref.1) | copy-start | bytes 2949124
  28.4 23.2 %copy-start.1 = (bf16[128,2560]{1,0:T(8,128)(2,1)S(1)}, bf16[128,2560]{1,0:T(8,128)(2,1)}, u32[]{:S(2)}) copy-start(bf16[128,2560]{1,0:T(8,128)(2,1)} %act_ref.1) | copy-start | bytes 1966084
  28.4 23.2 %copy-start.3 = (s32[128]{0:T(128)S(1)}, s32[128]{0:T(128)}, u32[]{:S(2)}) copy-start(s32[128]{0:T(128)} %param.14) | copy-start | bytes 1540
  31.1 45.3 %collective-permute-start.1 = (bf16[16,3712]{1,0:T(8,128)(2,1)S(1)}, bf16[16,3712]{1,0:T(8,128)(2,1)S(1)}, u32[]{:S(2)}, u32[]{:S(2)}) collective-permute-start(bf16[16,3712]{1,0:T(8,128)(2,1)S(1)} %get-tuple-element.38), channel_id=1, source_target_pairs={{0,512},{32,544},{64,576},{96,608},{128,640},{160,672},{192,704},{... | collective-permute-start | bytes 356360 | tf_op jit(solution)/shard_map/ppermute | solution.py:35
  45.7 30.7 %collective-permute-start.2 = (bf16[16,3712]{1,0:T(8,128)(2,1)S(1)}, bf16[16,3712]{1,0:T(8,128)(2,1)S(1)}, u32[]{:S(2)}, u32[]{:S(2)}) collective-permute-start(bf16[16,3712]{1,0:T(8,128)(2,1)S(1)} %get-tuple-element.39), channel_id=1, source_target_pairs={{0,256},{32,288},{64,320},{96,352},{128,384},{160,416},{192,448},{... | collective-permute-start | bytes 356360 | tf_op jit(solution)/shard_map/ppermute | solution.py:35
  51.6 23.7 %all-to-all-start = ((bf16[16,320,128]{2,1,0:T(8,128)(2,1)}), bf16[16,320,128]{2,1,0:T(8,128)(2,1)S(1)}, u32[]{:S(2)}, u32[]{:S(2)}) async-start(bf16[16,320,128]{2,1,0:T(8,128)(2,1)} %get-tuple-element.18), calls=%async_computation | async-start | bytes 2621440 | tf_op jit(solution)/shard_map/cond/branch_1_fun/all_to_all | solution.py:376
  58.1 18.3 %collective-permute-start = (bf16[128,2560]{1,0:T(8,128)(2,1)S(1)}, bf16[128,2560]{1,0:T(8,128)(2,1)}, u32[]{:S(2)}, u32[]{:S(2)}) collective-permute-start(bf16[128,2560]{1,0:T(8,128)(2,1)S(1)} %get-tuple-element.23), channel_id=1, source_target_pairs={{0,1},{1,0},{2,3},{3,2},{4,5},{5,4},{6,7},{7,6},{8,9},{9,8},{10,11... | collective-permute-start | bytes 1966088 | tf_op jit(solution)/shard_map/cond/branch_1_fun/ppermute | solution.py:35
  77.8 3.2 %collective-permute-start.3 = (bf16[128,512]{1,0:T(8,128)(2,1)S(1)}, bf16[128,512]{1,0:T(8,128)(2,1)S(1)}, u32[]{:S(2)}, u32[]{:S(2)}) collective-permute-start(bf16[128,512]{1,0:T(8,128)(2,1)S(1)} %own_rows.1.rows_ref), channel_id=1, source_target_pairs={{0,1},{1,0},{2,3},{3,2},{4,5},{5,4},{6,7},{7,6},{8,9},{9,8},{10,11... | collective-permute-start | bytes 393224 | tf_op jit(solution)/shard_map/ppermute | solution.py:35
  84.1 24.9 %all-to-all-start.2 = ((bf16[32,160,128]{2,1,0:T(8,128)(2,1)}), bf16[32,160,128]{2,1,0:T(8,128)(2,1)S(1)}, u32[]{:S(2)}, u32[]{:S(2)}) async-start(bf16[32,160,128]{2,1,0:T(8,128)(2,1)} %gradient_pieces.1), calls=%async_computation.2 | async-start | bytes 2621440 | tf_op jit(solution)/shard_map/all_to_all | solution.py:392
  90.0 41.5 %collective-permute-start.4 = (bf16[16,320,128]{2,1,0:T(8,128)(2,1)}, bf16[16,320,128]{2,1,0:T(8,128)(2,1)S(1)}, u32[]{:S(2)}, u32[]{:S(2)}) collective-permute-start(bf16[16,320,128]{2,1,0:T(8,128)(2,1)} %get-tuple-element.41.own_ref), channel_id=1, source_target_pairs={{0,1},{1,0},{2,3},{3,2},{4,5},{5,4},{6,7},{7,6},{8,9},{9,8},{10,11... | collective-permute-start | bytes 3932168 | tf_op jit(solution)/shard_map/ppermute | solution.py:35
  109.8 30.0 %all-to-all-start.3 = ((bf16[16,24,128]{2,1,0:T(8,128)(2,1)}), bf16[16,24,128]{2,1,0:T(8,128)(2,1)S(1)}, u32[]{:S(2)}, u32[]{:S(2)}) async-start(bf16[16,24,128]{2,1,0:T(8,128)(2,1)} %plane_sum.1), calls=%async_computation.3 | async-start | bytes 196608 | tf_op jit(solution)/shard_map/all_to_all | solution.py:403
  140.6 12.3 %all-to-all-start.4 = ((bf16[16,24,128]{2,1,0:T(8,128)(2,1)}), bf16[16,24,128]{2,1,0:T(8,128)(2,1)S(1)}, u32[]{:S(2)}, u32[]{:S(2)}) async-start(bf16[16,24,128]{2,1,0:T(8,128)(2,1)} %broadcast_in_dim.5), calls=%async_computation.4 | async-start | bytes 196608 | tf_op jit(solution)/shard_map/all_to_all | solution.py:376
  152.9 0.6 copy-start.2

commit v9 on v8

--- a/solution.py
+++ b/solution.py
@@ -139,7 +139,7 @@
     )(segment.reshape(tok, 1), segment.reshape(1, tok), queries, key_rows, context_grad)
 
 
-def rows_kernel(block, slot_ref, main_ref, first_ref, second_ref, out_ref):
+def rows_kernel(block, slot_ref, main_ref, second_ref, first_ref, out_ref):
     slot = slot_ref[...]
     tok = slot.shape[0]
     parts = [sent_block(slot, ref, tok + s * block, block) for s, ref in enumerate((first_ref, second_ref))]
@@ -150,7 +150,7 @@
 
 def own_rows(send_slot, main, first, second, block):
     tok = main.shape[0]
-    operands = (send_slot.reshape(tok, 1), main, first, second)
+    operands = (send_slot.reshape(tok, 1), main, second, first)
     return pl.pallas_call(
         functools.partial(rows_kernel, block),
         grid=(1,),
@@ -260,6 +260,7 @@
             out_specs=pl.BlockSpec((rows, WIDTH), lambda i, *_: (0, 0)),
         ),
         out_shape=jax.ShapeDtypeStruct((rows, WIDTH), BF16),
+        compiler_params=pltpu.CompilerParams(vmem_limit_bytes=24 * 2**20),
         name="join",
     )(later, pieces)
 
@@ -412,8 +413,8 @@
     later = (lax.axis_index("fsdp") // 4 % 2).astype(jnp.int32).reshape(1)
 
     first, second = messages(queries, key_rows, context_grad, tok, block)
+    second = swapped(second, "dp", half // 2)
     first = swapped(first, "dp", half)
-    second = swapped(second, "dp", half // 2)
     copies = spread(place, depth_gather(cut_out(value_weight, place)))
 
     def beside(held):

time: 156 us -> 155 us (level)
  transfers between devices with their start and end apart: 10 -> 10, of which waited for: 5 -> 6; matrix products, arithmetic and copies ran while one was open for 1% -> 1% of each run, Pallas kernels for 9% -> 9%
where the time goes in v9:
time: 155 us
  starting transfers between devices  92 us (59%)
  waiting for transfers between devices  39.3 us (25%)
  Pallas kernels  19.9 us (13%)
  local copies, waits for them, and re-layouts  2.62 us (2%)
    all_to_all x1, starting transfers between devices, depth_gather(): return lax.all_to_all(copies, 'fsdp', 0, 0, axis_index_groups=groups)  26.4 us
    ppermute x5, starting transfers between devices, swapped(): return lax.ppermute(block, axis, route)  24.4 us
    all_to_all x1, starting transfers between devices, depth_exchange(): return lax.all_to_all(pieces, BOTH, 0, 0, axis_index_groups=groups)  21.6 us
    all_to_all x2, waiting for transfers between devices, plane_exchange(): return lax.all_to_all(pieces, 'dp', 0, 0, axis_index_groups=groups)  16.9 us
    all_to_all x1, waiting for transfers between devices, planes_exchange(): return lax.all_to_all(pieces, BOTH, 0, 0, axis_index_groups=groups)  16.6 us
    all_to_all x2, starting transfers between devices, plane_exchange(): return lax.all_to_all(pieces, 'dp', 0, 0, axis_index_groups=groups)  12.5 us
    all_to_all x1, starting transfers between devices, planes_exchange(): return lax.all_to_all(pieces, BOTH, 0, 0, axis_index_groups=groups)  7.06 us
    pallas_call x1, Pallas kernels, project_back(): pl.pallas_call(project_kernel, grid_spec=pltpu.PrefetchScalarGridSpec(num...  4.26 us
  transfers between devices with their start and end apart: 10, of which 6 were waited for; matrix products, arithmetic and copies ran while one was open for 1% of the time, Pallas kernels for 9%

profile of v9, /device:TPU:2, one launch (start us, length us, event | category | flops | bytes accessed | tf_op | source)
XLA Modules:
  0.0 154.6 jit_solution(9796110942054199883)
XLA Ops:
  0.7 1.4 cut_out.1
  2.0 26.4 %all-to-all-start.1 = ((bf16[16,24,128]{2,1,0:T(8,128)(2,1)}), bf16[16,24,128]{2,1,0:T(8,128)(2,1)S(1)}, u32[]{:S(2)}, u32[]{:S(2)}) async-start(bf16[16,24,128]{2,1,0:T(8,128)(2,1)} %cut_out.1), calls=%async_computation.1 | async-start | bytes 196608 | tf_op jit(solution)/shard_map/all_to_all | solution.py:382
  28.4 0.0 copy-start.1
  28.4 0.0 copy-start.2
  28.4 2.7 %messages.1 = (bf16[16,3712]{1,0:T(8,128)(2,1)S(1)}, bf16[16,3712]{1,0:T(8,128)(2,1)S(1)}) custom-call(bf16[192,2560]{1,0:T(8,128)(2,1)} %q_ref.1, bf16[192,512]{1,0:T(8,128)(2,1)} %k_ref.1, bf16[192,2560]{1,0:T(8,128)(2,1)} %c_ref.1), custom_call_target="tpu_custom_call" | custom-call | tf_op jit(solution)/shard_map/messages/pallas_call | solution.py:79
  31.1 4.0 %collective-permute-start.1 = (bf16[16,3712]{1,0:T(8,128)(2,1)S(1)}, bf16[16,3712]{1,0:T(8,128)(2,1)S(1)}, u32[]{:S(2)}, u32[]{:S(2)}) collective-permute-start(bf16[16,3712]{1,0:T(8,128)(2,1)S(1)} %get-tuple-element.38), channel_id=1, source_target_pairs={{0,256},{32,288},{64,320},{96,352},{128,384},{160,416},{192,448},{... | collective-permute-start | bytes 356360 | tf_op jit(solution)/shard_map/ppermute | solution.py:35
  35.1 14.6 %collective-permute-start.2 = (bf16[16,3712]{1,0:T(8,128)(2,1)S(1)}, bf16[16,3712]{1,0:T(8,128)(2,1)S(1)}, u32[]{:S(2)}, u32[]{:S(2)}) collective-permute-start(bf16[16,3712]{1,0:T(8,128)(2,1)S(1)} %get-tuple-element.39), channel_id=1, source_target_pairs={{0,512},{32,544},{64,576},{96,608},{128,640},{160,672},{192,704},{... | collective-permute-start | bytes 356360 | tf_op jit(solution)/shard_map/ppermute | solution.py:35
  49.8 0.1 copy.11.slot_ref
  49.9 1.7 %spread.1 = bf16[16,320,128]{2,1,0:T(8,128)(2,1)} custom-call(s32[1]{0:T(128)} %bitcast.4.place_ref, bf16[16,24,128]{2,1,0:T(8,128)(2,1)S(1)} %all-to-all-done.1.pieces_ref), custom_call_target="tpu_custom_call" | custom-call | tf_op jit(solution)/shard_map/spread/pallas_call | solution.py:313
  51.6 24.8 %conditional.1 = (bf16[16,320,128]{2,1,0:T(8,128)(2,1)}, bf16[128,512]{1,0:T(8,128)(2,1)}, bf16[128,2560]{1,0:T(8,128)(2,1)}) conditional(s32[]{:T(128)} %convert_element_type.2, (bf16[16,320,128]{2,1,0:T(8,128)(2,1)}, bf16[128,2560]{1,0:T(8,128)(2,1)S(1)}) %tuple.26, (bf16[16,320,128]{2,1,0:T(8,128)(2,1)}, s32[128]{0:T(128)S(1)}, ...), branch_computations={%region_0.1_spmd, %region_1.2_spmd} | conditional | bytes 9176160 | solution.py:425
  51.6 6.5 %all-to-all-start = ((bf16[16,320,128]{2,1,0:T(8,128)(2,1)}), bf16[16,320,128]{2,1,0:T(8,128)(2,1)S(1)}, u32[]{:S(2)}, u32[]{:S(2)}) async-start(bf16[16,320,128]{2,1,0:T(8,128)(2,1)} %get-tuple-element.18), calls=%async_computation | async-start | bytes 2621440 | tf_op jit(solution)/shard_map/cond/branch_1_fun/all_to_all | solution.py:377
  58.1 1.9 %collective-permute-start = (bf16[128,2560]{1,0:T(8,128)(2,1)S(1)}, bf16[128,2560]{1,0:T(8,128)(2,1)}, u32[]{:S(2)}, u32[]{:S(2)}) collective-permute-start(bf16[128,2560]{1,0:T(8,128)(2,1)S(1)} %get-tuple-element.23), channel_id=1, source_target_pairs={{0,1},{1,0},{2,3},{3,2},{4,5},{5,4},{6,7},{7,6},{8,9},{9,8},{10,11... | collective-permute-start | bytes 1966088 | tf_op jit(solution)/shard_map/cond/branch_1_fun/ppermute | solution.py:35
  60.0 0.7 copy.10.col_ref
  60.8 4.0 %attend.1 = bf16[128,512]{1,0:T(8,128)(2,1)} custom-call(s32[128,1]{1,0:T(8,128)} %copy.10.col_ref, s32[1,128]{1,0:T(1,128)S(1)} %bitcast.7, bf16[192,2560]{1,0:T(8,128)(2,1)S(1)} %get-tuple-element.20.q_ref, bf16[192,512]{1,0:T(8,128)(2,1)} %get-tuple-element.21.k_ref, bf16[192,2560]{1,0:T(8,128)(2,1)} %get-tuple-element.22.c_ref), custom_call_target="tpu_custom_call" | custom-call | tf_op jit(solution)/shard_map/cond/branch_1_fun/attend/pallas_call | solution.py:126
  64.8 10.5 %all-to-all-done = bf16[16,320,128]{2,1,0:T(8,128)(2,1)S(1)} async-done(((bf16[16,320,128]{2,1,0:T(8,128)(2,1)}), bf16[16,320,128]{2,1,0:T(8,128)(2,1)S(1)}, u32[]{:S(2)}, u32[]{:S(2)}) %all-to-all-start) | async-done | bytes 1310752 | tf_op jit(solution)/shard_map/cond/branch_1_fun/all_to_all | solution.py:377
  75.3 1.1 copy.15
  76.4 0.5 collective-permute-done.2.first_ref
  76.9 1.4 own_rows.1.rows_ref
  78.3 1.9 %collective-permute-start.3 = (bf16[128,512]{1,0:T(8,128)(2,1)S(1)}, bf16[128,512]{1,0:T(8,128)(2,1)S(1)}, u32[]{:S(2)}, u32[]{:S(2)}) collective-permute-start(bf16[128,512]{1,0:T(8,128)(2,1)S(1)} %own_rows.1.rows_ref), channel_id=1, source_target_pairs={{0,1},{1,0},{2,3},{3,2},{4,5},{5,4},{6,7},{7,6},{8,9},{9,8},{10,11... | collective-permute-start | bytes 393224 | tf_op jit(solution)/shard_map/ppermute | solution.py:35
  80.2 1.3 collective-permute-done.3.other_rows_ref
  81.5 3.1 %gradient_pieces.1 = bf16[32,160,128]{2,1,0:T(8,128)(2,1)} custom-call(s32[1]{0:T(128)} %bitcast.2.core_ref, bf16[128,512]{1,0:T(8,128)(2,1)S(1)} %own_rows.1.rows_ref, bf16[128,512]{1,0:T(8,128)(2,1)S(1)} %collective-permute-done.3.other_rows_ref, bf16[128,2560]{1,0:T(8,128)(2,1)S(1)} %copy-done.1, bf16[128,2560]{1,0:T(8,128)(2,1)} %get-tuple-element.40.other_act_ref), custom_call_target="tpu_custom_call" | custom-call | tf_op jit(solution)/shard_map/gradient_pieces/pallas_call | solution.py:198
  84.6 7.1 %all-to-all-start.2 = ((bf16[32,160,128]{2,1,0:T(8,128)(2,1)}), bf16[32,160,128]{2,1,0:T(8,128)(2,1)S(1)}, u32[]{:S(2)}, u32[]{:S(2)}) async-start(bf16[32,160,128]{2,1,0:T(8,128)(2,1)} %gradient_pieces.1), calls=%async_computation.2 | async-start | bytes 2621440 | tf_op jit(solution)/shard_map/all_to_all | solution.py:393
  91.7 1.9 %collective-permute-start.4 = (bf16[16,320,128]{2,1,0:T(8,128)(2,1)}, bf16[16,320,128]{2,1,0:T(8,128)(2,1)S(1)}, u32[]{:S(2)}, u32[]{:S(2)}) collective-permute-start(bf16[16,320,128]{2,1,0:T(8,128)(2,1)} %get-tuple-element.41.own_ref), channel_id=1, source_target_pairs={{0,1},{1,0},{2,3},{3,2},{4,5},{5,4},{6,7},{7,6},{8,9},{9,8},{10,11... | collective-permute-start | bytes 3932168 | tf_op jit(solution)/shard_map/ppermute | solution.py:35
  93.6 16.6 %all-to-all-done.2.parts_ref = bf16[32,160,128]{2,1,0:T(8,128)(2,1)S(1)} async-done(((bf16[32,160,128]{2,1,0:T(8,128)(2,1)}), bf16[32,160,128]{2,1,0:T(8,128)(2,1)S(1)}, u32[]{:S(2)}, u32[]{:S(2)}) %all-to-all-start.2) | async-done | bytes 1310752 | tf_op jit(solution)/shard_map/all_to_all | solution.py:393
  110.3 0.8 plane_sum.1
  111.1 21.6 %all-to-all-start.3 = ((bf16[16,24,128]{2,1,0:T(8,128)(2,1)}), bf16[16,24,128]{2,1,0:T(8,128)(2,1)S(1)}, u32[]{:S(2)}, u32[]{:S(2)}) async-start(bf16[16,24,128]{2,1,0:T(8,128)(2,1)} %plane_sum.1), calls=%async_computation.3 | async-start | bytes 196608 | tf_op jit(solution)/shard_map/all_to_all | solution.py:404
  132.7 4.3 %project_back.1 = bf16[128,2560]{1,0:T(8,128)(2,1)} custom-call(s32[1]{0:T(128)} %bitcast.2.core_ref, bf16[128,512]{1,0:T(8,128)(2,1)S(1)} %own_rows.1.rows_ref, bf16[16,320,128]{2,1,0:T(8,128)(2,1)} %get-tuple-element.41.own_ref, bf16[16,320,128]{2,1,0:T(8,128)(2,1)S(1)} %collective-permute-done.4.other_ref), custom_call_target="tpu_custom_call" | custom-call | tf_op jit(solution)/shard_map/project_back/pallas_call | solution.py:360
  137.0 3.9 %all-to-all-done.3 = bf16[16,24,128]{2,1,0:T(8,128)(2,1)S(1)} async-done(((bf16[16,24,128]{2,1,0:T(8,128)(2,1)}), bf16[16,24,128]{2,1,0:T(8,128)(2,1)S(1)}, u32[]{:S(2)}, u32[]{:S(2)}) %all-to-all-start.3) | async-done | bytes 98336 | tf_op jit(solution)/shard_map/all_to_all | solution.py:404
  140.9 0.7 broadcast_in_dim.5
  141.6 6.0 %all-to-all-start.4 = ((bf16[16,24,128]{2,1,0:T(8,128)(2,1)}), bf16[16,24,128]{2,1,0:T(8,128)(2,1)S(1)}, u32[]{:S(2)}, u32[]{:S(2)}) async-start(bf16[16,24,128]{2,1,0:T(8,128)(2,1)} %broadcast_in_dim.5), calls=%async_computation.4 | async-start | bytes 196608 | tf_op jit(solution)/shard_map/all_to_all | solution.py:377
  147.6 6.4 %all-to-all-done.4.pieces_ref = bf16[16,24,128]{2,1,0:T(8,128)(2,1)S(1)} async-done(((bf16[16,24,128]{2,1,0:T(8,128)(2,1)}), bf16[16,24,128]{2,1,0:T(8,128)(2,1)S(1)}, u32[]{:S(2)}, u32[]{:S(2)}) %all-to-all-start.4) | async-done | bytes 98336 | tf_op jit(solution)/shard_map/all_to_all | solution.py:377
  154.0 0.7 join.1
  (11 shorter events, 0.0 us)
Async XLA Ops:
  0.6 49.1 %copy-start.3 = (s32[128]{0:T(128)S(1)}, s32[128]{0:T(128)}, u32[]{:S(2)}) copy-start(s32[128]{0:T(128)} %param.15) | copy-start | bytes 1540
  2.0 47.9 %all-to-all-start.1 = ((bf16[16,24,128]{2,1,0:T(8,128)(2,1)}), bf16[16,24,128]{2,1,0:T(8,128)(2,1)S(1)}, u32[]{:S(2)}, u32[]{:S(2)}) async-start(bf16[16,24,128]{2,1,0:T(8,128)(2,1)} %cut_out.1), calls=%async_computation.1 | async-start | bytes 196608 | tf_op jit(solution)/shard_map/all_to_all | solution.py:382
  28.4 23.2 %copy-start = (bf16[192,2560]{1,0:T(8,128)(2,1)S(1)}, bf16[192,2560]{1,0:T(8,128)(2,1)}, u32[]{:S(2)}) copy-start(bf16[192,2560]{1,0:T(8,128)(2,1)} %q_ref.1) | copy-start | bytes 2949124
  28.4 23.2 %copy-start.1 = (bf16[128,2560]{1,0:T(8,128)(2,1)S(1)}, bf16[128,2560]{1,0:T(8,128)(2,1)}, u32[]{:S(2)}) copy-start(bf16[128,2560]{1,0:T(8,128)(2,1)} %act_ref.1) | copy-start | bytes 1966084
  28.4 23.2 %copy-start.2 = (s32[128]{0:T(128)S(1)}, s32[128]{0:T(128)}, u32[]{:S(2)}) copy-start(s32[128]{0:T(128)} %param.14) | copy-start | bytes 1540
  31.1 45.3 %collective-permute-start.1 = (bf16[16,3712]{1,0:T(8,128)(2,1)S(1)}, bf16[16,3712]{1,0:T(8,128)(2,1)S(1)}, u32[]{:S(2)}, u32[]{:S(2)}) collective-permute-start(bf16[16,3712]{1,0:T(8,128)(2,1)S(1)} %get-tuple-element.38), channel_id=1, source_target_pairs={{0,256},{32,288},{64,320},{96,352},{128,384},{160,416},{192,448},{... | collective-permute-start | bytes 356360 | tf_op jit(solution)/shard_map/ppermute | solution.py:35
  35.1 41.8 %collective-permute-start.2 = (bf16[16,3712]{1,0:T(8,128)(2,1)S(1)}, bf16[16,3712]{1,0:T(8,128)(2,1)S(1)}, u32[]{:S(2)}, u32[]{:S(2)}) collective-permute-start(bf16[16,3712]{1,0:T(8,128)(2,1)S(1)} %get-tuple-element.39), channel_id=1, source_target_pairs={{0,512},{32,544},{64,576},{96,608},{128,640},{160,672},{192,704},{... | collective-permute-start | bytes 356360 | tf_op jit(solution)/shard_map/ppermute | solution.py:35
  51.6 23.7 %all-to-all-start = ((bf16[16,320,128]{2,1,0:T(8,128)(2,1)}), bf16[16,320,128]{2,1,0:T(8,128)(2,1)S(1)}, u32[]{:S(2)}, u32[]{:S(2)}) async-start(bf16[16,320,128]{2,1,0:T(8,128)(2,1)} %get-tuple-element.18), calls=%async_computation | async-start | bytes 2621440 | tf_op jit(solution)/shard_map/cond/branch_1_fun/all_to_all | solution.py:377
  58.1 18.3 %collective-permute-start = (bf16[128,2560]{1,0:T(8,128)(2,1)S(1)}, bf16[128,2560]{1,0:T(8,128)(2,1)}, u32[]{:S(2)}, u32[]{:S(2)}) collective-permute-start(bf16[128,2560]{1,0:T(8,128)(2,1)S(1)} %get-tuple-element.23), channel_id=1, source_target_pairs={{0,1},{1,0},{2,3},{3,2},{4,5},{5,4},{6,7},{7,6},{8,9},{9,8},{10,11... | collective-permute-start | bytes 1966088 | tf_op jit(solution)/shard_map/cond/branch_1_fun/ppermute | solution.py:35
  78.3 3.2 %collective-permute-start.3 = (bf16[128,512]{1,0:T(8,128)(2,1)S(1)}, bf16[128,512]{1,0:T(8,128)(2,1)S(1)}, u32[]{:S(2)}, u32[]{:S(2)}) collective-permute-start(bf16[128,512]{1,0:T(8,128)(2,1)S(1)} %own_rows.1.rows_ref), channel_id=1, source_target_pairs={{0,1},{1,0},{2,3},{3,2},{4,5},{5,4},{6,7},{7,6},{8,9},{9,8},{10,11... | collective-permute-start | bytes 393224 | tf_op jit(solution)/shard_map/ppermute | solution.py:35
  84.6 25.6 %all-to-all-start.2 = ((bf16[32,160,128]{2,1,0:T(8,128)(2,1)}), bf16[32,160,128]{2,1,0:T(8,128)(2,1)S(1)}, u32[]{:S(2)}, u32[]{:S(2)}) async-start(bf16[32,160,128]{2,1,0:T(8,128)(2,1)} %gradient_pieces.1), calls=%async_computation.2 | async-start | bytes 2621440 | tf_op jit(solution)/shard_map/all_to_all | solution.py:393
  91.7 41.0 %collective-permute-start.4 = (bf16[16,320,128]{2,1,0:T(8,128)(2,1)}, bf16[16,320,128]{2,1,0:T(8,128)(2,1)S(1)}, u32[]{:S(2)}, u32[]{:S(2)}) collective-permute-start(bf16[16,320,128]{2,1,0:T(8,128)(2,1)} %get-tuple-element.41.own_ref), channel_id=1, source_target_pairs={{0,1},{1,0},{2,3},{3,2},{4,5},{5,4},{6,7},{7,6},{8,9},{9,8},{10,11... | collective-permute-start | bytes 3932168 | tf_op jit(solution)/shard_map/ppermute | solution.py:35
  111.1 29.8 %all-to-all-start.3 = ((bf16[16,24,128]{2,1,0:T(8,128)(2,1)}), bf16[16,24,128]{2,1,0:T(8,128)(2,1)S(1)}, u32[]{:S(2)}, u32[]{:S(2)}) async-start(bf16[16,24,128]{2,1,0:T(8,128)(2,1)} %plane_sum.1), calls=%async_computation.3 | async-start | bytes 196608 | tf_op jit(solution)/shard_map/all_to_all | solution.py:404
  141.6 12.4 %all-to-all-start.4 = ((bf16[16,24,128]{2,1,0:T(8,128)(2,1)}), bf16[16,24,128]{2,1,0:T(8,128)(2,1)S(1)}, u32[]{:S(2)}, u32[]{:S(2)}) async-start(bf16[16,24,128]{2,1,0:T(8,128)(2,1)} %broadcast_in_dim.5), calls=%async_computation.4 | async-start | bytes 196608 | tf_op jit(solution)/shard_map/all_to_all | solution.py:377

commit v10 on v9

--- a/solution.py
+++ b/solution.py
@@ -265,11 +265,12 @@
     )(later, pieces)
 
 
-def cut_kernel(place_ref, rows_ref, tile_ref, out_ref):
-    del place_ref
+def cut_kernel(place_ref, rows_ref, tiles_ref, out_ref):
+    tiles = tiles_ref[...].astype(F32)
+    tile = jnp.where(place_ref[0] // (2 * CUTS) == 0, tiles[:8], tiles[8:]).astype(BF16)
     for at in range(out_ref.shape[0]):
         out_ref[at, :16, :] = rows_ref[...]
-        out_ref[at, 16:, :] = tile_ref[...]
+        out_ref[at, 16:, :] = tile
 
 
 def cut_out(shard, place):
@@ -280,7 +281,7 @@
             grid=(1,),
             in_specs=[
                 pl.BlockSpec((16, HD), lambda i, p: (p[0] // CUTS, p[0] % CUTS)),
-                pl.BlockSpec((8, HD), lambda i, p: (2 * CUTS + p[0] // (2 * CUTS), p[0] % CUTS)),
+                pl.BlockSpec((16, HD), lambda i, p: (CUTS, p[0] % CUTS)),
             ],
             out_specs=pl.BlockSpec((DEPTH, ROWS, HD), lambda i, p: (0, 0, 0)),
         ),

time: 155 us -> 155 us (level)
  no operation moved by 1% of the time
where the time goes in v10:
time: 155 us
  starting transfers between devices  92 us (59%)
  waiting for transfers between devices  39.3 us (25%)
  Pallas kernels  20 us (13%)
  local copies, waits for them, and re-layouts  2.62 us (2%)
    all_to_all x1, starting transfers between devices, depth_gather(): return lax.all_to_all(copies, 'fsdp', 0, 0, axis_index_groups=groups)  26.4 us
    ppermute x5, starting transfers between devices, swapped(): return lax.ppermute(block, axis, route)  24.4 us
    all_to_all x1, starting transfers between devices, depth_exchange(): return lax.all_to_all(pieces, BOTH, 0, 0, axis_index_groups=groups)  21.6 us
    all_to_all x2, waiting for transfers between devices, plane_exchange(): return lax.all_to_all(pieces, 'dp', 0, 0, axis_index_groups=groups)  16.9 us
    all_to_all x1, waiting for transfers between devices, planes_exchange(): return lax.all_to_all(pieces, BOTH, 0, 0, axis_index_groups=groups)  16.6 us
    all_to_all x2, starting transfers between devices, plane_exchange(): return lax.all_to_all(pieces, 'dp', 0, 0, axis_index_groups=groups)  12.5 us
    all_to_all x1, starting transfers between devices, planes_exchange(): return lax.all_to_all(pieces, BOTH, 0, 0, axis_index_groups=groups)  7.06 us
    pallas_call x1, Pallas kernels, project_back(): pl.pallas_call(project_kernel, grid_spec=pltpu.PrefetchScalarGridSpec(num...  4.26 us
  transfers between devices with their start and end apart: 10, of which 6 were waited for; matrix products, arithmetic and copies ran while one was open for 1% of the time, Pallas kernels for 9%

profile of v10, /device:TPU:2, one launch (start us, length us, event | category | flops | bytes accessed | tf_op | source)
XLA Modules:
  0.0 154.6 jit_solution(773468253631060975)
XLA Ops:
  0.7 1.4 cut_out.1
  2.0 26.4 %all-to-all-start.1 = ((bf16[16,24,128]{2,1,0:T(8,128)(2,1)}), bf16[16,24,128]{2,1,0:T(8,128)(2,1)S(1)}, u32[]{:S(2)}, u32[]{:S(2)}) async-start(bf16[16,24,128]{2,1,0:T(8,128)(2,1)} %cut_out.1), calls=%async_computation.1 | async-start | bytes 196608 | tf_op jit(solution)/shard_map/all_to_all | solution.py:383
  28.4 0.0 copy-start.1
  28.4 0.0 copy-start.2
  28.4 2.7 %messages.1 = (bf16[16,3712]{1,0:T(8,128)(2,1)S(1)}, bf16[16,3712]{1,0:T(8,128)(2,1)S(1)}) custom-call(bf16[192,2560]{1,0:T(8,128)(2,1)} %q_ref.1, bf16[192,512]{1,0:T(8,128)(2,1)} %k_ref.1, bf16[192,2560]{1,0:T(8,128)(2,1)} %c_ref.1), custom_call_target="tpu_custom_call" | custom-call | tf_op jit(solution)/shard_map/messages/pallas_call | solution.py:79
  31.1 4.0 %collective-permute-start.1 = (bf16[16,3712]{1,0:T(8,128)(2,1)S(1)}, bf16[16,3712]{1,0:T(8,128)(2,1)S(1)}, u32[]{:S(2)}, u32[]{:S(2)}) collective-permute-start(bf16[16,3712]{1,0:T(8,128)(2,1)S(1)} %get-tuple-element.38), channel_id=1, source_target_pairs={{0,256},{32,288},{64,320},{96,352},{128,384},{160,416},{192,448},{... | collective-permute-start | bytes 356360 | tf_op jit(solution)/shard_map/ppermute | solution.py:35
  35.1 14.6 %collective-permute-start.2 = (bf16[16,3712]{1,0:T(8,128)(2,1)S(1)}, bf16[16,3712]{1,0:T(8,128)(2,1)S(1)}, u32[]{:S(2)}, u32[]{:S(2)}) collective-permute-start(bf16[16,3712]{1,0:T(8,128)(2,1)S(1)} %get-tuple-element.39), channel_id=1, source_target_pairs={{0,512},{32,544},{64,576},{96,608},{128,640},{160,672},{192,704},{... | collective-permute-start | bytes 356360 | tf_op jit(solution)/shard_map/ppermute | solution.py:35
  49.8 0.1 copy.11.slot_ref
  49.9 1.7 %spread.1 = bf16[16,320,128]{2,1,0:T(8,128)(2,1)} custom-call(s32[1]{0:T(128)} %bitcast.4.place_ref, bf16[16,24,128]{2,1,0:T(8,128)(2,1)S(1)} %all-to-all-done.1.pieces_ref), custom_call_target="tpu_custom_call" | custom-call | tf_op jit(solution)/shard_map/spread/pallas_call | solution.py:314
  51.6 24.8 %conditional.1 = (bf16[16,320,128]{2,1,0:T(8,128)(2,1)}, bf16[128,512]{1,0:T(8,128)(2,1)}, bf16[128,2560]{1,0:T(8,128)(2,1)}) conditional(s32[]{:T(128)} %convert_element_type.2, (bf16[16,320,128]{2,1,0:T(8,128)(2,1)}, bf16[128,2560]{1,0:T(8,128)(2,1)S(1)}) %tuple.26, (bf16[16,320,128]{2,1,0:T(8,128)(2,1)}, s32[128]{0:T(128)S(1)}, ...), branch_computations={%region_0.1_spmd, %region_1.2_spmd} | conditional | bytes 9176160 | solution.py:426
  51.6 6.5 %all-to-all-start = ((bf16[16,320,128]{2,1,0:T(8,128)(2,1)}), bf16[16,320,128]{2,1,0:T(8,128)(2,1)S(1)}, u32[]{:S(2)}, u32[]{:S(2)}) async-start(bf16[16,320,128]{2,1,0:T(8,128)(2,1)} %get-tuple-element.18), calls=%async_computation | async-start | bytes 2621440 | tf_op jit(solution)/shard_map/cond/branch_1_fun/all_to_all | solution.py:378
  58.1 1.9 %collective-permute-start = (bf16[128,2560]{1,0:T(8,128)(2,1)S(1)}, bf16[128,2560]{1,0:T(8,128)(2,1)}, u32[]{:S(2)}, u32[]{:S(2)}) collective-permute-start(bf16[128,2560]{1,0:T(8,128)(2,1)S(1)} %get-tuple-element.23), channel_id=1, source_target_pairs={{0,1},{1,0},{2,3},{3,2},{4,5},{5,4},{6,7},{7,6},{8,9},{9,8},{10,11... | collective-permute-start | bytes 1966088 | tf_op jit(solution)/shard_map/cond/branch_1_fun/ppermute | solution.py:35
  60.0 0.7 copy.10.col_ref
  60.8 4.0 %attend.1 = bf16[128,512]{1,0:T(8,128)(2,1)} custom-call(s32[128,1]{1,0:T(8,128)} %copy.10.col_ref, s32[1,128]{1,0:T(1,128)S(1)} %bitcast.7, bf16[192,2560]{1,0:T(8,128)(2,1)S(1)} %get-tuple-element.20.q_ref, bf16[192,512]{1,0:T(8,128)(2,1)} %get-tuple-element.21.k_ref, bf16[192,2560]{1,0:T(8,128)(2,1)} %get-tuple-element.22.c_ref), custom_call_target="tpu_custom_call" | custom-call | tf_op jit(solution)/shard_map/cond/branch_1_fun/attend/pallas_call | solution.py:126
  64.8 10.5 %all-to-all-done = bf16[16,320,128]{2,1,0:T(8,128)(2,1)S(1)} async-done(((bf16[16,320,128]{2,1,0:T(8,128)(2,1)}), bf16[16,320,128]{2,1,0:T(8,128)(2,1)S(1)}, u32[]{:S(2)}, u32[]{:S(2)}) %all-to-all-start) | async-done | bytes 1310752 | tf_op jit(solution)/shard_map/cond/branch_1_fun/all_to_all | solution.py:378
  75.3 1.1 copy.15
  76.4 0.5 collective-permute-done.2.first_ref
  76.9 1.4 own_rows.1.rows_ref
  78.3 1.9 %collective-permute-start.3 = (bf16[128,512]{1,0:T(8,128)(2,1)S(1)}, bf16[128,512]{1,0:T(8,128)(2,1)S(1)}, u32[]{:S(2)}, u32[]{:S(2)}) collective-permute-start(bf16[128,512]{1,0:T(8,128)(2,1)S(1)} %own_rows.1.rows_ref), channel_id=1, source_target_pairs={{0,1},{1,0},{2,3},{3,2},{4,5},{5,4},{6,7},{7,6},{8,9},{9,8},{10,11... | collective-permute-start | bytes 393224 | tf_op jit(solution)/shard_map/ppermute | solution.py:35
  80.2 1.3 collective-permute-done.3.other_rows_ref
  81.5 3.1 %gradient_pieces.1 = bf16[32,160,128]{2,1,0:T(8,128)(2,1)} custom-call(s32[1]{0:T(128)} %bitcast.2.core_ref, bf16[128,512]{1,0:T(8,128)(2,1)S(1)} %own_rows.1.rows_ref, bf16[128,512]{1,0:T(8,128)(2,1)S(1)} %collective-permute-done.3.other_rows_ref, bf16[128,2560]{1,0:T(8,128)(2,1)S(1)} %copy-done.1, bf16[128,2560]{1,0:T(8,128)(2,1)} %get-tuple-element.40.other_act_ref), custom_call_target="tpu_custom_call" | custom-call | tf_op jit(solution)/shard_map/gradient_pieces/pallas_call | solution.py:198
  84.6 7.1 %all-to-all-start.2 = ((bf16[32,160,128]{2,1,0:T(8,128)(2,1)}), bf16[32,160,128]{2,1,0:T(8,128)(2,1)S(1)}, u32[]{:S(2)}, u32[]{:S(2)}) async-start(bf16[32,160,128]{2,1,0:T(8,128)(2,1)} %gradient_pieces.1), calls=%async_computation.2 | async-start | bytes 2621440 | tf_op jit(solution)/shard_map/all_to_all | solution.py:394
  91.7 1.9 %collective-permute-start.4 = (bf16[16,320,128]{2,1,0:T(8,128)(2,1)}, bf16[16,320,128]{2,1,0:T(8,128)(2,1)S(1)}, u32[]{:S(2)}, u32[]{:S(2)}) collective-permute-start(bf16[16,320,128]{2,1,0:T(8,128)(2,1)} %get-tuple-element.41.own_ref), channel_id=1, source_target_pairs={{0,1},{1,0},{2,3},{3,2},{4,5},{5,4},{6,7},{7,6},{8,9},{9,8},{10,11... | collective-permute-start | bytes 3932168 | tf_op jit(solution)/shard_map/ppermute | solution.py:35
  93.6 16.6 %all-to-all-done.2.parts_ref = bf16[32,160,128]{2,1,0:T(8,128)(2,1)S(1)} async-done(((bf16[32,160,128]{2,1,0:T(8,128)(2,1)}), bf16[32,160,128]{2,1,0:T(8,128)(2,1)S(1)}, u32[]{:S(2)}, u32[]{:S(2)}) %all-to-all-start.2) | async-done | bytes 1310752 | tf_op jit(solution)/shard_map/all_to_all | solution.py:394
  110.3 0.8 plane_sum.1
  111.1 21.6 %all-to-all-start.3 = ((bf16[16,24,128]{2,1,0:T(8,128)(2,1)}), bf16[16,24,128]{2,1,0:T(8,128)(2,1)S(1)}, u32[]{:S(2)}, u32[]{:S(2)}) async-start(bf16[16,24,128]{2,1,0:T(8,128)(2,1)} %plane_sum.1), calls=%async_computation.3 | async-start | bytes 196608 | tf_op jit(solution)/shard_map/all_to_all | solution.py:405
  132.7 4.3 %project_back.1 = bf16[128,2560]{1,0:T(8,128)(2,1)} custom-call(s32[1]{0:T(128)} %bitcast.2.core_ref, bf16[128,512]{1,0:T(8,128)(2,1)S(1)} %own_rows.1.rows_ref, bf16[16,320,128]{2,1,0:T(8,128)(2,1)} %get-tuple-element.41.own_ref, bf16[16,320,128]{2,1,0:T(8,128)(2,1)S(1)} %collective-permute-done.4.other_ref), custom_call_target="tpu_custom_call" | custom-call | tf_op jit(solution)/shard_map/project_back/pallas_call | solution.py:361
  137.0 3.9 %all-to-all-done.3 = bf16[16,24,128]{2,1,0:T(8,128)(2,1)S(1)} async-done(((bf16[16,24,128]{2,1,0:T(8,128)(2,1)}), bf16[16,24,128]{2,1,0:T(8,128)(2,1)S(1)}, u32[]{:S(2)}, u32[]{:S(2)}) %all-to-all-start.3) | async-done | bytes 98336 | tf_op jit(solution)/shard_map/all_to_all | solution.py:405
  140.9 0.7 broadcast_in_dim.5
  141.6 6.0 %all-to-all-start.4 = ((bf16[16,24,128]{2,1,0:T(8,128)(2,1)}), bf16[16,24,128]{2,1,0:T(8,128)(2,1)S(1)}, u32[]{:S(2)}, u32[]{:S(2)}) async-start(bf16[16,24,128]{2,1,0:T(8,128)(2,1)} %broadcast_in_dim.5), calls=%async_computation.4 | async-start | bytes 196608 | tf_op jit(solution)/shard_map/all_to_all | solution.py:378
  147.6 6.4 %all-to-all-done.4.pieces_ref = bf16[16,24,128]{2,1,0:T(8,128)(2,1)S(1)} async-done(((bf16[16,24,128]{2,1,0:T(8,128)(2,1)}), bf16[16,24,128]{2,1,0:T(8,128)(2,1)S(1)}, u32[]{:S(2)}, u32[]{:S(2)}) %all-to-all-start.4) | async-done | bytes 98336 | tf_op jit(solution)/shard_map/all_to_all | solution.py:378
  154.0 0.7 join.1
  (11 shorter events, 0.0 us)
Async XLA Ops:
  0.6 49.1 %copy-start.3 = (s32[128]{0:T(128)S(1)}, s32[128]{0:T(128)}, u32[]{:S(2)}) copy-start(s32[128]{0:T(128)} %param.15) | copy-start | bytes 1540
  2.0 47.9 %all-to-all-start.1 = ((bf16[16,24,128]{2,1,0:T(8,128)(2,1)}), bf16[16,24,128]{2,1,0:T(8,128)(2,1)S(1)}, u32[]{:S(2)}, u32[]{:S(2)}) async-start(bf16[16,24,128]{2,1,0:T(8,128)(2,1)} %cut_out.1), calls=%async_computation.1 | async-start | bytes 196608 | tf_op jit(solution)/shard_map/all_to_all | solution.py:383
  28.4 23.2 %copy-start = (bf16[192,2560]{1,0:T(8,128)(2,1)S(1)}, bf16[192,2560]{1,0:T(8,128)(2,1)}, u32[]{:S(2)}) copy-start(bf16[192,2560]{1,0:T(8,128)(2,1)} %q_ref.1) | copy-start | bytes 2949124
  28.4 23.2 %copy-start.1 = (bf16[128,2560]{1,0:T(8,128)(2,1)S(1)}, bf16[128,2560]{1,0:T(8,128)(2,1)}, u32[]{:S(2)}) copy-start(bf16[128,2560]{1,0:T(8,128)(2,1)} %act_ref.1) | copy-start | bytes 1966084
  28.4 23.2 %copy-start.2 = (s32[128]{0:T(128)S(1)}, s32[128]{0:T(128)}, u32[]{:S(2)}) copy-start(s32[128]{0:T(128)} %param.14) | copy-start | bytes 1540
  31.1 45.3 %collective-permute-start.1 = (bf16[16,3712]{1,0:T(8,128)(2,1)S(1)}, bf16[16,3712]{1,0:T(8,128)(2,1)S(1)}, u32[]{:S(2)}, u32[]{:S(2)}) collective-permute-start(bf16[16,3712]{1,0:T(8,128)(2,1)S(1)} %get-tuple-element.38), channel_id=1, source_target_pairs={{0,256},{32,288},{64,320},{96,352},{128,384},{160,416},{192,448},{... | collective-permute-start | bytes 356360 | tf_op jit(solution)/shard_map/ppermute | solution.py:35
  35.1 41.8 %collective-permute-start.2 = (bf16[16,3712]{1,0:T(8,128)(2,1)S(1)}, bf16[16,3712]{1,0:T(8,128)(2,1)S(1)}, u32[]{:S(2)}, u32[]{:S(2)}) collective-permute-start(bf16[16,3712]{1,0:T(8,128)(2,1)S(1)} %get-tuple-element.39), channel_id=1, source_target_pairs={{0,512},{32,544},{64,576},{96,608},{128,640},{160,672},{192,704},{... | collective-permute-start | bytes 356360 | tf_op jit(solution)/shard_map/ppermute | solution.py:35
  51.6 23.7 %all-to-all-start = ((bf16[16,320,128]{2,1,0:T(8,128)(2,1)}), bf16[16,320,128]{2,1,0:T(8,128)(2,1)S(1)}, u32[]{:S(2)}, u32[]{:S(2)}) async-start(bf16[16,320,128]{2,1,0:T(8,128)(2,1)} %get-tuple-element.18), calls=%async_computation | async-start | bytes 2621440 | tf_op jit(solution)/shard_map/cond/branch_1_fun/all_to_all | solution.py:378
  58.1 18.3 %collective-permute-start = (bf16[128,2560]{1,0:T(8,128)(2,1)S(1)}, bf16[128,2560]{1,0:T(8,128)(2,1)}, u32[]{:S(2)}, u32[]{:S(2)}) collective-permute-start(bf16[128,2560]{1,0:T(8,128)(2,1)S(1)} %get-tuple-element.23), channel_id=1, source_target_pairs={{0,1},{1,0},{2,3},{3,2},{4,5},{5,4},{6,7},{7,6},{8,9},{9,8},{10,11... | collective-permute-start | bytes 1966088 | tf_op jit(solution)/shard_map/cond/branch_1_fun/ppermute | solution.py:35
  78.3 3.2 %collective-permute-start.3 = (bf16[128,512]{1,0:T(8,128)(2,1)S(1)}, bf16[128,512]{1,0:T(8,128)(2,1)S(1)}, u32[]{:S(2)}, u32[]{:S(2)}) collective-permute-start(bf16[128,512]{1,0:T(8,128)(2,1)S(1)} %own_rows.1.rows_ref), channel_id=1, source_target_pairs={{0,1},{1,0},{2,3},{3,2},{4,5},{5,4},{6,7},{7,6},{8,9},{9,8},{10,11... | collective-permute-start | bytes 393224 | tf_op jit(solution)/shard_map/ppermute | solution.py:35
  84.6 25.6 %all-to-all-start.2 = ((bf16[32,160,128]{2,1,0:T(8,128)(2,1)}), bf16[32,160,128]{2,1,0:T(8,128)(2,1)S(1)}, u32[]{:S(2)}, u32[]{:S(2)}) async-start(bf16[32,160,128]{2,1,0:T(8,128)(2,1)} %gradient_pieces.1), calls=%async_computation.2 | async-start | bytes 2621440 | tf_op jit(solution)/shard_map/all_to_all | solution.py:394
  91.7 41.0 %collective-permute-start.4 = (bf16[16,320,128]{2,1,0:T(8,128)(2,1)}, bf16[16,320,128]{2,1,0:T(8,128)(2,1)S(1)}, u32[]{:S(2)}, u32[]{:S(2)}) collective-permute-start(bf16[16,320,128]{2,1,0:T(8,128)(2,1)} %get-tuple-element.41.own_ref), channel_id=1, source_target_pairs={{0,1},{1,0},{2,3},{3,2},{4,5},{5,4},{6,7},{7,6},{8,9},{9,8},{10,11... | collective-permute-start | bytes 3932168 | tf_op jit(solution)/shard_map/ppermute | solution.py:35
  111.1 29.8 %all-to-all-start.3 = ((bf16[16,24,128]{2,1,0:T(8,128)(2,1)}), bf16[16,24,128]{2,1,0:T(8,128)(2,1)S(1)}, u32[]{:S(2)}, u32[]{:S(2)}) async-start(bf16[16,24,128]{2,1,0:T(8,128)(2,1)} %plane_sum.1), calls=%async_computation.3 | async-start | bytes 196608 | tf_op jit(solution)/shard_map/all_to_all | solution.py:405
  141.6 12.4 %all-to-all-start.4 = ((bf16[16,24,128]{2,1,0:T(8,128)(2,1)}), bf16[16,24,128]{2,1,0:T(8,128)(2,1)S(1)}, u32[]{:S(2)}, u32[]{:S(2)}) async-start(bf16[16,24,128]{2,1,0:T(8,128)(2,1)} %broadcast_in_dim.5), calls=%async_computation.4 | async-start | bytes 196608 | tf_op jit(solution)/shard_map/all_to_all | solution.py:378
